TPU v7x, 256 devices: a whole 4x4x8 slice. The times are simulated.
256 devices in a mesh: prow: 16 (over x, y_lo, core), pcol: 16 (over y_hi, z).
Axes of the slice: x: 4, y: 4 (y_hi: 2, y_lo: 2; y = y_hi * 2 + y_lo), z: 8, core: 2. Of those that a mesh axis runs over, the one named last changes fastest.
Arguments:
- g_top: float32 [2, 4096, 2, 4096], P(None, 'prow', None, 'pcol')
- l_one: float32 [2, 4096, 2048], P(None, 'prow', 'pcol'), may hold values from -0.9 to 0.9
- struct_one: int32 [8, 16], replicated, may hold values from 0 to 31, as said below
- dinv_one: float32 [256, 2048], P('prow', 'pcol'), may hold values from -3 to 3
- l_two: float32 [2, 4096, 2048], P(None, 'prow', 'pcol'), may hold values from -0.9 to 0.9
- lp_two: float32 [256, 2048], P(None, 'pcol'), may hold values from -0.36 to 0.36
- parent_two: int32 [8], replicated, may hold values from 0 to 7
- pos_two: int32 [8, 8], replicated, may hold values from 0 to 15, as said below
- dinv_two: float32 [256, 2048], P('prow', 'pcol'), may hold values from -3 to 3
Outputs:
- panel_one: float32 [2, 4096, 2048], P(None, 'prow', 'pcol')
- diag_one: float32 [256, 2048], P('prow', 'pcol')
- panel_two: float32 [2, 4096, 2048], P(None, 'prow', 'pcol')
- parent_rows: float32 [256, 2048], P('prow', 'pcol')
- diag_two: float32 [256, 2048], P('prow', 'pcol')
Inputs may be any that keep to these rules, and one draw needn't show every extreme that they name: `struct_one`: each row holds 16 distinct top-separator block indices in increasing order. `pos_two`: each row holds 8 distinct positions in increasing order.
All inputs are finite; a program needn't handle non-finite values.
Results may differ from a plain program's by a relative error of at most 0.00012.
Values sent between devices are 32-bit elements; how exact they have to be, the bound alone decides.
No kernel may reach another device: no remote copies, remote signals or barrier semaphores. Data moves between devices by JAX's collectives and lax.ppermute only.
A program may use at most 128 MiB of HBM per device.

v0:
```python
import jax
import jax.numpy as jnp
from jax import lax
from jax.sharding import PartitionSpec as P

exact_mode = lax.Precision.HIGHEST


def broadcast(x, axis, root):
    mine = lax.axis_index(axis) == root
    return lax.psum(jnp.where(mine, x, jnp.zeros_like(x)), axis)


def spread(flag_rows, repeat_by):
    return jnp.repeat(flag_rows.astype(jnp.float32), repeat_by, axis=1)


def stacked_rows(pieces):
    joined = jnp.stack(pieces, axis=1)
    return joined.reshape((-1,) + joined.shape[2:])


def ancestor_product(g_top, rows_here):
    return -jnp.einsum("aucv,cve->aue", g_top, rows_here, precision=exact_mode)


def local(g_top, l_one, struct_one, dinv_one, l_two, lp_two, parent_two, pos_two, dinv_two):
    n_rows = lax.axis_size("prow")
    n_cols = lax.axis_size("pcol")
    row_index = lax.axis_index("prow")
    col_index = lax.axis_index("pcol")
    local_rows = g_top.shape[0]
    block_size = g_top.shape[1]
    supers = struct_one.shape[0]
    col_width = l_one.shape[2]
    slab_rows = dinv_one.shape[0]
    repeats = n_rows // n_cols
    rows_flat = local_rows * block_size
    blocks_here = jnp.arange(local_rows, dtype=jnp.int32) * n_rows + row_index
    struct_two = jnp.take_along_axis(jnp.take(struct_one, parent_two, axis=0), pos_two, axis=1)
    flags_one = jnp.any(struct_one[None, :, :] == blocks_here[:, None, None], axis=2)
    flags_two = jnp.any(struct_two[None, :, :] == blocks_here[:, None, None], axis=2)
    start_col = col_index * col_width
    keep_one = lax.dynamic_slice_in_dim(spread(flags_one, block_size), start_col, col_width, 1)
    keep_two = lax.dynamic_slice_in_dim(spread(flags_two, block_size), start_col, col_width, 1)
    masked_one = l_one * keep_one[:, None, :]
    masked_two = l_two * keep_two[:, None, :]
    all_one, all_two, lp_all, dinv_all = (
        lax.all_gather(masked_one, "pcol", axis=2, tiled=True),
        lax.all_gather(masked_two, "pcol", axis=2, tiled=True),
        lax.all_gather(lp_two, "pcol", axis=1, tiled=True),
        lax.all_gather(dinv_one, "pcol", axis=1, tiled=True),
    )
    one_blocks = all_one.reshape(rows_flat, supers, block_size)
    parent_panel = jnp.take(one_blocks, parent_two, axis=1)
    lp_blocks = lp_all.reshape(block_size, supers, block_size)
    folded = all_two.reshape(rows_flat, supers, block_size) - jnp.einsum(
        "rgb,bgc->rgc", parent_panel, lp_blocks, precision=exact_mode
    )
    folded_flat = folded.reshape(local_rows, block_size, supers * block_size)

    def one_level(values):
        pieces = [broadcast(values, "prow", col_index + 0 * n_cols)]
        return lax.psum_scatter(
            ancestor_product(g_top, stacked_rows(pieces)), "pcol", scatter_dimension=2, tiled=True
        )

    inverse_one = one_level(all_one)
    inverse_two = one_level(folded_flat)
    panel_one = inverse_one * keep_one[:, None, :]
    panel_two = inverse_two * keep_two[:, None, :]
    piece_count = max(col_width // block_size, 1)
    piece_width = min(col_width, block_size)
    first_super = start_col // block_size
    mine_one = lax.dynamic_slice_in_dim(one_blocks, first_super, piece_count, 1)
    inverse_one_here = inverse_one.reshape(rows_flat, piece_count, piece_width)
    term_one = jnp.einsum("rjb,rjc->bjc", mine_one, inverse_one_here, precision=exact_mode)
    my_parents = lax.dynamic_slice_in_dim(parent_two, first_super, piece_count, 0)
    parent_mine = jnp.take(one_blocks, my_parents, axis=1)
    inverse_two_here = inverse_two.reshape(rows_flat, piece_count, piece_width)
    term_parent = jnp.einsum("rjb,rjc->bjc", parent_mine, inverse_two_here, precision=exact_mode)
    folded_mine = lax.dynamic_slice_in_dim(folded, first_super, piece_count, 1)
    term_fold = jnp.einsum("rjb,rjc->bjc", folded_mine, inverse_two_here, precision=exact_mode)
    dinv_parents = jnp.take(dinv_all.reshape(slab_rows, supers, block_size), my_parents, axis=1)
    lp_mine = lp_two.reshape(block_size, piece_count, piece_width)
    lp_slab = lax.dynamic_slice_in_dim(lp_blocks, row_index * slab_rows, slab_rows, 0)
    lp_slab = lax.dynamic_slice_in_dim(lp_slab, first_super, piece_count, 1)
    scaled = jnp.einsum("ajb,bjc->ajc", dinv_parents, lp_mine, precision=exact_mode)
    term_quad = jnp.einsum("ajb,ajc->bjc", lp_slab, scaled, precision=exact_mode)
    sum_one, sum_parent, sum_two = (
        lax.psum_scatter(
            term_one.reshape(block_size, col_width), "prow", scatter_dimension=0, tiled=True
        ),
        lax.psum_scatter(
            term_parent.reshape(block_size, col_width), "prow", scatter_dimension=0, tiled=True
        ),
        lax.psum_scatter(
            (term_quad - term_fold).reshape(block_size, col_width),
            "prow",
            scatter_dimension=0,
            tiled=True,
        ),
    )
    diag_one = dinv_one - sum_one
    parent_rows = -(sum_parent + scaled.reshape(slab_rows, col_width))
    diag_two = dinv_two + sum_two
    return (panel_one, diag_one, panel_two, parent_rows, diag_two)


def solution(mesh):
    placed = (
        P(None, "prow", None, "pcol"),
        P(None, "prow", "pcol"),
        P(),
        P("prow", "pcol"),
        P(None, "prow", "pcol"),
        P(None, "pcol"),
        P(),
        P(),
        P("prow", "pcol"),
    )
    return jax.shard_map(
        local,
        mesh=mesh,
        in_specs=placed,
        out_specs=(
            P(None, "prow", "pcol"),
            P("prow", "pcol"),
            P(None, "prow", "pcol"),
            P("prow", "pcol"),
            P("prow", "pcol"),
        ),
        check_vma=False,
    )
```

profile of v0, /device:TPU:1, one launch (start us, length us, event | category | flops | bytes accessed | tf_op | source)
XLA Modules:
  0.0 1153.3 jit_solution(17447788048560057199)
XLA Ops:
  8.4 1.1 copy.69
  11.0 1.2 gather_fusion
  16.8 95.1 %all-gather.4.cloned.1.call-done = f32[2,256,2048]{1,2,0:T(8,128)} async-done(((f32[2,256,128]{1,2,0:T(8,128)}), f32[2,256,2048]{1,2,0:T(8,128)}) %all-gather.4.cloned.1.call-update) | async-done | bytes 4194320 | tf_op jit(solution)/shard_map/all_gather | solution.py:49
  111.9 5.4 copy.72
  117.3 4.1 copy.103
  121.4 1.9 copy-done.1
  123.4 3.2 copy.76
  126.6 5.1 gather_fusion.1
  131.7 80.0 %all-gather.6.cloned.1.call-done = f32[2,256,2048]{1,2,0:T(8,128)} async-done(((f32[2,256,128]{1,2,0:T(8,128)}), f32[2,256,2048]{1,2,0:T(8,128)}) %all-gather.6.cloned.1.call-update) | async-done | bytes 4194320 | tf_op jit(solution)/shard_map/all_gather | solution.py:50
  211.7 5.4 copy.75
  217.1 6.1 copy.105
  223.2 72.8 %all-gather.8.cloned.1.call-done = f32[256,2048]{0,1:T(8,128)} async-done(((f32[256,128]{0,1:T(8,128)}), f32[256,2048]{0,1:T(8,128)}) %all-gather.8.cloned.1.call-update) | async-done | bytes 2097168 | tf_op jit(solution)/shard_map/all_gather | solution.py:51
  296.0 11.3 broadcast_select_fusion
  307.2 4.4 copy.80
  311.6 4.9 select_n.119
  316.5 5.4 copy.81
  321.9 2.3 broadcast_select_fusion.1
  324.2 202.1 %all-reduce.3.cloned.1.call-done = (f32[2,256,2048]{1,2,0:T(8,128)}, f32[2,256,2048]{1,2,0:T(8,128)}) async-done(((f32[2,256,2048]{1,2,0:T(8,128)}, f32[2,256,2048]{1,2,0:T(8,128)}), (f32[2,256,2048]{1,2,0:T(8,128)}, f32[2,256,2048]{1,2,0:T(8,128)})) %all-reduce.3.cloned.1.call-update) | async-done | bytes 8388624 | tf_op jit(solution)/shard_map/psum | solution.py:11
  526.3 9.9 fusion
  536.3 9.9 fusion.5
  549.4 34.5 %all_gather.15 = f32[16,2048]{1,0:T(8,128)S(1)} all-gather(f32[16,128]{1,0:T(8,128)S(1)} %copy-done.6), channel_id=1, replica_groups=mesh['prow'=16,'pcol'=16] {'pcol'}, dimensions={1}, use_global_device_ids=true | all-gather | bytes 139264 | tf_op jit(solution)/shard_map/all_gather | solution.py:52
  584.0 4.4 broadcast_select_fusion.2
  588.4 153.4 %reduce-scatter.14.cloned.1.call-done = f32[2,256,128]{1,2,0:T(8,128)} async-done(((f32[2,256,2048]{1,2,0:T(8,128)}), f32[2,256,128]{1,2,0:T(8,128)}) %reduce-scatter.14.cloned.1.call-update) | async-done | bytes 262160 | tf_op jit(solution)/shard_map/reduce_scatter | solution.py:64
  741.8 1.1 copy.83
  744.6 208.1 %reduce-scatter.12.cloned.1.call-done = f32[2,256,128]{1,2,0:T(8,128)} async-done(((f32[2,256,2048]{1,2,0:T(8,128)}), f32[2,256,128]{1,2,0:T(8,128)}) %reduce-scatter.12.cloned.1.call-update) | async-done | bytes 262160 | tf_op jit(solution)/shard_map/reduce_scatter | solution.py:64
  952.7 1.1 copy.71
  955.3 62.4 %reduce-scatter.18.cloned.1.call-done = f32[16,128]{1,0:T(8,128)} async-done(((f32[256,128]{1,0:T(8,128)}), f32[16,128]{1,0:T(8,128)}) %reduce-scatter.18.cloned.1.call-update) | async-done | bytes 8208 | tf_op jit(solution)/shard_map/reduce_scatter | solution.py:94
  1017.7 1.5 add_negate_fusion
  1019.2 1.3 fusion.26
  1020.5 1.7 fusion.17
  1024.8 56.7 %reduce-scatter.16.cloned.1.call-done = f32[16,128]{1,0:T(8,128)} async-done(((f32[256,128]{1,0:T(8,128)}), f32[16,128]{1,0:T(8,128)}) %reduce-scatter.16.cloned.1.call-update) | async-done | bytes 8208
  1083.0 62.3 %reduce-scatter.20.cloned.1.call-done = f32[16,128]{1,0:T(8,128)} async-done(((f32[256,128]{1,0:T(8,128)}), f32[16,128]{1,0:T(8,128)}) %reduce-scatter.20.cloned.1.call-update) | async-done | bytes 8208
  (81 shorter events, 17.2 us)
Async XLA Ops:
  7.2 519.2 %copy-start = (f32[2,256,2,256]{3,2,1,0:T(2,128)S(1)}, f32[2,256,2,256]{3,2,1,0:T(2,128)}, u32[]{:S(2)}) copy-start(f32[2,256,2,256]{3,2,1,0:T(2,128)} %param.9) | copy-start | bytes 3145732
  7.2 7.4 copy-start.7
  7.2 7.7 copy-start.5
  7.2 8.8 copy-start.4
  7.2 104.7 %all-gather.4.cloned.1.call-start = ((), (), s32[]{:S(2)}) async-start(), calls=%async_computation.5 | async-start | bytes 4456448 | tf_op jit(solution)/shard_map/all_gather | solution.py:49
  10.3 201.4 %all-gather.6.cloned.1.call-start = ((), (), s32[]{:S(2)}) async-start(), calls=%async_computation.7 | async-start | bytes 4456448 | tf_op jit(solution)/shard_map/all_gather | solution.py:50
  15.9 280.0 %all-gather.8.cloned.1.call-start = ((), (), s32[]{:S(2)}) async-start(), calls=%async_computation.8 | async-start | bytes 2228224 | tf_op jit(solution)/shard_map/all_gather | solution.py:51
  16.8 509.5 %all-reduce.3.cloned.1.call-start = ((), (), s32[]{:S(2)}) async-start(), calls=%async_computation.13 | async-start | bytes 16777216 | tf_op jit(solution)/shard_map/psum | solution.py:11
  121.4 2.0 copy-start.1
  324.2 417.6 %reduce-scatter.14.cloned.1.call-start = ((), (), s32[]{:S(2)}) async-start(), calls=%async_computation.9 | async-start | bytes 4456448 | tf_op jit(solution)/shard_map/reduce_scatter | solution.py:64
  536.3 416.4 %reduce-scatter.12.cloned.1.call-start = ((), (), s32[]{:S(2)}) async-start(), calls=%async_computation.6 | async-start | bytes 4456448 | tf_op jit(solution)/shard_map/reduce_scatter | solution.py:64
  546.2 0.7 copy-start.9
  546.2 3.2 copy-start.6
  546.2 198.3 %copy-start.8 = (f32[16,128]{1,0:T(8,128)S(1)}, f32[16,128]{1,0:T(8,128)}, u32[]{:S(2)}) copy-start(f32[16,128]{1,0:T(8,128)} %param.17) | copy-start | bytes 24580
  546.3 471.4 %reduce-scatter.18.cloned.1.call-start = ((), (), s32[]{:S(2)}) async-start(), calls=%async_computation.11 | async-start | bytes 139264 | tf_op jit(solution)/shard_map/reduce_scatter | solution.py:94
  741.8 281.2 %copy-start.2 = (f32[2,256,128]{1,2,0:T(8,128)S(1)}, f32[2,256,128]{1,2,0:T(8,128)}, u32[]{:S(2)}) copy-start(f32[2,256,128]{1,2,0:T(8,128)} %reduce-scatter.14.cloned.1.call-done) | copy-start | bytes 786436
  744.3 337.2 %reduce-scatter.16.cloned.1.call-start = ((), (), s32[]{:S(2)}) async-start(), calls=%async_computation.10 | async-start | bytes 139264
  952.7 71.2 %copy-start.3 = (f32[2,256,128]{1,2,0:T(8,128)S(1)}, f32[2,256,128]{1,2,0:T(8,128)}, u32[]{:S(2)}) copy-start(f32[2,256,128]{1,2,0:T(8,128)} %reduce-scatter.12.cloned.1.call-done) | copy-start | bytes 786436
  955.2 190.0 %reduce-scatter.20.cloned.1.call-start = ((), (), s32[]{:S(2)}) async-start(), calls=%async_computation.12 | async-start | bytes 139264
Sparse Core Ops, SparseCore 0:
  11.2 100.6 all-gather.3
  115.1 96.5 all-gather.5
  214.3 81.6 all-gather.7
  324.3 201.9 all-reduce.2
  536.4 205.3 reduce-scatter.13
  746.2 206.4 reduce-scatter.11
  955.8 61.8 reduce-scatter.17
  1020.3 61.1 reduce-scatter.15
  1084.0 61.2 reduce-scatter.19
where the time goes:
time: 1160 us; the launch traced here: 1150 us
  waiting for transfers between devices  993 us (86%)
  local copies, waits for them, and re-layouts  60.8 us (5%)
  matrix products  36.8 us (3%)
  blocking collectives  34.5 us (3%)
  between operations  16.1 us (1%)
  other arithmetic  11.8 us (1%)
    reduce_scatter x2, waiting for transfers between devices, one_level(): lax.psum_scatter(ancestor_product(g_top, stacked_rows(pieces)), 'pcol', s...  361 us
    psum x1, waiting for transfers between devices, broadcast(): return lax.psum(jnp.where(mine, x, jnp.zeros_like(x)), axis)  202 us
    unnamed x11, waiting for transfers between devices  119 us
    all_gather x1, waiting for transfers between devices, local(): lax.all_gather(masked_one, 'pcol', axis=2, tiled=True)  95.1 us
    all_gather x1, waiting for transfers between devices, local(): lax.all_gather(masked_two, 'pcol', axis=2, tiled=True)  80 us
    all_gather x1, waiting for transfers between devices, local(): lax.all_gather(lp_two, 'pcol', axis=1, tiled=True)  72.8 us
    reduce_scatter x1, waiting for transfers between devices, local(): lax.psum_scatter(term_parent.reshape(block_size, col_width), 'prow', scat...  62.4 us
    all_gather x1, blocking collectives, local(): lax.all_gather(dinv_one, 'pcol', axis=1, tiled=True)  34.5 us
  transfers between devices with their start and end apart: 9, of which 9 were waited for; matrix products, arithmetic and copies ran while one was open for 6% of the time, Pallas kernels for 0%

commit v1 on v0

v1 whole, which is shorter than its diff:
```python
import functools

import jax
import jax.numpy as jnp
from jax import lax
from jax.experimental import pallas as pl
from jax.experimental.pallas import tpu as pltpu
from jax.sharding import PartitionSpec as P

ROW_AXES = ("x", "y_lo", "core")
COL_AXES = ("y_hi", "z")
ALL_AXES = ROW_AXES + COL_AXES
exact = lax.Precision.HIGHEST


def split(a):
    hi = a.astype(jnp.bfloat16)
    return hi, (a - hi.astype(jnp.float32)).astype(jnp.bfloat16)


def dot3(a, b):
    f = functools.partial(jnp.dot, preferred_element_type=jnp.float32)
    return f(a[0], b[0]) + (f(a[0], b[1]) + f(a[1], b[0]))


def product_kernel(sc_ref, gh_ref, gl_ref, one_ref, two_ref, par_ref, lp_ref, out_ref):
    h = sc_ref[8]
    lp = jnp.concatenate(
        [jnp.concatenate([lp_ref[0, t], lp_ref[1, t]], axis=0) for t in range(2)], axis=1
    )
    lp = split(lp)
    acc = None
    for k in range(2):
        half = h if k == 0 else 1 - h
        one = jnp.concatenate([one_ref[half, 0], one_ref[half, 1]], axis=1)
        two = jnp.concatenate([two_ref[half, 0], two_ref[half, 1]], axis=1)
        par = jnp.concatenate([par_ref[half, 0], par_ref[half, 1]], axis=1)
        folded = two - dot3(split(par), lp)
        both = split(jnp.concatenate([one, folded], axis=1))
        term = dot3((gh_ref[k], gl_ref[k]), both)
        acc = term if acc is None else acc + term
    for level in range(2):
        for t in range(2):
            col = level * 256 + t * 128
            out_ref[t, level] = -acc[:, col : col + 128]


def product(scalars, g_hi, g_lo, gathered):
    rows = lambda n: (2, 2, n, 128)
    whole = pl.BlockSpec((2, 512, 512), lambda j, sc: (0, 0, 0))
    return pl.pallas_call(
        product_kernel,
        grid_spec=pltpu.PrefetchScalarGridSpec(
            num_scalar_prefetch=1,
            grid=(4,),
            in_specs=[
                whole,
                whole,
                pl.BlockSpec(rows(512), lambda j, sc: (0, j, 0, 0)),
                pl.BlockSpec(rows(512), lambda j, sc: (0, j, 1, 0)),
                pl.BlockSpec(rows(512), lambda j, sc: (0, sc[j], sc[4 + j], 0)),
                pl.BlockSpec(rows(128), lambda j, sc: (0, j, 12, 0)),
            ],
            out_specs=pl.BlockSpec((2, 2, 512, 128), lambda j, sc: (j, 0, 0, 0)),
        ),
        out_shape=jax.ShapeDtypeStruct((8, 2, 512, 128), jnp.float32),
        compiler_params=pltpu.CompilerParams(vmem_limit_bytes=48 * 2**20),
        cost_estimate=pl.CostEstimate(
            flops=8_000_000_000, bytes_accessed=24_000_000, transcendentals=0
        ),
    )(scalars, g_hi, g_lo, gathered, gathered, gathered, gathered)


def swap_pairs(flip):
    pairs = []
    for i in range(256):
        row, col = divmod(i, 16)
        pairs.append((i, (row // 8 * 8 + col % 8) * 16 + (col // 8 ^ flip) * 8 + row % 8))
    return pairs


def ring(n, step):
    return [(i, (i + step) % n) for i in range(n)]


def local(g_top, l_one, struct_one, dinv_one, l_two, lp_two, parent_two, pos_two, dinv_two):
    row = lax.axis_index(ROW_AXES)
    h = lax.axis_index("y_hi")
    z = lax.axis_index("z")
    mine = h * 4 + z // 2
    parent = parent_two[mine]

    blocks = jnp.arange(2, dtype=jnp.int32) * 16 + row
    list_one = lax.dynamic_index_in_dim(struct_one, mine, 0, keepdims=False)
    list_parent = lax.dynamic_index_in_dim(struct_one, parent, 0, keepdims=False)
    places = lax.dynamic_index_in_dim(pos_two, mine, 0, keepdims=False)
    picked = jnp.any(places[:, None] == jnp.arange(16)[None, :], axis=0)
    keep_one = jnp.any(list_one[None, :] == blocks[:, None], axis=1)[:, None, None]
    keep_two = jnp.any((list_parent[None, :] == blocks[:, None]) & picked[None, :], axis=1)
    keep_two = keep_two[:, None, None]
    one = jnp.where(keep_one, l_one, 0.0).reshape(512, 128)
    two = jnp.where(keep_two, l_two, 0.0).reshape(512, 128)

    lp_piece = lax.dynamic_slice_in_dim(lp_two, row // 8 * 128, 128, 0)
    near = lax.ppermute(jnp.concatenate([one, two, lp_piece]), ALL_AXES, swap_pairs(0))
    far = lax.ppermute(one, ALL_AXES, swap_pairs(1))
    payload = jnp.concatenate([near[:1024], far, near[1024:]])
    gathered = lax.all_gather(payload, ROW_AXES, axis=0, tiled=False)
    gathered = gathered.reshape(2, 8, 1664, 128)

    g_other = lax.ppermute(g_top, "y_hi", ring(2, 1))
    g = jnp.stack([g_top, g_other]).reshape(2, 512, 512)
    g_hi32 = lax.reduce_precision(g, 8, 7)
    g_hi = g_hi32.astype(jnp.bfloat16)
    g_lo = (g - g_hi32).astype(jnp.bfloat16)

    packed = jnp.concatenate([one, dinv_one])
    packed_far = lax.ppermute(packed, "y_hi", ring(2, 1))
    pair = jnp.stack([jnp.where(h == 0, packed, packed_far), jnp.where(h == 0, packed_far, packed)])
    pieces = {0: pair}
    right = left = pair
    for d in range(1, 5):
        right = lax.ppermute(right, "z", ring(8, 1))
        pieces[-d] = right
        if d < 4:
            left = lax.ppermute(left, "z", ring(8, -1))
            pieces[d] = left

    def fetch(super_index, part):
        want_h, want_z = super_index // 4, super_index % 4 * 2 + part
        total = jnp.zeros((528, 128), jnp.float32)
        for d, piece in pieces.items():
            for hh in range(2):
                hit = (want_h == hh) & (want_z == (z + d) % 8)
                total = jnp.where(hit, piece[hh], total)
        return total

    par = jnp.concatenate([fetch(parent, 0), fetch(parent, 1)], axis=1)
    sibling = z ^ 1
    one_next = jnp.where(sibling > z, pieces[1][h], pieces[-1][h])[:512]
    two_next = lax.ppermute(two, "z", [(i, i ^ 1) for i in range(8)])
    own_two = jnp.where(z % 2 == 0, jnp.concatenate([two, two_next], 1), jnp.concatenate([two_next, two], 1))
    own_one = jnp.where(z % 2 == 0, jnp.concatenate([one, one_next], 1), jnp.concatenate([one_next, one], 1))

    parents = lax.dynamic_slice_in_dim(parent_two, h * 4, 4, 0)
    place = jnp.where(parents // 4 == h, 0, 2)
    scalars = jnp.concatenate([parents % 4, place, h[None]]).astype(jnp.int32)
    partial = product(scalars, g_hi, g_lo, gathered)
    inverse = lax.psum_scatter(partial, "z", scatter_dimension=0, tiled=False)
    inv_one, inv_two = inverse[0], inverse[1]
    panel_one = jnp.where(keep_one, inv_one.reshape(2, 256, 128), 0.0)
    panel_two = jnp.where(keep_two, inv_two.reshape(2, 256, 128), 0.0)

    dot_t = lambda a, b: lax.dot_general(a, b, (((0,), (0,)), ((), ())), precision=exact)
    lp_pair = lax.dynamic_slice(gathered, (0, z // 2 * 2, 1536, 0), (2, 2, 128, 128))
    lp_own = lp_pair.transpose(0, 2, 1, 3).reshape(256, 256)
    scaled = jnp.dot(par[512:], lp_two, precision=exact)
    lp_slab = lax.dynamic_slice_in_dim(lp_own, row * 16, 16, 0)
    quad = dot_t(lp_slab, scaled)
    term_one = dot_t(own_one, inv_one)
    term_par = dot_t(par[:512], inv_two)
    term_two = quad - dot_t(own_two, inv_two) + dot_t(lp_own, term_par)
    terms = jnp.stack([term_one, term_par, term_two]).reshape(3, 16, 16, 128).transpose(1, 0, 2, 3)
    sums = jnp.sum(lax.all_to_all(terms, ROW_AXES, 0, 0), axis=0)
    diag_one = dinv_one - sums[0]
    parent_rows = -(sums[1] + scaled)
    diag_two = dinv_two + sums[2]
    return (panel_one, diag_one, panel_two, parent_rows, diag_two)


def solution(mesh):
    fine = jax.sharding.Mesh(mesh.devices.reshape(4, 2, 2, 2, 8), ALL_AXES)
    tall = P(None, ROW_AXES, COL_AXES)
    flat = P(ROW_AXES, COL_AXES)
    return jax.shard_map(
        local,
        mesh=fine,
        in_specs=(
            P(None, ROW_AXES, None, COL_AXES),
            tall,
            P(),
            flat,
            tall,
            P(None, COL_AXES),
            P(),
            P(),
            flat,
        ),
        out_specs=(tall, flat, tall, flat, flat),
        check_vma=False,
    )
```

time: 1160 us -> 324 us (0.28)
  waiting for transfers between devices: 993 us -> 217 us
  local copies, waits for them, and re-layouts: 60.8 us -> 11.5 us
  starting transfers between devices: 0.37 us -> 41.7 us
  blocking collectives: 34.5 us -> 0 us
  matrix products: 36.8 us -> 5.87 us
  Pallas kernels: 0 us -> 18.2 us
    reduce_scatter x3 -> x1, waiting for transfers between devices: 424 us -> 0.02 us  [local(): inverse = lax.psum_scatter(partial, 'z', scatter_dimension=0, tiled=False)]
    psum x1 -> x0, waiting for transfers between devices: 202 us -> none  [broadcast(): return lax.psum(jnp.where(mine, x, jnp.zeros_like(x)), axis)]
    all_gather x3 -> x1, waiting for transfers between devices: 248 us -> 95.2 us  [local(): gathered = lax.all_gather(payload, ROW_AXES, axis=0, tiled=False)]
    unnamed x11 -> x2, waiting for transfers between devices: 119 us -> 0.03 us
    ppermute x0 -> x12, waiting for transfers between devices: none -> 114 us  [the longest x4 70.8 us: local(): right = lax.ppermute(right, 'z', ring(8, 1))]
    all_gather x1 -> x0, blocking collectives: 34.5 us -> none  [local(): lax.all_gather(dinv_one, 'pcol', axis=1, tiled=True)]
    ppermute x0 -> x12, starting transfers between devices: none -> 31.1 us  [the longest x4 15.3 us: local(): right = lax.ppermute(right, 'z', ring(8, 1))]
    dot_general x8 -> x6, matrix products: 36.8 us -> 5.87 us  [the longest x5 5.69 us: local(): lax.dot_general(a, b, (((0,), (0,)), ((), ())), precision=exact)]
  transfers between devices with their start and end apart: 9 -> 15, of which waited for: 9 -> 11; matrix products, arithmetic and copies ran while one was open for 6% -> 5% of each run, Pallas kernels for 0% -> 0%
where the time goes in v1:
time: 324 us; the launch traced here: 323 us
  waiting for transfers between devices  217 us (67%)
  starting transfers between devices  41.7 us (13%)
  between operations  18.5 us (6%)
  Pallas kernels  18.2 us (6%)
  local copies, waits for them, and re-layouts  11.5 us (4%)
  other arithmetic  10.8 us (3%)
  matrix products  5.87 us (2%)
    all_gather x1, waiting for transfers between devices, local(): gathered = lax.all_gather(payload, ROW_AXES, axis=0, tiled=False)  95.2 us
    ppermute x4, waiting for transfers between devices, local(): right = lax.ppermute(right, 'z', ring(8, 1))  70.8 us
    ppermute x1, waiting for transfers between devices, local(): g_other = lax.ppermute(g_top, 'y_hi', ring(2, 1))  24.1 us
    pallas_call x1, Pallas kernels, product(): pl.pallas_call(product_kernel, grid_spec=pltpu.PrefetchScalarGridSpec(num...  18.2 us
    ppermute x4, starting transfers between devices, local(): right = lax.ppermute(right, 'z', ring(8, 1))  15.3 us
    all_to_all x1, starting transfers between devices, local(): sums = jnp.sum(lax.all_to_all(terms, ROW_AXES, 0, 0), axis=0)  10.5 us
    all_to_all x1, waiting for transfers between devices, local(): sums = jnp.sum(lax.all_to_all(terms, ROW_AXES, 0, 0), axis=0)  7.65 us
    ppermute x1, waiting for transfers between devices, local(): packed_far = lax.ppermute(packed, 'y_hi', ring(2, 1))  6.71 us
  transfers between devices with their start and end apart: 15, of which 11 were waited for; matrix products, arithmetic and copies ran while one was open for 5% of the time, Pallas kernels for 0%

profile of v1, /device:TPU:1, one launch (start us, length us, event | category | flops | bytes accessed | tf_op | source)
XLA Modules:
  0.0 323.2 jit_solution(16112291572112141213)
XLA Ops:
  7.3 1.2 dynamic_slice.34
  13.3 1.0 broadcast_select_fusion.5
  14.4 5.1 %collective-permute-start.1 = (f32[1152,128]{1,0:T(8,128)S(1)}, f32[1152,128]{1,0:T(8,128)S(1)}, u32[]{:S(2)}, u32[]{:S(2)}) collective-permute-start(f32[1152,128]{1,0:T(8,128)S(1)} %pad_maximum_fusion.1), channel_id=1, source_target_pairs={{0,0},{1,16},{2,32},{3,48},{4,64},{5,80},{6,96},{7,112},{8,8},{9,2... | collective-permute-start | bytes 1769480 | tf_op jit(solution)/shard_map/ppermute | solution.py:105
  19.5 2.7 collective-permute-start.2
  22.2 6.2 %collective-permute-done.1 = f32[1152,128]{1,0:T(8,128)S(1)} collective-permute-done((f32[1152,128]{1,0:T(8,128)S(1)}, f32[1152,128]{1,0:T(8,128)S(1)}, u32[]{:S(2)}, u32[]{:S(2)}) %collective-permute-start.1) | collective-permute-done | bytes 589856 | tf_op jit(solution)/shard_map/ppermute | solution.py:105
  28.5 5.7 %collective-permute-done.2 = f32[512,128]{1,0:T(8,128)S(1)} collective-permute-done((f32[512,128]{1,0:T(8,128)S(1)}, f32[512,128]{1,0:T(8,128)S(1)}, u32[]{:S(2)}, u32[]{:S(2)}) %collective-permute-start.2) | collective-permute-done | bytes 262176 | tf_op jit(solution)/shard_map/ppermute | solution.py:106
  36.5 1.1 constant_dynamic-update-slice_fusion.1
  37.5 24.1 %collective-permute-done = f32[2,256,2,256]{3,2,1,0:T(2,128)} collective-permute-done((f32[2,256,2,256]{3,2,1,0:T(2,128)S(1)}, f32[2,256,2,256]{3,2,1,0:T(2,128)}, u32[]{:S(2)}, u32[]{:S(2)}) %collective-permute-start) | collective-permute-done | bytes 1048608 | tf_op jit(solution)/shard_map/ppermute | solution.py:111
  61.7 2.1 stack.29
  63.7 1.1 constant_dynamic-update-slice_fusion
  64.8 1.9 fusion
  66.7 95.2 %all-gather.3.cloned.1.call-done = f32[26624,128]{1,0:T(8,128)} async-done(((f32[1664,128]{1,0:T(8,128)}), f32[26624,128]{1,0:T(8,128)}) %all-gather.3.cloned.1.call-update) | async-done | bytes 13631504 | tf_op jit(solution)/shard_map/all_gather | solution.py:108
  162.0 18.2 %shard_map.128 = f32[8,2,512,128]{3,2,1,0:T(8,128)} custom-call(s32[9]{0:T(128)S(1)} %pad_add_fusion.sc_ref, bf16[2,512,512]{2,1,0:T(8,128)(2,1)S(1)} %get-tuple-element.10.gh_ref, bf16[2,512,512]{2,1,0:T(8,128)(2,1)S(1)} %get-tuple-element.9.gl_ref, f32[2,8,1664,128]{3,2,1,0:T(8,128)} %bitcast.146, f32[2,8,1664,128]{3,2,1,0:T(8,128)} %bitcast.147, ...), custom_call_target="tpu_custom_call" | custom-call | flops 8000000000 | bytes 24000000 | tf_op jit(solution)/shard_map/pallas_call | solution.py:51
  180.9 2.7 collective-permute-start.3
  183.6 6.7 %collective-permute-done.3 = f32[528,128]{1,0:T(8,128)S(1)} collective-permute-done((f32[528,128]{1,0:T(8,128)S(1)}, f32[528,128]{1,0:T(8,128)S(1)}, u32[]{:S(2)}, u32[]{:S(2)}) %collective-permute-start.3) | collective-permute-done | bytes 270368 | tf_op jit(solution)/shard_map/ppermute | solution.py:118
  190.4 8.7 %collective-permute-start.5 = (f32[2,528,128]{2,1,0:T(8,128)S(1)}, f32[2,528,128]{2,1,0:T(8,128)S(1)}, u32[]{:S(2)}, u32[]{:S(2)}) collective-permute-start(f32[2,528,128]{2,1,0:T(8,128)S(1)} %pad_maximum_fusion.2), channel_id=1, source_target_pairs={{0,1},{1,2},{2,3},{3,4},{4,5},{5,6},{6,7},{7,0},{8,9},{9,10},{10,1... | collective-permute-start | bytes 1622024 | tf_op jit(solution)/shard_map/ppermute | solution.py:123
  199.1 22.7 %collective-permute-done.5 = f32[2,528,128]{2,1,0:T(8,128)S(1)} collective-permute-done((f32[2,528,128]{2,1,0:T(8,128)S(1)}, f32[2,528,128]{2,1,0:T(8,128)S(1)}, u32[]{:S(2)}, u32[]{:S(2)}) %collective-permute-start.5) | collective-permute-done | bytes 540704 | tf_op jit(solution)/shard_map/ppermute | solution.py:123
  221.9 2.3 collective-permute-start.6
  224.2 1.1 collective-permute-start.9
  225.4 21.8 %collective-permute-done.6 = f32[2,528,128]{2,1,0:T(8,128)S(1)} collective-permute-done((f32[2,528,128]{2,1,0:T(8,128)S(1)}, f32[2,528,128]{2,1,0:T(8,128)S(1)}, u32[]{:S(2)}, u32[]{:S(2)}) %collective-permute-start.6) | collective-permute-done | bytes 540704 | tf_op jit(solution)/shard_map/ppermute | solution.py:123
  247.1 2.3 collective-permute-start.7
  249.5 2.4 collective-permute-start.10
  251.9 19.5 %collective-permute-done.7 = f32[2,528,128]{2,1,0:T(8,128)} collective-permute-done((f32[2,528,128]{2,1,0:T(8,128)S(1)}, f32[2,528,128]{2,1,0:T(8,128)}, u32[]{:S(2)}, u32[]{:S(2)}) %collective-permute-start.7) | collective-permute-done | bytes 540704 | tf_op jit(solution)/shard_map/ppermute | solution.py:123
  271.4 2.0 collective-permute-start.8
  273.4 1.6 collective-permute-start.11
  278.3 6.8 %collective-permute-done.8 = f32[2,528,128]{2,1,0:T(8,128)} collective-permute-done((f32[2,528,128]{2,1,0:T(8,128)}, f32[2,528,128]{2,1,0:T(8,128)}, u32[]{:S(2)}, u32[]{:S(2)}) %collective-permute-start.8) | collective-permute-done | bytes 540704 | tf_op jit(solution)/shard_map/ppermute | solution.py:123
  285.1 1.8 select_select_fusion
  286.8 1.8 select_select_fusion.1
  290.5 2.0 fusion.2
  292.5 2.1 convolution_subtract_fusion
  296.6 10.5 %all-to-all-start = ((f32[16,3,16,128]{3,2,1,0:T(8,128)}), f32[16,3,16,128]{3,2,1,0:T(8,128)S(1)}, u32[]{:S(2)}, u32[]{:S(2)}) async-start(f32[16,3,16,128]{3,2,1,0:T(8,128)} %copy.22), calls=%async_computation.1 | async-start | bytes 786432 | tf_op jit(solution)/shard_map/all_to_all | solution.py:164
  308.1 7.6 %all-to-all-done = f32[16,3,16,128]{3,2,1,0:T(8,128)S(1)} async-done(((f32[16,3,16,128]{3,2,1,0:T(8,128)}), f32[16,3,16,128]{3,2,1,0:T(8,128)S(1)}, u32[]{:S(2)}, u32[]{:S(2)}) %all-to-all-start) | async-done | bytes 393248 | tf_op jit(solution)/shard_map/all_to_all | solution.py:164
  (59 shorter events, 12.5 us)
Async XLA Ops:
  7.2 3.5 %copy-start = (f32[256,128]{1,0:T(8,128)S(1)}, f32[256,128]{1,0:T(8,128)}, u32[]{:S(2)}) copy-start(f32[256,128]{1,0:T(8,128)} %param.14) | copy-start | bytes 393220
  7.2 154.8 %all-gather.3.cloned.1.call-start = ((), (), s32[]{:S(2)}) async-start(), calls=%async_computation.3 | async-start | bytes 14483456 | tf_op jit(solution)/shard_map/all_gather | solution.py:108
  14.4 20.9 %copy-start.3 = (f32[2,256,2,256]{3,2,1,0:T(2,128)S(1)}, f32[2,256,2,256]{3,2,1,0:T(2,128)}, u32[]{:S(2)}) copy-start(f32[2,256,2,256]{3,2,1,0:T(2,128)} %param.9) | copy-start | bytes 3145732
  14.4 14.0 %collective-permute-start.1 = (f32[1152,128]{1,0:T(8,128)S(1)}, f32[1152,128]{1,0:T(8,128)S(1)}, u32[]{:S(2)}, u32[]{:S(2)}) collective-permute-start(f32[1152,128]{1,0:T(8,128)S(1)} %pad_maximum_fusion.1), channel_id=1, source_target_pairs={{0,0},{1,16},{2,32},{3,48},{4,64},{5,80},{6,96},{7,112},{8,8},{9,2... | collective-permute-start | bytes 1769480 | tf_op jit(solution)/shard_map/ppermute | solution.py:105
  19.5 14.8 %collective-permute-start.2 = (f32[512,128]{1,0:T(8,128)S(1)}, f32[512,128]{1,0:T(8,128)S(1)}, u32[]{:S(2)}, u32[]{:S(2)}) collective-permute-start(f32[512,128]{1,0:T(8,128)S(1)} %bitcast.152), channel_id=1, source_target_pairs={{0,8},{1,24},{2,40},{3,56},{4,72},{5,88},{6,104},{7,120},{8,0},{9,... | collective-permute-start | bytes 786440 | tf_op jit(solution)/shard_map/ppermute | solution.py:106
  28.5 7.8 %copy-start.6 = (s32[8]{0:T(128)S(1)}, s32[8]{0:T(128)}, u32[]{:S(2)}) copy-start(s32[8]{0:T(128)} %param.15) | copy-start | bytes 100
  35.2 255.2 %reduce-scatter.2.cloned.1.call-start = ((), (), s32[]{:S(2)}) async-start(), calls=%async_computation.2 | async-start | bytes 4718592 | tf_op jit(solution)/shard_map/reduce_scatter | solution.py:149
  35.3 26.4 %collective-permute-start = (f32[2,256,2,256]{3,2,1,0:T(2,128)S(1)}, f32[2,256,2,256]{3,2,1,0:T(2,128)}, u32[]{:S(2)}, u32[]{:S(2)}) collective-permute-start(f32[2,256,2,256]{3,2,1,0:T(2,128)S(1)} %copy-done.3), channel_id=1, source_target_pairs={{0,8},{8,0},{1,9},{9,1},{2,10},{10,2},{3,11},{11,3},{4,12},{12,4},... | collective-permute-start | bytes 3145736 | tf_op jit(solution)/shard_map/ppermute | solution.py:111
  180.2 0.7 copy-start.4
  180.9 9.4 %collective-permute-start.3 = (f32[528,128]{1,0:T(8,128)S(1)}, f32[528,128]{1,0:T(8,128)S(1)}, u32[]{:S(2)}, u32[]{:S(2)}) collective-permute-start(f32[528,128]{1,0:T(8,128)S(1)} %pad_maximum_fusion.3), channel_id=1, source_target_pairs={{0,8},{8,0},{1,9},{9,1},{2,10},{10,2},{3,11},{11,3},{4,12},{12,4},... | collective-permute-start | bytes 811016 | tf_op jit(solution)/shard_map/ppermute | solution.py:118
  190.4 31.4 %collective-permute-start.5 = (f32[2,528,128]{2,1,0:T(8,128)S(1)}, f32[2,528,128]{2,1,0:T(8,128)S(1)}, u32[]{:S(2)}, u32[]{:S(2)}) collective-permute-start(f32[2,528,128]{2,1,0:T(8,128)S(1)} %pad_maximum_fusion.2), channel_id=1, source_target_pairs={{0,1},{1,2},{2,3},{3,4},{4,5},{5,6},{6,7},{7,0},{8,9},{9,10},{10,1... | collective-permute-start | bytes 1622024 | tf_op jit(solution)/shard_map/ppermute | solution.py:123
  199.1 25.1 %collective-permute-start.4 = (f32[2,528,128]{2,1,0:T(8,128)S(1)}, f32[2,528,128]{2,1,0:T(8,128)S(1)}, u32[]{:S(2)}, u32[]{:S(2)}) collective-permute-start(f32[2,528,128]{2,1,0:T(8,128)S(1)} %pad_maximum_fusion.2), channel_id=1, source_target_pairs={{0,7},{1,0},{2,1},{3,2},{4,3},{5,4},{6,5},{7,6},{8,15},{9,8},{10,9... | collective-permute-start | bytes 1622024 | tf_op jit(solution)/shard_map/ppermute | solution.py:126
  221.9 25.3 %collective-permute-start.6 = (f32[2,528,128]{2,1,0:T(8,128)S(1)}, f32[2,528,128]{2,1,0:T(8,128)S(1)}, u32[]{:S(2)}, u32[]{:S(2)}) collective-permute-start(f32[2,528,128]{2,1,0:T(8,128)S(1)} %collective-permute-done.5), channel_id=1, source_target_pairs={{0,1},{1,2},{2,3},{3,4},{4,5},{5,6},{6,7},{7,0},{8,9},{9,10},{10,1... | collective-permute-start | bytes 1622024 | tf_op jit(solution)/shard_map/ppermute | solution.py:123
  224.2 25.2 %collective-permute-start.9 = (f32[2,528,128]{2,1,0:T(8,128)S(1)}, f32[2,528,128]{2,1,0:T(8,128)}, u32[]{:S(2)}, u32[]{:S(2)}) collective-permute-start(f32[2,528,128]{2,1,0:T(8,128)S(1)} %collective-permute-done.4), channel_id=1, source_target_pairs={{0,7},{1,0},{2,1},{3,2},{4,3},{5,4},{6,5},{7,6},{8,15},{9,8},{10,9... | collective-permute-start | bytes 1622024 | tf_op jit(solution)/shard_map/ppermute | solution.py:126
  247.1 24.2 %collective-permute-start.7 = (f32[2,528,128]{2,1,0:T(8,128)S(1)}, f32[2,528,128]{2,1,0:T(8,128)}, u32[]{:S(2)}, u32[]{:S(2)}) collective-permute-start(f32[2,528,128]{2,1,0:T(8,128)S(1)} %collective-permute-done.6), channel_id=1, source_target_pairs={{0,1},{1,2},{2,3},{3,4},{4,5},{5,6},{6,7},{7,0},{8,9},{9,10},{10,1... | collective-permute-start | bytes 1622024 | tf_op jit(solution)/shard_map/ppermute | solution.py:123
  249.5 28.8 %collective-permute-start.10 = (f32[2,528,128]{2,1,0:T(8,128)}, f32[2,528,128]{2,1,0:T(8,128)}, u32[]{:S(2)}, u32[]{:S(2)}) collective-permute-start(f32[2,528,128]{2,1,0:T(8,128)} %collective-permute-done.9), channel_id=1, source_target_pairs={{0,7},{1,0},{2,1},{3,2},{4,3},{5,4},{6,5},{7,6},{8,15},{9,8},{10,9... | collective-permute-start | bytes 1622024 | tf_op jit(solution)/shard_map/ppermute | solution.py:126
  271.4 13.7 %collective-permute-start.8 = (f32[2,528,128]{2,1,0:T(8,128)}, f32[2,528,128]{2,1,0:T(8,128)}, u32[]{:S(2)}, u32[]{:S(2)}) collective-permute-start(f32[2,528,128]{2,1,0:T(8,128)} %collective-permute-done.7), channel_id=1, source_target_pairs={{0,1},{1,2},{2,3},{3,4},{4,5},{5,6},{6,7},{7,0},{8,9},{9,10},{10,1... | collective-permute-start | bytes 1622024 | tf_op jit(solution)/shard_map/ppermute | solution.py:123
  273.4 19.1 %collective-permute-start.11 = (f32[512,128]{1,0:T(8,128)S(1)}, f32[512,128]{1,0:T(8,128)}, u32[]{:S(2)}, u32[]{:S(2)}) collective-permute-start(f32[512,128]{1,0:T(8,128)S(1)} %bitcast.165), channel_id=1, source_target_pairs={{0,1},{1,0},{2,3},{3,2},{4,5},{5,4},{6,7},{7,6},{8,9},{9,8},{10,11... | collective-permute-start | bytes 786440 | tf_op jit(solution)/shard_map/ppermute | solution.py:141
  289.8 5.4 %copy-start.2 = (f32[256,512]{1,0:T(8,128)S(1)}, f32[256,512]{1,0:T(8,128)}, u32[]{:S(2)}) copy-start(f32[256,512]{1,0:T(8,128)} %copy.20) | copy-start | bytes 1572868
  290.5 4.8 %copy-start.1 = (f32[1,2,512,128]{3,2,1,0:T(8,128)S(1)}, f32[1,2,512,128]{3,2,1,0:T(8,128)}, u32[]{:S(2)}) copy-start(f32[1,2,512,128]{3,2,1,0:T(8,128)} %reduce-scatter.2.cloned.1.call-done) | copy-start | bytes 1572868
  295.9 19.9 %copy-start.5 = (f32[16,128]{1,0:T(8,128)S(1)}, f32[16,128]{1,0:T(8,128)}, u32[]{:S(2)}) copy-start(f32[16,128]{1,0:T(8,128)} %param.17) | copy-start | bytes 24580
  296.6 19.1 %all-to-all-start = ((f32[16,3,16,128]{3,2,1,0:T(8,128)}), f32[16,3,16,128]{3,2,1,0:T(8,128)S(1)}, u32[]{:S(2)}, u32[]{:S(2)}) async-start(f32[16,3,16,128]{3,2,1,0:T(8,128)} %copy.22), calls=%async_computation.1 | async-start | bytes 786432 | tf_op jit(solution)/shard_map/all_to_all | solution.py:164
Sparse Core Ops, SparseCore 0:
  35.3 126.5 all-gather.2
  180.3 90.3 reduce-scatter.1

commit v2 on v1

--- a/solution.py
+++ b/solution.py
@@ -23,59 +23,105 @@
     return f(a[0], b[0]) + (f(a[0], b[1]) + f(a[1], b[0]))
 
 
-def product_kernel(sc_ref, gh_ref, gl_ref, one_ref, two_ref, par_ref, lp_ref, out_ref):
-    h = sc_ref[8]
-    lp = jnp.concatenate(
-        [jnp.concatenate([lp_ref[0, t], lp_ref[1, t]], axis=0) for t in range(2)], axis=1
-    )
+def one_kernel(sc_ref, gh_ref, gl_ref, one_ref, out_ref):
+    h = sc_ref[0]
+    acc = None
+    for k in range(2):
+        half = h if k == 0 else 1 - h
+        one = jnp.concatenate([one_ref[half, 0, 0, 0], one_ref[half, 0, 0, 1]], axis=1)
+        term = dot3((gh_ref[k], gl_ref[k]), split(one))
+        acc = term if acc is None else acc + term
+    out_ref[0] = -acc[:, :128]
+    out_ref[1] = -acc[:, 128:]
+
+
+def two_kernel(sc_ref, gh_ref, gl_ref, two_ref, par_ref, lp_ref, out_ref):
+    h = sc_ref[0]
+    lp = jnp.concatenate([lp_ref[0, 0, 0, 0], lp_ref[1, 0, 0, 0]], axis=0)
     lp = split(lp)
     acc = None
     for k in range(2):
         half = h if k == 0 else 1 - h
-        one = jnp.concatenate([one_ref[half, 0], one_ref[half, 1]], axis=1)
-        two = jnp.concatenate([two_ref[half, 0], two_ref[half, 1]], axis=1)
-        par = jnp.concatenate([par_ref[half, 0], par_ref[half, 1]], axis=1)
-        folded = two - dot3(split(par), lp)
-        both = split(jnp.concatenate([one, folded], axis=1))
-        term = dot3((gh_ref[k], gl_ref[k]), both)
+        par = jnp.concatenate([par_ref[half, 0, 0, 0], par_ref[half, 0, 0, 1]], axis=1)
+        folded = two_ref[half, 0, 0, 0] - dot3(split(par), lp)
+        term = dot3((gh_ref[k], gl_ref[k]), split(folded))
         acc = term if acc is None else acc + term
-    for level in range(2):
-        for t in range(2):
-            col = level * 256 + t * 128
-            out_ref[t, level] = -acc[:, col : col + 128]
-
-
-def product(scalars, g_hi, g_lo, gathered):
-    rows = lambda n: (2, 2, n, 128)
-    whole = pl.BlockSpec((2, 512, 512), lambda j, sc: (0, 0, 0))
+    out_ref[0] = -acc
+
+
+WHOLE_G = pl.BlockSpec((2, 512, 512), lambda i, sc: (0, 0, 0))
+PARAMS = pltpu.CompilerParams(vmem_limit_bytes=40 * 2**20)
+
+
+def cost(slots, side):
+    return pl.CostEstimate(
+        flops=slots * 512 * (1024 + side) * 128 * 6,
+        bytes_accessed=2**21 + slots * (2**20 + side * 4096),
+        transcendentals=0,
+    )
+
+
+def product_one(h, g_hi, g_lo, gathered):
     return pl.pallas_call(
-        product_kernel,
+        one_kernel,
         grid_spec=pltpu.PrefetchScalarGridSpec(
             num_scalar_prefetch=1,
             grid=(4,),
             in_specs=[
-                whole,
-                whole,
-                pl.BlockSpec(rows(512), lambda j, sc: (0, j, 0, 0)),
-                pl.BlockSpec(rows(512), lambda j, sc: (0, j, 1, 0)),
-                pl.BlockSpec(rows(512), lambda j, sc: (0, sc[j], sc[4 + j], 0)),
-                pl.BlockSpec(rows(128), lambda j, sc: (0, j, 12, 0)),
+                WHOLE_G,
+                WHOLE_G,
+                pl.BlockSpec((2, 1, 1, 2, 512, 128), lambda j, sc: (0, j // 2, sc[0], j % 2, 0, 0)),
             ],
-            out_specs=pl.BlockSpec((2, 2, 512, 128), lambda j, sc: (j, 0, 0, 0)),
+            out_specs=pl.BlockSpec((2, 512, 128), lambda j, sc: (j, 0, 0)),
         ),
-        out_shape=jax.ShapeDtypeStruct((8, 2, 512, 128), jnp.float32),
-        compiler_params=pltpu.CompilerParams(vmem_limit_bytes=48 * 2**20),
-        cost_estimate=pl.CostEstimate(
-            flops=8_000_000_000, bytes_accessed=24_000_000, transcendentals=0
+        out_shape=jax.ShapeDtypeStruct((8, 512, 128), jnp.float32),
+        compiler_params=PARAMS,
+        cost_estimate=cost(8, 0),
+    )(h[None], g_hi, g_lo, gathered)
+
+
+def product_two(h, slots, parents, g_hi, g_lo, gathered):
+    n = slots.shape[0]
+    scalars = jnp.concatenate([h[None], slots, parents]).astype(jnp.int32)
+    par_map = lambda i, sc: (
+        0,
+        sc[1 + n + i] % 4 // 2,
+        sc[1 + n + i] // 4,
+        sc[1 + n + i] % 2,
+        0,
+        0,
+    )
+    return pl.pallas_call(
+        two_kernel,
+        grid_spec=pltpu.PrefetchScalarGridSpec(
+            num_scalar_prefetch=1,
+            grid=(n,),
+            in_specs=[
+                WHOLE_G,
+                WHOLE_G,
+                pl.BlockSpec(
+                    (2, 1, 1, 1, 512, 128),
+                    lambda i, sc: (0, sc[1 + i] // 4, sc[0], sc[1 + i] % 4, 1, 0),
+                ),
+                pl.BlockSpec((2, 1, 1, 2, 512, 128), par_map),
+                pl.BlockSpec(
+                    (2, 1, 1, 1, 128, 128),
+                    lambda i, sc: (0, sc[1 + i] // 4, sc[0], sc[1 + i] % 4, 8, 0),
+                ),
+            ],
+            out_specs=pl.BlockSpec((1, 512, 128), lambda i, sc: (i, 0, 0)),
         ),
-    )(scalars, g_hi, g_lo, gathered, gathered, gathered, gathered)
-
-
-def swap_pairs(flip):
+        out_shape=jax.ShapeDtypeStruct((n, 512, 128), jnp.float32),
+        compiler_params=PARAMS,
+        cost_estimate=cost(n, 512),
+    )(scalars, g_hi, g_lo, gathered, gathered, gathered)
+
+
+def swap_pairs():
     pairs = []
     for i in range(256):
         row, col = divmod(i, 16)
-        pairs.append((i, (row // 8 * 8 + col % 8) * 16 + (col // 8 ^ flip) * 8 + row % 8))
+        pairs.append((i, (row // 8 * 8 + col % 8) * 16 + col // 8 * 8 + row % 8))
     return pairs
 
 
@@ -102,11 +148,12 @@
     two = jnp.where(keep_two, l_two, 0.0).reshape(512, 128)
 
     lp_piece = lax.dynamic_slice_in_dim(lp_two, row // 8 * 128, 128, 0)
-    near = lax.ppermute(jnp.concatenate([one, two, lp_piece]), ALL_AXES, swap_pairs(0))
-    far = lax.ppermute(one, ALL_AXES, swap_pairs(1))
-    payload = jnp.concatenate([near[:1024], far, near[1024:]])
-    gathered = lax.all_gather(payload, ROW_AXES, axis=0, tiled=False)
-    gathered = gathered.reshape(2, 8, 1664, 128)
+    near = lax.ppermute(jnp.concatenate([one, two, lp_piece]), ALL_AXES, swap_pairs())
+    near, g_top, packed, two_sent = lax.optimization_barrier(
+        (near, g_top, jnp.concatenate([one, dinv_one]), two)
+    )
+    gathered = lax.all_gather(near, ("x", "y_hi", "y_lo", "core"), axis=0, tiled=False)
+    gathered = gathered.reshape(2, 2, 2, 4, 1152, 128)
 
     g_other = lax.ppermute(g_top, "y_hi", ring(2, 1))
     g = jnp.stack([g_top, g_other]).reshape(2, 512, 512)
@@ -114,7 +161,6 @@
     g_hi = g_hi32.astype(jnp.bfloat16)
     g_lo = (g - g_hi32).astype(jnp.bfloat16)
 
-    packed = jnp.concatenate([one, dinv_one])
     packed_far = lax.ppermute(packed, "y_hi", ring(2, 1))
     pair = jnp.stack([jnp.where(h == 0, packed, packed_far), jnp.where(h == 0, packed_far, packed)])
     pieces = {0: pair}
@@ -138,22 +184,38 @@
     par = jnp.concatenate([fetch(parent, 0), fetch(parent, 1)], axis=1)
     sibling = z ^ 1
     one_next = jnp.where(sibling > z, pieces[1][h], pieces[-1][h])[:512]
-    two_next = lax.ppermute(two, "z", [(i, i ^ 1) for i in range(8)])
+    two_next = lax.ppermute(two_sent, "z", [(i, i ^ 1) for i in range(8)])
     own_two = jnp.where(z % 2 == 0, jnp.concatenate([two, two_next], 1), jnp.concatenate([two_next, two], 1))
     own_one = jnp.where(z % 2 == 0, jnp.concatenate([one, one_next], 1), jnp.concatenate([one_next, one], 1))
 
-    parents = lax.dynamic_slice_in_dim(parent_two, h * 4, 4, 0)
-    place = jnp.where(parents // 4 == h, 0, 2)
-    scalars = jnp.concatenate([parents % 4, place, h[None]]).astype(jnp.int32)
-    partial = product(scalars, g_hi, g_lo, gathered)
-    inverse = lax.psum_scatter(partial, "z", scatter_dimension=0, tiled=False)
-    inv_one, inv_two = inverse[0], inverse[1]
+    h_now, par, own_one, own_two = lax.optimization_barrier((h, par, own_one, own_two))
+    part_one = product_one(h_now, g_hi, g_lo, gathered)
+    inv_one = lax.psum_scatter(part_one, "z", scatter_dimension=0, tiled=False)
+
+    def level_two(steps, h_in):
+        slots = (z + jnp.array(steps, jnp.int32)) % 8
+        parents = jnp.take(parent_two, h * 4 + slots // 2)
+        return product_two(h_in, slots, parents, g_hi, g_lo, gathered)
+
+    h_next, part_one = lax.optimization_barrier((h_now, part_one[0, :8]))
+    first = level_two((4, 5), h_next)
+    h_last, first = lax.optimization_barrier((h_next, first))
+    rest = level_two((3, 6, 2, 7, 1, 0), h_last)
+    up, down = first[0], first[1]
+    for d in range(3):
+        up = lax.ppermute(up, "z", ring(8, 1)) + rest[2 * d]
+        down = lax.ppermute(down, "z", ring(8, -1))
+        if d < 2:
+            down = down + rest[2 * d + 1]
+    inv_two = lax.ppermute(up, "z", ring(8, 1)) + down + rest[5]
     panel_one = jnp.where(keep_one, inv_one.reshape(2, 256, 128), 0.0)
     panel_two = jnp.where(keep_two, inv_two.reshape(2, 256, 128), 0.0)
 
     dot_t = lambda a, b: lax.dot_general(a, b, (((0,), (0,)), ((), ())), precision=exact)
-    lp_pair = lax.dynamic_slice(gathered, (0, z // 2 * 2, 1536, 0), (2, 2, 128, 128))
-    lp_own = lp_pair.transpose(0, 2, 1, 3).reshape(256, 256)
+    lp_pair = lax.dynamic_slice(
+        gathered, (0, z // 4, h, z % 4 // 2 * 2, 1024, 0), (2, 1, 1, 2, 128, 128)
+    )
+    lp_own = lp_pair.reshape(2, 2, 128, 128).transpose(0, 2, 1, 3).reshape(256, 256)
     scaled = jnp.dot(par[512:], lp_two, precision=exact)
     lp_slab = lax.dynamic_slice_in_dim(lp_own, row * 16, 16, 0)
     quad = dot_t(lp_slab, scaled)

time: 324 us -> 268 us (0.83)
  waiting for transfers between devices: 217 us -> 106 us
  starting transfers between devices: 41.7 us -> 77 us
  Pallas kernels: 18.2 us -> 28.7 us
  other arithmetic: 10.8 us -> 16.7 us
  local copies, waits for them, and re-layouts: 11.5 us -> 15.3 us
    ppermute x4, waiting for transfers between devices: 70.8 us -> 11.2 us  [local(): right = lax.ppermute(right, 'z', ring(8, 1))]
    all_gather x1, waiting for transfers between devices: 95.2 us -> 46.5 us  [local(): lax.all_gather(near, ('x', 'y_hi', 'y_lo', 'core'), axis=0, tiled=False)]
    ppermute x3, starting transfers between devices: 3.53 us -> 32.9 us  [local(): left = lax.ppermute(left, 'z', ring(8, -1))]
    ppermute x1, waiting for transfers between devices: 24.1 us -> 2.11 us  [local(): g_other = lax.ppermute(g_top, 'y_hi', ring(2, 1))]
    ppermute x3 -> x9, waiting for transfers between devices: 12 us -> 31 us  [the longest x3 19.6 us: local(): up = lax.ppermute(up, 'z', ring(8, 1)) + rest[2 * d]]
    pallas_call x1 -> x3, Pallas kernels: 18.2 us -> 28.7 us  [the longest x2 23.1 us: product_two(): pl.pallas_call(two_kernel, grid_spec=pltpu.PrefetchScalarGridSpec(num_sca...]
    ppermute x3 -> x9, starting transfers between devices: 9.4 us -> 16.1 us  [the longest x3 7.21 us: local(): down = lax.ppermute(down, 'z', ring(8, -1))]
    ppermute x3, waiting for transfers between devices: 0.11 us -> 4.06 us  [local(): left = lax.ppermute(left, 'z', ring(8, -1))]
  transfers between devices with their start and end apart: 15 -> 21, of which waited for: 11 -> 13; matrix products, arithmetic and copies ran while one was open for 5% -> 9% of each run, Pallas kernels for 0% -> 9%
where the time goes in v2:
time: 268 us; the launch traced here: 267 us
  waiting for transfers between devices  106 us (40%)
  starting transfers between devices  77 us (29%)
  Pallas kernels  28.7 us (11%)
  between operations  18.6 us (7%)
  other arithmetic  16.7 us (6%)
  local copies, waits for them, and re-layouts  15.3 us (6%)
  matrix products  4.76 us (2%)
    all_gather x1, waiting for transfers between devices, local(): lax.all_gather(near, ('x', 'y_hi', 'y_lo', 'core'), axis=0, tiled=False)  46.5 us
    ppermute x3, starting transfers between devices, local(): left = lax.ppermute(left, 'z', ring(8, -1))  32.9 us
    pallas_call x2, Pallas kernels, product_two(): pl.pallas_call(two_kernel, grid_spec=pltpu.PrefetchScalarGridSpec(num_sca...  23.1 us
    ppermute x3, waiting for transfers between devices, local(): up = lax.ppermute(up, 'z', ring(8, 1)) + rest[2 * d]  19.6 us
    ppermute x4, starting transfers between devices, local(): right = lax.ppermute(right, 'z', ring(8, 1))  14.3 us
    ppermute x4, waiting for transfers between devices, local(): right = lax.ppermute(right, 'z', ring(8, 1))  11.2 us
    ppermute x1, waiting for transfers between devices, local(): lax.ppermute(jnp.concatenate([one, two, lp_piece]), ALL_AXES, swap_pairs())  8.92 us
    all_to_all x1, starting transfers between devices, local(): sums = jnp.sum(lax.all_to_all(terms, ROW_AXES, 0, 0), axis=0)  7.53 us
  transfers between devices with their start and end apart: 21, of which 13 were waited for; matrix products, arithmetic and copies ran while one was open for 9% of the time, Pallas kernels for 9%

profile of v2, /device:TPU:1, one launch (start us, length us, event | category | flops | bytes accessed | tf_op | source)
XLA Modules:
  0.0 266.8 jit_solution(14389220078799575573)
XLA Ops:
  15.1 4.9 %collective-permute-start = (f32[1152,128]{1,0:T(8,128)S(1)}, f32[1152,128]{1,0:T(8,128)S(1)}, u32[]{:S(2)}, u32[]{:S(2)}) collective-permute-start(f32[1152,128]{1,0:T(8,128)S(1)} %pad_maximum_fusion), channel_id=1, source_target_pairs={{0,0},{1,16},{2,32},{3,48},{4,64},{5,80},{6,96},{7,112},{8,8},{9,2... | collective-permute-start | bytes 1769480 | tf_op jit(solution)/shard_map/ppermute | solution.py:151
  20.1 8.9 %collective-permute-done = f32[1152,128]{1,0:T(8,128)S(1)} collective-permute-done((f32[1152,128]{1,0:T(8,128)S(1)}, f32[1152,128]{1,0:T(8,128)S(1)}, u32[]{:S(2)}, u32[]{:S(2)}) %collective-permute-start) | collective-permute-done | bytes 589856 | tf_op jit(solution)/shard_map/ppermute | solution.py:151
  29.9 3.0 %collective-permute-start.1 = (f32[528,128]{1,0:T(8,128)S(1)}, f32[528,128]{1,0:T(8,128)S(1)}, u32[]{:S(2)}, u32[]{:S(2)}) collective-permute-start(f32[528,128]{1,0:T(8,128)S(1)} %pad_maximum_fusion.3), channel_id=1, source_target_pairs={{0,8},{8,0},{1,9},{9,1},{2,10},{10,2},{3,11},{11,3},{4,12},{12,4},... | collective-permute-start | bytes 811016 | tf_op jit(solution)/shard_map/ppermute | solution.py:164
  32.9 3.9 %collective-permute-done.1 = f32[528,128]{1,0:T(8,128)S(1)} collective-permute-done((f32[528,128]{1,0:T(8,128)S(1)}, f32[528,128]{1,0:T(8,128)S(1)}, u32[]{:S(2)}, u32[]{:S(2)}) %collective-permute-start.1) | collective-permute-done | bytes 270368 | tf_op jit(solution)/shard_map/ppermute | solution.py:164
  37.0 32.9 %collective-permute-start.6 = (f32[2,528,128]{2,1,0:T(8,128)S(1)}, f32[2,528,128]{2,1,0:T(8,128)S(1)}, u32[]{:S(2)}, u32[]{:S(2)}) collective-permute-start(f32[2,528,128]{2,1,0:T(8,128)S(1)} %pad_maximum_fusion.1), channel_id=1, source_target_pairs={{0,7},{1,0},{2,1},{3,2},{4,3},{5,4},{6,5},{7,6},{8,15},{9,8},{10,9... | collective-permute-start | bytes 1622024 | tf_op jit(solution)/shard_map/ppermute | solution.py:172
  69.9 6.7 %collective-permute-done.2 = f32[2,528,128]{2,1,0:T(8,128)S(1)} collective-permute-done((f32[2,528,128]{2,1,0:T(8,128)S(1)}, f32[2,528,128]{2,1,0:T(8,128)S(1)}, u32[]{:S(2)}, u32[]{:S(2)}) %collective-permute-start.2) | collective-permute-done | bytes 540704 | tf_op jit(solution)/shard_map/ppermute | solution.py:169
  76.5 7.4 %collective-permute-start.3 = (f32[2,528,128]{2,1,0:T(8,128)S(1)}, f32[2,528,128]{2,1,0:T(8,128)}, u32[]{:S(2)}, u32[]{:S(2)}) collective-permute-start(f32[2,528,128]{2,1,0:T(8,128)S(1)} %collective-permute-done.2), channel_id=1, source_target_pairs={{0,1},{1,2},{2,3},{3,4},{4,5},{5,6},{6,7},{7,0},{8,9},{9,10},{10,1... | collective-permute-start | bytes 1622024 | tf_op jit(solution)/shard_map/ppermute | solution.py:169
  83.9 3.0 %collective-permute-start.10 = (f32[2,256,2,256]{3,2,1,0:T(2,128)}, f32[2,256,2,256]{3,2,1,0:T(2,128)}, u32[]{:S(2)}, u32[]{:S(2)}) collective-permute-start(f32[2,256,2,256]{3,2,1,0:T(2,128)} %param.11), channel_id=1, source_target_pairs={{0,8},{8,0},{1,9},{9,1},{2,10},{10,2},{3,11},{11,3},{4,12},{12,4},... | collective-permute-start | bytes 3145736 | tf_op jit(solution)/shard_map/ppermute | solution.py:158
  89.0 2.4 collective-permute-start.9
  92.0 4.6 %collective-permute-start.4 = (f32[2,528,128]{2,1,0:T(8,128)}, f32[2,528,128]{2,1,0:T(8,128)}, u32[]{:S(2)}, u32[]{:S(2)}) collective-permute-start(f32[2,528,128]{2,1,0:T(8,128)} %collective-permute-done.3), channel_id=1, source_target_pairs={{0,1},{1,2},{2,3},{3,4},{4,5},{5,6},{6,7},{7,0},{8,9},{9,10},{10,1... | collective-permute-start | bytes 1622024 | tf_op jit(solution)/shard_map/ppermute | solution.py:169
  96.7 2.1 stack.31
  99.8 2.1 maximum_select_fusion.1
  101.9 4.1 %collective-permute-done.7 = f32[2,528,128]{2,1,0:T(8,128)} collective-permute-done((f32[2,528,128]{2,1,0:T(8,128)S(1)}, f32[2,528,128]{2,1,0:T(8,128)}, u32[]{:S(2)}, u32[]{:S(2)}) %collective-permute-start.7) | collective-permute-done | bytes 540704 | tf_op jit(solution)/shard_map/ppermute | solution.py:172
  106.0 3.6 %collective-permute-done.4 = f32[2,528,128]{2,1,0:T(8,128)} collective-permute-done((f32[2,528,128]{2,1,0:T(8,128)}, f32[2,528,128]{2,1,0:T(8,128)}, u32[]{:S(2)}, u32[]{:S(2)}) %collective-permute-start.4) | collective-permute-done | bytes 540704 | tf_op jit(solution)/shard_map/ppermute | solution.py:169
  109.5 2.2 collective-permute-start.5
  112.6 2.1 collective-permute-done.10
  114.7 2.1 stack.32
  117.8 2.0 fusion
  120.3 2.0 select_select_fusion.1
  122.2 2.0 select_select_fusion
  124.3 46.5 %all-gather.3.cloned.1.call-done = f32[36864,128]{1,0:T(8,128)} async-done(((f32[1152,128]{1,0:T(8,128)}), f32[36864,128]{1,0:T(8,128)}) %all-gather.3.cloned.1.call-update) | async-done | bytes 18874384 | tf_op jit(solution)/shard_map/all_gather | solution.py:155
  170.7 5.5 %shard_map.146 = f32[8,512,128]{2,1,0:T(8,128)S(1)} custom-call(s32[1]{0:T(128)} %bitcast.23.sc_ref, bf16[2,512,512]{2,1,0:T(8,128)(2,1)S(1)} %get-tuple-element.32.gh_ref, bf16[2,512,512]{2,1,0:T(8,128)(2,1)S(1)} %get-tuple-element.31.gl_ref, f32[2,2,2,4,1152,128]{5,4,3,2,1,0:T(8,128)} %bitcast.174), custom_call_target="tpu_custom_call" | custom-call | flops 3221225472 | bytes 10485760 | tf_op jit(solution)/shard_map/pallas_call | solution.py:65
  179.7 6.7 %shard_map.147 = f32[2,512,128]{2,1,0:T(8,128)S(1)} custom-call(s32[5]{0:T(128)S(1)} %pad_add_fusion.sc_ref, bf16[2,512,512]{2,1,0:T(8,128)(2,1)S(1)} %get-tuple-element.32.gh_ref, bf16[2,512,512]{2,1,0:T(8,128)(2,1)S(1)} %get-tuple-element.31.gl_ref, f32[2,2,2,4,1152,128]{5,4,3,2,1,0:T(8,128)} %bitcast.175, f32[2,2,2,4,1152,128]{5,4,3,2,1,0:T(8,128)} %bitcast.176, ...), custom_call_target="tpu_custom_call" | custom-call | flops 1207959552 | bytes 8388608 | tf_op jit(solution)/shard_map/pallas_call | solution.py:94
  187.8 1.9 collective-permute-start.15
  189.7 16.4 %shard_map.148 = f32[6,512,128]{2,1,0:T(8,128)S(1)} custom-call(s32[13]{0:T(128)S(1)} %pad_add_fusion.1.sc_ref, bf16[2,512,512]{2,1,0:T(8,128)(2,1)S(1)} %get-tuple-element.32.gh_ref, bf16[2,512,512]{2,1,0:T(8,128)(2,1)S(1)} %get-tuple-element.31.gl_ref, f32[2,2,2,4,1152,128]{5,4,3,2,1,0:T(8,128)} %bitcast.178, f32[2,2,2,4,1152,128]{5,4,3,2,1,0:T(8,128)} %bitcast.179, ...), custom_call_target="tpu_custom_call" | custom-call | flops 3623878656 | bytes 20971520 | tf_op jit(solution)/shard_map/pallas_call | solution.py:94
  206.3 14.9 %collective-permute-done.12 = f32[512,128]{1,0:T(8,128)S(1)} collective-permute-done((f32[512,128]{1,0:T(8,128)S(1)}, f32[512,128]{1,0:T(8,128)S(1)}, u32[]{:S(2)}, u32[]{:S(2)}) %collective-permute-start.12) | collective-permute-done | bytes 262176 | tf_op jit(solution)/shard_map/ppermute | solution.py:206
  221.4 2.7 collective-permute-start.16
  224.4 4.7 %collective-permute-done.13 = f32[512,128]{1,0:T(8,128)S(1)} collective-permute-done((f32[512,128]{1,0:T(8,128)S(1)}, f32[512,128]{1,0:T(8,128)S(1)}, u32[]{:S(2)}, u32[]{:S(2)}) %collective-permute-start.13) | collective-permute-done | bytes 262176 | tf_op jit(solution)/shard_map/ppermute | solution.py:206
  230.3 2.7 %collective-permute-start.17 = (f32[512,128]{1,0:T(8,128)S(1)}, f32[512,128]{1,0:T(8,128)S(1)}, u32[]{:S(2)}, u32[]{:S(2)}) collective-permute-start(f32[512,128]{1,0:T(8,128)S(1)} %get-tuple-element.33), channel_id=1, source_target_pairs={{0,7},{1,0},{2,1},{3,2},{4,3},{5,4},{6,5},{7,6},{8,15},{9,8},{10,9... | collective-permute-start | bytes 786440 | tf_op jit(solution)/shard_map/ppermute | solution.py:207
  234.6 2.5 collective-permute-done.14
  243.2 7.5 %all-to-all-start = ((f32[16,3,16,128]{3,2,1,0:T(8,128)}), f32[16,3,16,128]{3,2,1,0:T(8,128)S(1)}, u32[]{:S(2)}, u32[]{:S(2)}) async-start(f32[16,3,16,128]{3,2,1,0:T(8,128)} %copy.25), calls=%async_computation.1 | async-start | bytes 786432 | tf_op jit(solution)/shard_map/all_to_all | solution.py:226
  252.3 7.0 %all-to-all-done = f32[16,3,16,128]{3,2,1,0:T(8,128)S(1)} async-done(((f32[16,3,16,128]{3,2,1,0:T(8,128)}), f32[16,3,16,128]{3,2,1,0:T(8,128)S(1)}, u32[]{:S(2)}, u32[]{:S(2)}) %all-to-all-start) | async-done | bytes 393248 | tf_op jit(solution)/shard_map/all_to_all | solution.py:226
  (96 shorter events, 27.5 us)
Async XLA Ops:
  7.2 4.9 %copy-start = (f32[256,128]{1,0:T(8,128)S(1)}, f32[256,128]{1,0:T(8,128)}, u32[]{:S(2)}) copy-start(f32[256,128]{1,0:T(8,128)} %param.16) | copy-start | bytes 393220
  7.2 12.8 %copy-start.10 = (f32[16,128]{1,0:T(8,128)S(1)}, f32[16,128]{1,0:T(8,128)}, u32[]{:S(2)}) copy-start(f32[16,128]{1,0:T(8,128)} %param.14) | copy-start | bytes 24580
  7.2 163.5 %all-gather.3.cloned.1.call-start = ((), (), s32[]{:S(2)}) async-start(), calls=%async_computation.3 | async-start | bytes 19464192 | tf_op jit(solution)/shard_map/all_gather | solution.py:155
  15.1 81.6 %copy-start.13 = (s32[2]{0:T(128)S(1)}, s32[2]{0:T(128)}, u32[]{:S(2)}) copy-start(s32[2]{0:T(128)} %constant.279.clone) | copy-start | bytes 28
  15.1 13.9 %collective-permute-start = (f32[1152,128]{1,0:T(8,128)S(1)}, f32[1152,128]{1,0:T(8,128)S(1)}, u32[]{:S(2)}, u32[]{:S(2)}) collective-permute-start(f32[1152,128]{1,0:T(8,128)S(1)} %pad_maximum_fusion), channel_id=1, source_target_pairs={{0,0},{1,16},{2,32},{3,48},{4,64},{5,80},{6,96},{7,112},{8,8},{9,2... | collective-permute-start | bytes 1769480 | tf_op jit(solution)/shard_map/ppermute | solution.py:151
  29.8 210.9 %reduce-scatter.2.cloned.1.call-start = ((), (), s32[]{:S(2)}) async-start(), calls=%async_computation.2 | async-start | bytes 2359296 | tf_op jit(solution)/shard_map/reduce_scatter | solution.py:193
  29.9 6.9 %collective-permute-start.1 = (f32[528,128]{1,0:T(8,128)S(1)}, f32[528,128]{1,0:T(8,128)S(1)}, u32[]{:S(2)}, u32[]{:S(2)}) collective-permute-start(f32[528,128]{1,0:T(8,128)S(1)} %pad_maximum_fusion.3), channel_id=1, source_target_pairs={{0,8},{8,0},{1,9},{9,1},{2,10},{10,2},{3,11},{11,3},{4,12},{12,4},... | collective-permute-start | bytes 811016 | tf_op jit(solution)/shard_map/ppermute | solution.py:164
  36.9 39.6 %collective-permute-start.2 = (f32[2,528,128]{2,1,0:T(8,128)S(1)}, f32[2,528,128]{2,1,0:T(8,128)S(1)}, u32[]{:S(2)}, u32[]{:S(2)}) collective-permute-start(f32[2,528,128]{2,1,0:T(8,128)S(1)} %pad_maximum_fusion.1), channel_id=1, source_target_pairs={{0,1},{1,2},{2,3},{3,4},{4,5},{5,6},{6,7},{7,0},{8,9},{9,10},{10,1... | collective-permute-start | bytes 1622024 | tf_op jit(solution)/shard_map/ppermute | solution.py:169
  37.0 54.5 %collective-permute-start.6 = (f32[2,528,128]{2,1,0:T(8,128)S(1)}, f32[2,528,128]{2,1,0:T(8,128)S(1)}, u32[]{:S(2)}, u32[]{:S(2)}) collective-permute-start(f32[2,528,128]{2,1,0:T(8,128)S(1)} %pad_maximum_fusion.1), channel_id=1, source_target_pairs={{0,7},{1,0},{2,1},{3,2},{4,3},{5,4},{6,5},{7,6},{8,15},{9,8},{10,9... | collective-permute-start | bytes 1622024 | tf_op jit(solution)/shard_map/ppermute | solution.py:172
  76.5 15.5 %collective-permute-start.3 = (f32[2,528,128]{2,1,0:T(8,128)S(1)}, f32[2,528,128]{2,1,0:T(8,128)}, u32[]{:S(2)}, u32[]{:S(2)}) collective-permute-start(f32[2,528,128]{2,1,0:T(8,128)S(1)} %collective-permute-done.2), channel_id=1, source_target_pairs={{0,1},{1,2},{2,3},{3,4},{4,5},{5,6},{6,7},{7,0},{8,9},{9,10},{10,1... | collective-permute-start | bytes 1622024 | tf_op jit(solution)/shard_map/ppermute | solution.py:169
  83.9 30.8 %collective-permute-start.10 = (f32[2,256,2,256]{3,2,1,0:T(2,128)}, f32[2,256,2,256]{3,2,1,0:T(2,128)}, u32[]{:S(2)}, u32[]{:S(2)}) collective-permute-start(f32[2,256,2,256]{3,2,1,0:T(2,128)} %param.11), channel_id=1, source_target_pairs={{0,8},{8,0},{1,9},{9,1},{2,10},{10,2},{3,11},{11,3},{4,12},{12,4},... | collective-permute-start | bytes 3145736 | tf_op jit(solution)/shard_map/ppermute | solution.py:158
  89.0 10.8 %collective-permute-start.9 = (f32[512,128]{1,0:T(8,128)}, f32[512,128]{1,0:T(8,128)}, u32[]{:S(2)}, u32[]{:S(2)}) collective-permute-start(f32[512,128]{1,0:T(8,128)} %bitcast.5), channel_id=1, source_target_pairs={{0,1},{1,0},{2,3},{3,2},{4,5},{5,4},{6,7},{7,6},{8,9},{9,8},{10,11... | collective-permute-start | bytes 786440 | tf_op jit(solution)/shard_map/ppermute | solution.py:187
  91.4 10.4 %copy-start.4 = (f32[2,528,128]{2,1,0:T(8,128)}, f32[2,528,128]{2,1,0:T(8,128)S(1)}, u32[]{:S(2)}) copy-start(f32[2,528,128]{2,1,0:T(8,128)S(1)} %collective-permute-done.6) | copy-start | bytes 1622020
  91.4 14.5 %collective-permute-start.7 = (f32[2,528,128]{2,1,0:T(8,128)S(1)}, f32[2,528,128]{2,1,0:T(8,128)}, u32[]{:S(2)}, u32[]{:S(2)}) collective-permute-start(f32[2,528,128]{2,1,0:T(8,128)S(1)} %collective-permute-done.6), channel_id=1, source_target_pairs={{0,7},{1,0},{2,1},{3,2},{4,3},{5,4},{6,5},{7,6},{8,15},{9,8},{10,9... | collective-permute-start | bytes 1622024 | tf_op jit(solution)/shard_map/ppermute | solution.py:172
  92.0 17.5 %collective-permute-start.4 = (f32[2,528,128]{2,1,0:T(8,128)}, f32[2,528,128]{2,1,0:T(8,128)}, u32[]{:S(2)}, u32[]{:S(2)}) collective-permute-start(f32[2,528,128]{2,1,0:T(8,128)} %collective-permute-done.3), channel_id=1, source_target_pairs={{0,1},{1,2},{2,3},{3,4},{4,5},{5,6},{6,7},{7,0},{8,9},{9,10},{10,1... | collective-permute-start | bytes 1622024 | tf_op jit(solution)/shard_map/ppermute | solution.py:169
  106.0 13.8 %collective-permute-start.8 = (f32[2,528,128]{2,1,0:T(8,128)}, f32[2,528,128]{2,1,0:T(8,128)}, u32[]{:S(2)}, u32[]{:S(2)}) collective-permute-start(f32[2,528,128]{2,1,0:T(8,128)} %collective-permute-done.7), channel_id=1, source_target_pairs={{0,7},{1,0},{2,1},{3,2},{4,3},{5,4},{6,5},{7,6},{8,15},{9,8},{10,9... | collective-permute-start | bytes 1622024 | tf_op jit(solution)/shard_map/ppermute | solution.py:172
  109.5 10.7 %collective-permute-start.5 = (f32[2,528,128]{2,1,0:T(8,128)}, f32[2,528,128]{2,1,0:T(8,128)}, u32[]{:S(2)}, u32[]{:S(2)}) collective-permute-start(f32[2,528,128]{2,1,0:T(8,128)} %collective-permute-done.4), channel_id=1, source_target_pairs={{0,1},{1,2},{2,3},{3,4},{4,5},{5,6},{6,7},{7,0},{8,9},{9,10},{10,1... | collective-permute-start | bytes 1622024 | tf_op jit(solution)/shard_map/ppermute | solution.py:169
  117.8 2.5 copy-start.5
  176.3 1.3 copy-start.1
  186.5 19.7 %collective-permute-start.11 = (f32[512,128]{1,0:T(8,128)S(1)}, f32[512,128]{1,0:T(8,128)S(1)}, u32[]{:S(2)}, u32[]{:S(2)}) collective-permute-start(f32[512,128]{1,0:T(8,128)S(1)} %get-tuple-element.40), channel_id=1, source_target_pairs={{0,1},{1,2},{2,3},{3,4},{4,5},{5,6},{6,7},{7,0},{8,9},{9,10},{10,1... | collective-permute-start | bytes 786440 | tf_op jit(solution)/shard_map/ppermute | solution.py:206
  187.8 18.5 %collective-permute-start.15 = (f32[512,128]{1,0:T(8,128)S(1)}, f32[512,128]{1,0:T(8,128)S(1)}, u32[]{:S(2)}, u32[]{:S(2)}) collective-permute-start(f32[512,128]{1,0:T(8,128)S(1)} %get-tuple-element.39), channel_id=1, source_target_pairs={{0,7},{1,0},{2,1},{3,2},{4,3},{5,4},{6,5},{7,6},{8,15},{9,8},{10,9... | collective-permute-start | bytes 786440 | tf_op jit(solution)/shard_map/ppermute | solution.py:207
  206.2 15.1 %copy-start.2 = (f32[6,512,128]{2,1,0:T(8,128)}, f32[6,512,128]{2,1,0:T(8,128)S(1)}, u32[]{:S(2)}) copy-start(f32[6,512,128]{2,1,0:T(8,128)S(1)} %shard_map.148) | copy-start | bytes 4718596
  206.2 17.9 %copy-start.7 = (f32[512,256]{1,0:T(8,128)S(1)}, f32[512,256]{1,0:T(8,128)}, u32[]{:S(2)}) copy-start(f32[512,256]{1,0:T(8,128)} %maximum_select_fusion) | copy-start | bytes 1572868
  206.2 15.0 %collective-permute-start.12 = (f32[512,128]{1,0:T(8,128)S(1)}, f32[512,128]{1,0:T(8,128)S(1)}, u32[]{:S(2)}, u32[]{:S(2)}) collective-permute-start(f32[512,128]{1,0:T(8,128)S(1)} %fusion.8), channel_id=1, source_target_pairs={{0,1},{1,2},{2,3},{3,4},{4,5},{5,6},{6,7},{7,0},{8,9},{9,10},{10,1... | collective-permute-start | bytes 786440 | tf_op jit(solution)/shard_map/ppermute | solution.py:206
  221.3 7.8 %collective-permute-start.13 = (f32[512,128]{1,0:T(8,128)S(1)}, f32[512,128]{1,0:T(8,128)S(1)}, u32[]{:S(2)}, u32[]{:S(2)}) collective-permute-start(f32[512,128]{1,0:T(8,128)S(1)} %get-tuple-element.36), channel_id=1, source_target_pairs={{0,1},{1,2},{2,3},{3,4},{4,5},{5,6},{6,7},{7,0},{8,9},{9,10},{10,1... | collective-permute-start | bytes 786440 | tf_op jit(solution)/shard_map/ppermute | solution.py:206
  221.4 7.7 %collective-permute-start.16 = (f32[512,128]{1,0:T(8,128)S(1)}, f32[512,128]{1,0:T(8,128)S(1)}, u32[]{:S(2)}, u32[]{:S(2)}) collective-permute-start(f32[512,128]{1,0:T(8,128)S(1)} %get-tuple-element.35), channel_id=1, source_target_pairs={{0,7},{1,0},{2,1},{3,2},{4,3},{5,4},{6,5},{7,6},{8,15},{9,8},{10,9... | collective-permute-start | bytes 786440 | tf_op jit(solution)/shard_map/ppermute | solution.py:207
  230.2 8.9 %copy-start.6 = (f32[512,256]{1,0:T(8,128)S(1)}, f32[512,256]{1,0:T(8,128)}, u32[]{:S(2)}) copy-start(f32[512,256]{1,0:T(8,128)} %maximum_select_fusion.1) | copy-start | bytes 1572868
  230.2 6.9 %collective-permute-start.14 = (f32[512,128]{1,0:T(8,128)S(1)}, f32[512,128]{1,0:T(8,128)S(1)}, u32[]{:S(2)}, u32[]{:S(2)}) collective-permute-start(f32[512,128]{1,0:T(8,128)S(1)} %get-tuple-element.34), channel_id=1, source_target_pairs={{0,1},{1,2},{2,3},{3,4},{4,5},{5,6},{6,7},{7,0},{8,9},{9,10},{10,1... | collective-permute-start | bytes 786440 | tf_op jit(solution)/shard_map/ppermute | solution.py:210
  230.3 6.8 %collective-permute-start.17 = (f32[512,128]{1,0:T(8,128)S(1)}, f32[512,128]{1,0:T(8,128)S(1)}, u32[]{:S(2)}, u32[]{:S(2)}) collective-permute-start(f32[512,128]{1,0:T(8,128)S(1)} %get-tuple-element.33), channel_id=1, source_target_pairs={{0,7},{1,0},{2,1},{3,2},{4,3},{5,4},{6,5},{7,6},{8,15},{9,8},{10,9... | collective-permute-start | bytes 786440 | tf_op jit(solution)/shard_map/ppermute | solution.py:207
  240.8 10.8 %copy-start.8 = (f32[1,512,128]{2,1,0:T(8,128)S(1)}, f32[1,512,128]{2,1,0:T(8,128)}, u32[]{:S(2)}) copy-start(f32[1,512,128]{2,1,0:T(8,128)} %reduce-scatter.2.cloned.1.call-done) | copy-start | bytes 786436
  242.4 17.0 %copy-start.11 = (f32[16,128]{1,0:T(8,128)S(1)}, f32[16,128]{1,0:T(8,128)}, u32[]{:S(2)}) copy-start(f32[16,128]{1,0:T(8,128)} %param.19) | copy-start | bytes 24580
  243.2 16.1 %all-to-all-start = ((f32[16,3,16,128]{3,2,1,0:T(8,128)}), f32[16,3,16,128]{3,2,1,0:T(8,128)S(1)}, u32[]{:S(2)}, u32[]{:S(2)}) async-start(f32[16,3,16,128]{3,2,1,0:T(8,128)} %copy.25), calls=%async_computation.1 | async-start | bytes 786432 | tf_op jit(solution)/shard_map/all_to_all | solution.py:226
  (3 other events, 2.2 us)
Sparse Core Ops, SparseCore 0:
  30.0 140.7 all-gather.2
  177.8 46.0 reduce-scatter.1

commit v3 on v1

--- a/solution.py
+++ b/solution.py
@@ -23,59 +23,90 @@
     return f(a[0], b[0]) + (f(a[0], b[1]) + f(a[1], b[0]))
 
 
-def product_kernel(sc_ref, gh_ref, gl_ref, one_ref, two_ref, par_ref, lp_ref, out_ref):
-    h = sc_ref[8]
+def one_kernel(sc_ref, gh_ref, gl_ref, a_ref, b_ref, out_ref):
+    h = sc_ref[0]
+    acc = None
+    for k in range(2):
+        half = h if k == 0 else 1 - h
+        one = jnp.concatenate([a_ref[half, 0, 0, 0], b_ref[half, 0, 0, 0]], axis=1)
+        term = dot3((gh_ref[k], gl_ref[k]), split(one))
+        acc = term if acc is None else acc + term
+    out_ref[0] = -acc[:, :128]
+    out_ref[1] = -acc[:, 128:]
+
+
+def two_kernel(sc_ref, gh_ref, gl_ref, a_ref, b_ref, pa_ref, pb_ref, la_ref, lb_ref, out_ref):
+    h = sc_ref[0]
     lp = jnp.concatenate(
-        [jnp.concatenate([lp_ref[0, t], lp_ref[1, t]], axis=0) for t in range(2)], axis=1
+        [jnp.concatenate([r[0, 0, 0, 0], r[1, 0, 0, 0]], axis=0) for r in (la_ref, lb_ref)], axis=1
     )
     lp = split(lp)
     acc = None
     for k in range(2):
         half = h if k == 0 else 1 - h
-        one = jnp.concatenate([one_ref[half, 0], one_ref[half, 1]], axis=1)
-        two = jnp.concatenate([two_ref[half, 0], two_ref[half, 1]], axis=1)
-        par = jnp.concatenate([par_ref[half, 0], par_ref[half, 1]], axis=1)
+        two = jnp.concatenate([a_ref[half, 0, 0, 0], b_ref[half, 0, 0, 0]], axis=1)
+        par = jnp.concatenate([pa_ref[half, 0, 0, 0], pb_ref[half, 0, 0, 0]], axis=1)
         folded = two - dot3(split(par), lp)
-        both = split(jnp.concatenate([one, folded], axis=1))
-        term = dot3((gh_ref[k], gl_ref[k]), both)
+        term = dot3((gh_ref[k], gl_ref[k]), split(folded))
         acc = term if acc is None else acc + term
-    for level in range(2):
-        for t in range(2):
-            col = level * 256 + t * 128
-            out_ref[t, level] = -acc[:, col : col + 128]
-
-
-def product(scalars, g_hi, g_lo, gathered):
-    rows = lambda n: (2, 2, n, 128)
-    whole = pl.BlockSpec((2, 512, 512), lambda j, sc: (0, 0, 0))
+    out_ref[0] = -acc[:, :128]
+    out_ref[1] = -acc[:, 128:]
+
+
+WHOLE_G = pl.BlockSpec((2, 512, 512), lambda i, sc: (0, 0, 0))
+PARAMS = pltpu.CompilerParams(vmem_limit_bytes=40 * 2**20)
+
+
+def piece(rows, block, first, stride):
+    def place(i, sc):
+        code = sc[first + stride * i]
+        return (0, code // 8, code // 4 % 2, code % 4, block, 0)
+
+    return pl.BlockSpec((2, 1, 1, 1, rows, 128), place)
+
+
+def product(kernel, pieces, flops, scalars, pairs, g_hi, g_lo, gathered):
     return pl.pallas_call(
-        product_kernel,
+        kernel,
         grid_spec=pltpu.PrefetchScalarGridSpec(
             num_scalar_prefetch=1,
-            grid=(4,),
-            in_specs=[
-                whole,
-                whole,
-                pl.BlockSpec(rows(512), lambda j, sc: (0, j, 0, 0)),
-                pl.BlockSpec(rows(512), lambda j, sc: (0, j, 1, 0)),
-                pl.BlockSpec(rows(512), lambda j, sc: (0, sc[j], sc[4 + j], 0)),
-                pl.BlockSpec(rows(128), lambda j, sc: (0, j, 12, 0)),
-            ],
-            out_specs=pl.BlockSpec((2, 2, 512, 128), lambda j, sc: (j, 0, 0, 0)),
+            grid=(pairs,),
+            in_specs=[WHOLE_G, WHOLE_G, *pieces],
+            out_specs=pl.BlockSpec((2, 512, 128), lambda i, sc: (i, 0, 0)),
         ),
-        out_shape=jax.ShapeDtypeStruct((8, 2, 512, 128), jnp.float32),
-        compiler_params=pltpu.CompilerParams(vmem_limit_bytes=48 * 2**20),
+        out_shape=jax.ShapeDtypeStruct((2 * pairs, 512, 128), jnp.float32),
+        compiler_params=PARAMS,
         cost_estimate=pl.CostEstimate(
-            flops=8_000_000_000, bytes_accessed=24_000_000, transcendentals=0
+            flops=pairs * flops, bytes_accessed=pairs * 4_000_000, transcendentals=0
         ),
-    )(scalars, g_hi, g_lo, gathered, gathered, gathered, gathered)
-
-
-def swap_pairs(flip):
+    )(scalars, g_hi, g_lo, *[gathered] * len(pieces))
+
+
+product_one = functools.partial(
+    product, one_kernel, [piece(512, 0, 1 + t, 2) for t in range(2)], 800_000_000
+)
+product_two = functools.partial(
+    product,
+    two_kernel,
+    [piece(512, 1, 1 + t, 4) for t in range(2)]
+    + [piece(512, 0, 3 + t, 4) for t in range(2)]
+    + [piece(128, 8, 1 + t, 4) for t in range(2)],
+    1_600_000_000,
+)
+
+
+def chip_and_core(shift):
+    up = (shift >= 1) & (shift <= 4)
+    return (up * (4 - shift) + (1 - up) * (8 - shift)) % 4, 1 - up
+
+
+def spread_pairs(sign):
     pairs = []
     for i in range(256):
         row, col = divmod(i, 16)
-        pairs.append((i, (row // 8 * 8 + col % 8) * 16 + (col // 8 ^ flip) * 8 + row % 8))
+        half, z, h, s = row // 8, row % 8, col // 8, col % 8
+        chip, core = chip_and_core(sign * (z - s) % 8)
+        pairs.append((i, (half * 8 + chip * 2 + int(core)) * 16 + h * 8 + z))
     return pairs
 
 
@@ -102,20 +133,27 @@
     two = jnp.where(keep_two, l_two, 0.0).reshape(512, 128)
 
     lp_piece = lax.dynamic_slice_in_dim(lp_two, row // 8 * 128, 128, 0)
-    near = lax.ppermute(jnp.concatenate([one, two, lp_piece]), ALL_AXES, swap_pairs(0))
-    far = lax.ppermute(one, ALL_AXES, swap_pairs(1))
-    payload = jnp.concatenate([near[:1024], far, near[1024:]])
-    gathered = lax.all_gather(payload, ROW_AXES, axis=0, tiled=False)
-    gathered = gathered.reshape(2, 8, 1664, 128)
-
+    near_one = lax.ppermute(one, ALL_AXES, spread_pairs(1))
+    near_two = lax.ppermute(jnp.concatenate([two, lp_piece]), ALL_AXES, spread_pairs(-1))
+    packed = jnp.concatenate([one, dinv_one])
+    packed_far = lax.ppermute(packed, "y_hi", ring(2, 1))
     g_other = lax.ppermute(g_top, "y_hi", ring(2, 1))
+    near_one, near_two, packed, packed_far, two_sent, g_other = lax.optimization_barrier(
+        (near_one, near_two, packed, packed_far, two, g_other)
+    )
+    near = jnp.concatenate([near_one, near_two])
+    gathered = lax.all_gather(near, ("x", "y_hi", "y_lo", "core"), axis=0, tiled=False)
+    gathered = gathered.reshape(2, 2, 2, 4, 1152, 128)
+
+    def place(slot, sign):
+        chip, core = chip_and_core(sign * (z - slot) % 8)
+        return chip // 2 * 8 + slot // 8 * 4 + chip % 2 * 2 + core
+
     g = jnp.stack([g_top, g_other]).reshape(2, 512, 512)
     g_hi32 = lax.reduce_precision(g, 8, 7)
     g_hi = g_hi32.astype(jnp.bfloat16)
     g_lo = (g - g_hi32).astype(jnp.bfloat16)
 
-    packed = jnp.concatenate([one, dinv_one])
-    packed_far = lax.ppermute(packed, "y_hi", ring(2, 1))
     pair = jnp.stack([jnp.where(h == 0, packed, packed_far), jnp.where(h == 0, packed_far, packed)])
     pieces = {0: pair}
     right = left = pair
@@ -138,22 +176,53 @@
     par = jnp.concatenate([fetch(parent, 0), fetch(parent, 1)], axis=1)
     sibling = z ^ 1
     one_next = jnp.where(sibling > z, pieces[1][h], pieces[-1][h])[:512]
-    two_next = lax.ppermute(two, "z", [(i, i ^ 1) for i in range(8)])
+    two_next = lax.ppermute(two_sent, "z", [(i, i ^ 1) for i in range(8)])
     own_two = jnp.where(z % 2 == 0, jnp.concatenate([two, two_next], 1), jnp.concatenate([two_next, two], 1))
     own_one = jnp.where(z % 2 == 0, jnp.concatenate([one, one_next], 1), jnp.concatenate([one_next, one], 1))
 
-    parents = lax.dynamic_slice_in_dim(parent_two, h * 4, 4, 0)
-    place = jnp.where(parents // 4 == h, 0, 2)
-    scalars = jnp.concatenate([parents % 4, place, h[None]]).astype(jnp.int32)
-    partial = product(scalars, g_hi, g_lo, gathered)
-    inverse = lax.psum_scatter(partial, "z", scatter_dimension=0, tiled=False)
-    inv_one, inv_two = inverse[0], inverse[1]
+    slots = h * 8 + jnp.arange(8, dtype=jnp.int32)
+    h_now, par, own_one, own_two = lax.optimization_barrier((h, par, own_one, own_two))
+    scalars = jnp.concatenate([h_now[None], place(slots, 1)]).astype(jnp.int32)
+    part_one = product_one(scalars, 4, g_hi, g_lo, gathered)
+    inv_one = lax.psum_scatter(part_one, "z", scatter_dimension=0, tiled=False)
+
+    def level_two(first_pair, h_in):
+        supers = h * 4 + (first_pair + jnp.arange(2, dtype=jnp.int32)) % 4
+        parents = parent_two.at[supers].get(mode="promise_in_bounds")
+        two_slots = supers[:, None] * 2 + jnp.arange(2, dtype=jnp.int32)[None, :]
+        par_slots = parents[:, None] * 2 + jnp.arange(2, dtype=jnp.int32)[None, :]
+        codes = jnp.concatenate([place(two_slots, -1), place(par_slots, 1)], axis=1)
+        scalars = jnp.concatenate([h_in[None], codes.reshape(8)]).astype(jnp.int32)
+        return product_two(scalars, 2, g_hi, g_lo, gathered)
+
+    pair_now = (z + 4) // 2
+    h_next, part_one = lax.optimization_barrier((h_now, part_one[0, :8]))
+    early = level_two(pair_now, h_next)
+    h_last, early = lax.optimization_barrier((h_next, early))
+    late = level_two(pair_now + 2, h_last)
+    even = z % 2 == 0
+
+    def term(d):
+        take = lambda i: early[i] if i < 4 else late[i - 4]
+        return jnp.where(even, take((d - 4) % 8), take((d - 3) % 8))
+
+    up, down = term(4), term(-3)
+    for d in range(3):
+        up = lax.ppermute(up, "z", ring(8, 1)) + term(3 - d)
+        down = lax.ppermute(down, "z", ring(8, -1))
+        if d < 2:
+            down = down + term(d - 2)
+    inv_two = lax.ppermute(up, "z", ring(8, 1)) + down + term(0)
     panel_one = jnp.where(keep_one, inv_one.reshape(2, 256, 128), 0.0)
     panel_two = jnp.where(keep_two, inv_two.reshape(2, 256, 128), 0.0)
 
     dot_t = lambda a, b: lax.dot_general(a, b, (((0,), (0,)), ((), ())), precision=exact)
-    lp_pair = lax.dynamic_slice(gathered, (0, z // 2 * 2, 1536, 0), (2, 2, 128, 128))
-    lp_own = lp_pair.transpose(0, 2, 1, 3).reshape(256, 256)
+    lp_halves = []
+    for t in range(2):
+        code = place(mine * 2 + t, -1)
+        at = (0, code // 8, h, code % 4, 1024, 0)
+        lp_halves.append(lax.dynamic_slice(gathered, at, (2, 1, 1, 1, 128, 128)).reshape(256, 128))
+    lp_own = jnp.concatenate(lp_halves, axis=1)
     scaled = jnp.dot(par[512:], lp_two, precision=exact)
     lp_slab = lax.dynamic_slice_in_dim(lp_own, row * 16, 16, 0)
     quad = dot_t(lp_slab, scaled)

time: 324 us -> 251 us (0.77)
  waiting for transfers between devices: 217 us -> 116 us
  starting transfers between devices: 41.7 us -> 57.3 us
  other arithmetic: 10.8 us -> 19.6 us
    all_gather x1, waiting for transfers between devices: 95.2 us -> 25.5 us  [local(): lax.all_gather(near, ('x', 'y_hi', 'y_lo', 'core'), axis=0, tiled=False)]
    ppermute x4, waiting for transfers between devices: 70.8 us -> 25.5 us  [local(): right = lax.ppermute(right, 'z', ring(8, 1))]
    ppermute x3 -> x10, waiting for transfers between devices: 12 us -> 37.6 us  [the longest x3 17.9 us: local(): up = lax.ppermute(up, 'z', ring(8, 1)) + term(3 - d)]
    ppermute x1, waiting for transfers between devices: 24.1 us -> 0.01 us  [local(): g_other = lax.ppermute(g_top, 'y_hi', ring(2, 1))]
    ppermute x3 -> x10, starting transfers between devices: 9.4 us -> 24.5 us  [the longest x1 9.16 us: local(): near_one = lax.ppermute(one, ALL_AXES, spread_pairs(1))]
    ppermute x4, starting transfers between devices: 15.3 us -> 1.96 us  [local(): right = lax.ppermute(right, 'z', ring(8, 1))]
    ppermute x3, starting transfers between devices: 3.53 us -> 15.1 us  [local(): left = lax.ppermute(left, 'z', ring(8, -1))]
    ppermute x3, waiting for transfers between devices: 0.11 us -> 8.68 us  [local(): left = lax.ppermute(left, 'z', ring(8, -1))]
  transfers between devices with their start and end apart: 15 -> 22, of which waited for: 11 -> 15; matrix products, arithmetic and copies ran while one was open for 5% -> 12% of each run, Pallas kernels for 0% -> 6%
where the time goes in v3:
time: 251 us; the launch traced here: 250 us
  waiting for transfers between devices  116 us (46%)
  starting transfers between devices  57.3 us (23%)
  Pallas kernels  20.9 us (8%)
  other arithmetic  19.6 us (8%)
  between operations  19.1 us (8%)
  local copies, waits for them, and re-layouts  12.7 us (5%)
  matrix products  4.76 us (2%)
    all_gather x1, waiting for transfers between devices, local(): lax.all_gather(near, ('x', 'y_hi', 'y_lo', 'core'), axis=0, tiled=False)  25.5 us
    ppermute x4, waiting for transfers between devices, local(): right = lax.ppermute(right, 'z', ring(8, 1))  25.5 us
    pallas_call x3, Pallas kernels, product(): pl.pallas_call(kernel, grid_spec=pltpu.PrefetchScalarGridSpec(num_scalar_...  20.9 us
    ppermute x3, waiting for transfers between devices, local(): up = lax.ppermute(up, 'z', ring(8, 1)) + term(3 - d)  17.9 us
    ppermute x3, starting transfers between devices, local(): left = lax.ppermute(left, 'z', ring(8, -1))  15.1 us
    ppermute x3, waiting for transfers between devices, local(): down = lax.ppermute(down, 'z', ring(8, -1))  11.5 us
    ppermute x1, waiting for transfers between devices, local(): packed_far = lax.ppermute(packed, 'y_hi', ring(2, 1))  11.3 us
    all_to_all x1, starting transfers between devices, local(): sums = jnp.sum(lax.all_to_all(terms, ROW_AXES, 0, 0), axis=0)  10.3 us
  transfers between devices with their start and end apart: 22, of which 15 were waited for; matrix products, arithmetic and copies ran while one was open for 12% of the time, Pallas kernels for 6%

profile of v3, /device:TPU:1, one launch (start us, length us, event | category | flops | bytes accessed | tf_op | source)
XLA Modules:
  0.0 249.9 jit_solution(10545206022504811473)
XLA Ops:
  7.2 3.8 %collective-permute-start.3 = (f32[2,256,2,256]{3,2,1,0:T(2,128)}, f32[2,256,2,256]{3,2,1,0:T(2,128)S(1)}, u32[]{:S(2)}, u32[]{:S(2)}) collective-permute-start(f32[2,256,2,256]{3,2,1,0:T(2,128)} %param.9), channel_id=1, source_target_pairs={{0,8},{8,0},{1,9},{9,1},{2,10},{10,2},{3,11},{11,3},{4,12},{12,4},... | collective-permute-start | bytes 3145736 | tf_op jit(solution)/shard_map/ppermute | solution.py:140
  17.1 3.7 %collective-permute-start.1 = (f32[640,128]{1,0:T(8,128)S(1)}, f32[640,128]{1,0:T(8,128)S(1)}, u32[]{:S(2)}, u32[]{:S(2)}) collective-permute-start(f32[640,128]{1,0:T(8,128)S(1)} %pad_maximum_fusion.3), channel_id=1, source_target_pairs={{0,16},{1,96},{2,64},{3,32},{4,0},{5,112},{6,80},{7,48},{8,24},{9,... | collective-permute-start | bytes 983048 | tf_op jit(solution)/shard_map/ppermute | solution.py:137
  22.7 1.6 collective-permute-start.2
  24.3 9.2 %collective-permute-start = (f32[512,128]{1,0:T(8,128)S(1)}, f32[512,128]{1,0:T(8,128)S(1)}, u32[]{:S(2)}, u32[]{:S(2)}) collective-permute-start(f32[512,128]{1,0:T(8,128)S(1)} %bitcast.180), channel_id=1, source_target_pairs={{0,16},{1,48},{2,80},{3,112},{4,0},{5,32},{6,64},{7,96},{8,24},{9,... | collective-permute-start | bytes 786440 | tf_op jit(solution)/shard_map/ppermute | solution.py:136
  33.5 3.3 %collective-permute-done = f32[512,128]{1,0:T(8,128)S(1)} collective-permute-done((f32[512,128]{1,0:T(8,128)S(1)}, f32[512,128]{1,0:T(8,128)S(1)}, u32[]{:S(2)}, u32[]{:S(2)}) %collective-permute-start) | collective-permute-done | bytes 262176 | tf_op jit(solution)/shard_map/ppermute | solution.py:136
  36.8 11.3 %collective-permute-done.2 = f32[528,128]{1,0:T(8,128)S(1)} collective-permute-done((f32[528,128]{1,0:T(8,128)S(1)}, f32[528,128]{1,0:T(8,128)S(1)}, u32[]{:S(2)}, u32[]{:S(2)}) %collective-permute-start.2) | collective-permute-done | bytes 270368 | tf_op jit(solution)/shard_map/ppermute | solution.py:139
  52.9 13.1 %collective-permute-start.8 = (f32[2,528,128]{2,1,0:T(8,128)S(1)}, f32[2,528,128]{2,1,0:T(8,128)}, u32[]{:S(2)}, u32[]{:S(2)}) collective-permute-start(f32[2,528,128]{2,1,0:T(8,128)S(1)} %pad_maximum_fusion.1), channel_id=1, source_target_pairs={{0,7},{1,0},{2,1},{3,2},{4,3},{5,4},{6,5},{7,6},{8,15},{9,8},{10,9... | collective-permute-start | bytes 1622024 | tf_op jit(solution)/shard_map/ppermute | solution.py:164
  66.0 10.3 %collective-permute-done.4 = f32[2,528,128]{2,1,0:T(8,128)S(1)} collective-permute-done((f32[2,528,128]{2,1,0:T(8,128)S(1)}, f32[2,528,128]{2,1,0:T(8,128)S(1)}, u32[]{:S(2)}, u32[]{:S(2)}) %collective-permute-start.4) | collective-permute-done | bytes 540704 | tf_op jit(solution)/shard_map/ppermute | solution.py:161
  77.0 2.0 collective-permute-done.8
  80.2 9.7 %collective-permute-done.5 = f32[2,528,128]{2,1,0:T(8,128)} collective-permute-done((f32[2,528,128]{2,1,0:T(8,128)S(1)}, f32[2,528,128]{2,1,0:T(8,128)}, u32[]{:S(2)}, u32[]{:S(2)}) %collective-permute-start.5) | collective-permute-done | bytes 540704 | tf_op jit(solution)/shard_map/ppermute | solution.py:161
  94.3 2.1 stack.32
  96.4 2.1 collective-permute-start.11
  99.4 3.3 %collective-permute-done.6 = f32[2,528,128]{2,1,0:T(8,128)} collective-permute-done((f32[2,528,128]{2,1,0:T(8,128)}, f32[2,528,128]{2,1,0:T(8,128)}, u32[]{:S(2)}, u32[]{:S(2)}) %collective-permute-start.6) | collective-permute-done | bytes 540704 | tf_op jit(solution)/shard_map/ppermute | solution.py:161
  102.7 2.5 %fusion = (bf16[2,512,512]{2,1,0:T(8,128)(2,1)S(1)}, bf16[2,512,512]{2,1,0:T(8,128)(2,1)S(1)}) fusion(f32[2,512,512]{2,1,0:T(8,128)} %copy-done.5), kind=kLoop, calls=%fused_computation.4 | loop fusion | flops 2097152 | bytes 4194304 | tf_op jit(solution)/shard_map/convert_element_type | solution.py:155
  108.0 6.6 %collective-permute-done.10 = f32[2,528,128]{2,1,0:T(8,128)S(1)} collective-permute-done((f32[2,528,128]{2,1,0:T(8,128)}, f32[2,528,128]{2,1,0:T(8,128)S(1)}, u32[]{:S(2)}, u32[]{:S(2)}) %collective-permute-start.10) | collective-permute-done | bytes 540704 | tf_op jit(solution)/shard_map/ppermute | solution.py:164
  114.7 2.1 collective-permute-done.7
  116.8 1.9 select_select_fusion.1
  118.7 1.8 select_select_fusion
  121.5 25.5 %all-gather.3.cloned.1.call-done = f32[36864,128]{1,0:T(8,128)} async-done(((f32[1152,128]{1,0:T(8,128)}), f32[36864,128]{1,0:T(8,128)}) %all-gather.3.cloned.1.call-update) | async-done | bytes 18874384 | tf_op jit(solution)/shard_map/all_gather | solution.py:145
  147.0 6.3 %shard_map.128 = f32[8,512,128]{2,1,0:T(8,128)S(1)} custom-call(s32[9]{0:T(128)S(1)} %pad_add_fusion.2.sc_ref, bf16[2,512,512]{2,1,0:T(8,128)(2,1)S(1)} %get-tuple-element.36.gh_ref, bf16[2,512,512]{2,1,0:T(8,128)(2,1)S(1)} %get-tuple-element.35.gl_ref, f32[2,2,2,4,1152,128]{5,4,3,2,1,0:T(8,128)} %bitcast.158, f32[2,2,2,4,1152,128]{5,4,3,2,1,0:T(8,128)} %bitcast.159), custom_call_target="tpu_custom_call" | custom-call | flops 3200000000 | bytes 16000000 | tf_op jit(solution)/shard_map/pallas_call | solution.py:69
  155.3 7.3 %shard_map.129 = f32[4,512,128]{2,1,0:T(8,128)S(1)} custom-call(s32[9]{0:T(128)S(1)} %pad_add_fusion.3.sc_ref, bf16[2,512,512]{2,1,0:T(8,128)(2,1)S(1)} %get-tuple-element.36.gh_ref, bf16[2,512,512]{2,1,0:T(8,128)(2,1)S(1)} %get-tuple-element.35.gl_ref, f32[2,2,2,4,1152,128]{5,4,3,2,1,0:T(8,128)} %bitcast.160, f32[2,2,2,4,1152,128]{5,4,3,2,1,0:T(8,128)} %bitcast.161, ...), custom_call_target="tpu_custom_call" | custom-call | flops 3200000000 | bytes 8000000 | tf_op jit(solution)/shard_map/pallas_call | solution.py:69
  163.4 3.0 %collective-permute-start.16 = (f32[512,128]{1,0:T(8,128)}, f32[512,128]{1,0:T(8,128)}, u32[]{:S(2)}, u32[]{:S(2)}) collective-permute-start(f32[512,128]{1,0:T(8,128)} %get-tuple-element.37), channel_id=1, source_target_pairs={{0,7},{1,0},{2,1},{3,2},{4,3},{5,4},{6,5},{7,6},{8,15},{9,8},{10,9... | collective-permute-start | bytes 786440 | tf_op jit(solution)/shard_map/ppermute | solution.py:212
  166.8 9.0 %collective-permute-done.16 = f32[512,128]{1,0:T(8,128)} collective-permute-done((f32[512,128]{1,0:T(8,128)}, f32[512,128]{1,0:T(8,128)}, u32[]{:S(2)}, u32[]{:S(2)}) %collective-permute-start.16) | collective-permute-done | bytes 262176 | tf_op jit(solution)/shard_map/ppermute | solution.py:212
  176.9 3.6 %collective-permute-start.17 = (f32[512,128]{1,0:T(8,128)S(1)}, f32[512,128]{1,0:T(8,128)S(1)}, u32[]{:S(2)}, u32[]{:S(2)}) collective-permute-start(f32[512,128]{1,0:T(8,128)S(1)} %bitcast_add_fusion.2), channel_id=1, source_target_pairs={{0,7},{1,0},{2,1},{3,2},{4,3},{5,4},{6,5},{7,6},{8,15},{9,8},{10,9... | collective-permute-start | bytes 786440 | tf_op jit(solution)/shard_map/ppermute | solution.py:212
  180.5 7.3 %shard_map.130 = f32[4,512,128]{2,1,0:T(8,128)S(1)} custom-call(s32[9]{0:T(128)S(1)} %pad_add_fusion.4.sc_ref, bf16[2,512,512]{2,1,0:T(8,128)(2,1)S(1)} %get-tuple-element.36.gh_ref, bf16[2,512,512]{2,1,0:T(8,128)(2,1)S(1)} %get-tuple-element.35.gl_ref, f32[2,2,2,4,1152,128]{5,4,3,2,1,0:T(8,128)} %bitcast.166, f32[2,2,2,4,1152,128]{5,4,3,2,1,0:T(8,128)} %bitcast.167, ...), custom_call_target="tpu_custom_call" | custom-call | flops 3200000000 | bytes 8000000 | tf_op jit(solution)/shard_map/pallas_call | solution.py:69
  187.8 2.4 collective-permute-done.17
  190.5 13.5 %collective-permute-done.13 = f32[512,128]{1,0:T(8,128)S(1)} collective-permute-done((f32[512,128]{1,0:T(8,128)S(1)}, f32[512,128]{1,0:T(8,128)S(1)}, u32[]{:S(2)}, u32[]{:S(2)}) %collective-permute-start.13) | collective-permute-done | bytes 262176 | tf_op jit(solution)/shard_map/ppermute | solution.py:211
  204.8 2.5 collective-permute-start.18
  207.2 4.4 %collective-permute-done.14 = f32[512,128]{1,0:T(8,128)S(1)} collective-permute-done((f32[512,128]{1,0:T(8,128)S(1)}, f32[512,128]{1,0:T(8,128)S(1)}, u32[]{:S(2)}, u32[]{:S(2)}) %collective-permute-start.14) | collective-permute-done | bytes 262176 | tf_op jit(solution)/shard_map/ppermute | solution.py:211
  213.4 5.0 %collective-permute-done.15 = f32[512,128]{1,0:T(8,128)S(1)} collective-permute-done((f32[512,128]{1,0:T(8,128)S(1)}, f32[512,128]{1,0:T(8,128)S(1)}, u32[]{:S(2)}, u32[]{:S(2)}) %collective-permute-start.15) | collective-permute-done | bytes 262176 | tf_op jit(solution)/shard_map/ppermute | solution.py:215
  223.5 10.3 %all-to-all-start = ((f32[16,3,16,128]{3,2,1,0:T(8,128)}), f32[16,3,16,128]{3,2,1,0:T(8,128)S(1)}, u32[]{:S(2)}, u32[]{:S(2)}) async-start(f32[16,3,16,128]{3,2,1,0:T(8,128)} %copy.19), calls=%async_computation.1 | async-start | bytes 786432 | tf_op jit(solution)/shard_map/all_to_all | solution.py:233
  235.4 7.0 %all-to-all-done = f32[16,3,16,128]{3,2,1,0:T(8,128)S(1)} async-done(((f32[16,3,16,128]{3,2,1,0:T(8,128)}), f32[16,3,16,128]{3,2,1,0:T(8,128)S(1)}, u32[]{:S(2)}, u32[]{:S(2)}) %all-to-all-start) | async-done | bytes 393248 | tf_op jit(solution)/shard_map/all_to_all | solution.py:233
  (138 shorter events, 33.2 us)
Async XLA Ops:
  7.2 139.8 %all-gather.3.cloned.1.call-start = ((), (), s32[]{:S(2)}) async-start(), calls=%async_computation.3 | async-start | bytes 19464192 | tf_op jit(solution)/shard_map/all_gather | solution.py:145
  7.2 40.8 %collective-permute-start.3 = (f32[2,256,2,256]{3,2,1,0:T(2,128)}, f32[2,256,2,256]{3,2,1,0:T(2,128)S(1)}, u32[]{:S(2)}, u32[]{:S(2)}) collective-permute-start(f32[2,256,2,256]{3,2,1,0:T(2,128)} %param.9), channel_id=1, source_target_pairs={{0,8},{8,0},{1,9},{9,1},{2,10},{10,2},{3,11},{11,3},{4,12},{12,4},... | collective-permute-start | bytes 3145736 | tf_op jit(solution)/shard_map/ppermute | solution.py:140
  16.0 33.9 %copy-start.22 = (pred[2]{0:T(512)(128)(4,1)}, pred[2]{0:T(512)(128)(4,1)S(1)}, u32[]{:S(2)}) copy-start(pred[2]{0:T(512)(128)(4,1)S(1)} %get-tuple-element.30) | copy-start | bytes 10
  16.0 33.9 %copy-start.24 = (pred[2]{0:T(512)(128)(4,1)}, pred[2]{0:T(512)(128)(4,1)S(1)}, u32[]{:S(2)}) copy-start(pred[2]{0:T(512)(128)(4,1)S(1)} %get-tuple-element.29) | copy-start | bytes 10
  17.1 30.9 %collective-permute-start.1 = (f32[640,128]{1,0:T(8,128)S(1)}, f32[640,128]{1,0:T(8,128)S(1)}, u32[]{:S(2)}, u32[]{:S(2)}) collective-permute-start(f32[640,128]{1,0:T(8,128)S(1)} %pad_maximum_fusion.3), channel_id=1, source_target_pairs={{0,16},{1,96},{2,64},{3,32},{4,0},{5,112},{6,80},{7,48},{8,24},{9,... | collective-permute-start | bytes 983048 | tf_op jit(solution)/shard_map/ppermute | solution.py:137
  22.6 28.9 %copy-start.4 = (s32[8]{0:T(128)S(1)}, s32[8]{0:T(128)}, u32[]{:S(2)}) copy-start(s32[8]{0:T(128)} %param.15) | copy-start | bytes 100
  22.7 25.4 %collective-permute-start.2 = (f32[528,128]{1,0:T(8,128)S(1)}, f32[528,128]{1,0:T(8,128)S(1)}, u32[]{:S(2)}, u32[]{:S(2)}) collective-permute-start(f32[528,128]{1,0:T(8,128)S(1)} %pad_maximum_fusion.5), channel_id=1, source_target_pairs={{0,8},{8,0},{1,9},{9,1},{2,10},{10,2},{3,11},{11,3},{4,12},{12,4},... | collective-permute-start | bytes 811016 | tf_op jit(solution)/shard_map/ppermute | solution.py:139
  24.3 12.5 %collective-permute-start = (f32[512,128]{1,0:T(8,128)S(1)}, f32[512,128]{1,0:T(8,128)S(1)}, u32[]{:S(2)}, u32[]{:S(2)}) collective-permute-start(f32[512,128]{1,0:T(8,128)S(1)} %bitcast.180), channel_id=1, source_target_pairs={{0,16},{1,48},{2,80},{3,112},{4,0},{5,32},{6,64},{7,96},{8,24},{9,... | collective-permute-start | bytes 786440 | tf_op jit(solution)/shard_map/ppermute | solution.py:136
  49.8 40.1 %copy-start.18 = (f32[2,256,2,256]{3,2,1,0:T(2,128)S(1)}, f32[2,256,2,256]{3,2,1,0:T(2,128)}, u32[]{:S(2)}) copy-start(f32[2,256,2,256]{3,2,1,0:T(2,128)} %param.9) | copy-start | bytes 3145732
  49.9 171.2 %reduce-scatter.2.cloned.1.call-start = ((), (), s32[]{:S(2)}) async-start(), calls=%async_computation.2 | async-start | bytes 2359296 | tf_op jit(solution)/shard_map/reduce_scatter | solution.py:187
  50.0 40.8 %copy-start.6 = (f32[528,128]{1,0:T(8,128)}, f32[528,128]{1,0:T(8,128)S(1)}, u32[]{:S(2)}) copy-start(f32[528,128]{1,0:T(8,128)S(1)} %get-tuple-element.40) | copy-start | bytes 811012
  50.1 26.2 %collective-permute-start.4 = (f32[2,528,128]{2,1,0:T(8,128)S(1)}, f32[2,528,128]{2,1,0:T(8,128)S(1)}, u32[]{:S(2)}, u32[]{:S(2)}) collective-permute-start(f32[2,528,128]{2,1,0:T(8,128)S(1)} %pad_maximum_fusion.1), channel_id=1, source_target_pairs={{0,1},{1,2},{2,3},{3,4},{4,5},{5,6},{6,7},{7,0},{8,9},{9,10},{10,1... | collective-permute-start | bytes 1622024 | tf_op jit(solution)/shard_map/ppermute | solution.py:161
  52.9 26.1 %collective-permute-start.8 = (f32[2,528,128]{2,1,0:T(8,128)S(1)}, f32[2,528,128]{2,1,0:T(8,128)}, u32[]{:S(2)}, u32[]{:S(2)}) collective-permute-start(f32[2,528,128]{2,1,0:T(8,128)S(1)} %pad_maximum_fusion.1), channel_id=1, source_target_pairs={{0,7},{1,0},{2,1},{3,2},{4,3},{5,4},{6,5},{7,6},{8,15},{9,8},{10,9... | collective-permute-start | bytes 1622024 | tf_op jit(solution)/shard_map/ppermute | solution.py:164
  76.3 17.4 %copy-start.8 = (f32[2,528,128]{2,1,0:T(8,128)}, f32[2,528,128]{2,1,0:T(8,128)S(1)}, u32[]{:S(2)}) copy-start(f32[2,528,128]{2,1,0:T(8,128)S(1)} %collective-permute-done.4) | copy-start | bytes 1622020
  76.3 13.5 %collective-permute-start.5 = (f32[2,528,128]{2,1,0:T(8,128)S(1)}, f32[2,528,128]{2,1,0:T(8,128)}, u32[]{:S(2)}, u32[]{:S(2)}) collective-permute-start(f32[2,528,128]{2,1,0:T(8,128)S(1)} %collective-permute-done.4), channel_id=1, source_target_pairs={{0,1},{1,2},{2,3},{3,4},{4,5},{5,6},{6,7},{7,0},{8,9},{9,10},{10,1... | collective-permute-start | bytes 1622024 | tf_op jit(solution)/shard_map/ppermute | solution.py:161
  79.0 19.6 %collective-permute-start.9 = (f32[2,528,128]{2,1,0:T(8,128)}, f32[2,528,128]{2,1,0:T(8,128)}, u32[]{:S(2)}, u32[]{:S(2)}) collective-permute-start(f32[2,528,128]{2,1,0:T(8,128)} %collective-permute-done.8), channel_id=1, source_target_pairs={{0,7},{1,0},{2,1},{3,2},{4,3},{5,4},{6,5},{7,6},{8,15},{9,8},{10,9... | collective-permute-start | bytes 1622024 | tf_op jit(solution)/shard_map/ppermute | solution.py:164
  89.9 12.8 %collective-permute-start.6 = (f32[2,528,128]{2,1,0:T(8,128)}, f32[2,528,128]{2,1,0:T(8,128)}, u32[]{:S(2)}, u32[]{:S(2)}) collective-permute-start(f32[2,528,128]{2,1,0:T(8,128)} %collective-permute-done.5), channel_id=1, source_target_pairs={{0,1},{1,2},{2,3},{3,4},{4,5},{5,6},{6,7},{7,0},{8,9},{9,10},{10,1... | collective-permute-start | bytes 1622024 | tf_op jit(solution)/shard_map/ppermute | solution.py:161
  96.4 8.9 %collective-permute-start.11 = (f32[512,128]{1,0:T(8,128)}, f32[512,128]{1,0:T(8,128)S(1)}, u32[]{:S(2)}, u32[]{:S(2)}) collective-permute-start(f32[512,128]{1,0:T(8,128)} %bitcast.177), channel_id=1, source_target_pairs={{0,1},{1,0},{2,3},{3,2},{4,5},{5,4},{6,7},{7,6},{8,9},{9,8},{10,11... | collective-permute-start | bytes 786440 | tf_op jit(solution)/shard_map/ppermute | solution.py:179
  98.6 16.1 %collective-permute-start.10 = (f32[2,528,128]{2,1,0:T(8,128)}, f32[2,528,128]{2,1,0:T(8,128)S(1)}, u32[]{:S(2)}, u32[]{:S(2)}) collective-permute-start(f32[2,528,128]{2,1,0:T(8,128)} %collective-permute-done.9), channel_id=1, source_target_pairs={{0,7},{1,0},{2,1},{3,2},{4,3},{5,4},{6,5},{7,6},{8,15},{9,8},{10,9... | collective-permute-start | bytes 1622024 | tf_op jit(solution)/shard_map/ppermute | solution.py:164
  102.7 14.1 %collective-permute-start.7 = (f32[2,528,128]{2,1,0:T(8,128)}, f32[2,528,128]{2,1,0:T(8,128)S(1)}, u32[]{:S(2)}, u32[]{:S(2)}) collective-permute-start(f32[2,528,128]{2,1,0:T(8,128)} %collective-permute-done.6), channel_id=1, source_target_pairs={{0,1},{1,2},{2,3},{3,4},{4,5},{5,6},{6,7},{7,0},{8,9},{9,10},{10,1... | collective-permute-start | bytes 1622024 | tf_op jit(solution)/shard_map/ppermute | solution.py:161
  163.4 12.4 %collective-permute-start.16 = (f32[512,128]{1,0:T(8,128)}, f32[512,128]{1,0:T(8,128)}, u32[]{:S(2)}, u32[]{:S(2)}) collective-permute-start(f32[512,128]{1,0:T(8,128)} %get-tuple-element.37), channel_id=1, source_target_pairs={{0,7},{1,0},{2,1},{3,2},{4,3},{5,4},{6,5},{7,6},{8,15},{9,8},{10,9... | collective-permute-start | bytes 786440 | tf_op jit(solution)/shard_map/ppermute | solution.py:212
  166.7 21.1 %collective-permute-start.12 = (f32[512,128]{1,0:T(8,128)S(1)}, f32[512,128]{1,0:T(8,128)S(1)}, u32[]{:S(2)}, u32[]{:S(2)}) collective-permute-start(f32[512,128]{1,0:T(8,128)S(1)} %get-tuple-element.38), channel_id=1, source_target_pairs={{0,1},{1,2},{2,3},{3,4},{4,5},{5,6},{6,7},{7,0},{8,9},{9,10},{10,1... | collective-permute-start | bytes 786440 | tf_op jit(solution)/shard_map/ppermute | solution.py:211
  176.9 13.4 %collective-permute-start.17 = (f32[512,128]{1,0:T(8,128)S(1)}, f32[512,128]{1,0:T(8,128)S(1)}, u32[]{:S(2)}, u32[]{:S(2)}) collective-permute-start(f32[512,128]{1,0:T(8,128)S(1)} %bitcast_add_fusion.2), channel_id=1, source_target_pairs={{0,7},{1,0},{2,1},{3,2},{4,3},{5,4},{6,5},{7,6},{8,15},{9,8},{10,9... | collective-permute-start | bytes 786440 | tf_op jit(solution)/shard_map/ppermute | solution.py:212
  187.8 16.6 %copy-start.16 = (f32[512,256]{1,0:T(8,128)S(1)}, f32[512,256]{1,0:T(8,128)}, u32[]{:S(2)}) copy-start(f32[512,256]{1,0:T(8,128)} %maximum_select_fusion) | copy-start | bytes 1572868
  187.8 16.8 %copy-start.14 = (f32[528,256]{1,0:T(8,128)S(1)}, f32[528,256]{1,0:T(8,128)}, u32[]{:S(2)}) copy-start(f32[528,256]{1,0:T(8,128)} %pad_maximum_fusion.2) | copy-start | bytes 1622020
  190.4 13.6 %collective-permute-start.13 = (f32[512,128]{1,0:T(8,128)S(1)}, f32[512,128]{1,0:T(8,128)S(1)}, u32[]{:S(2)}, u32[]{:S(2)}) collective-permute-start(f32[512,128]{1,0:T(8,128)S(1)} %get-tuple-element.34), channel_id=1, source_target_pairs={{0,1},{1,2},{2,3},{3,4},{4,5},{5,6},{6,7},{7,0},{8,9},{9,10},{10,1... | collective-permute-start | bytes 786440 | tf_op jit(solution)/shard_map/ppermute | solution.py:211
  204.0 7.6 %collective-permute-start.14 = (f32[512,128]{1,0:T(8,128)S(1)}, f32[512,128]{1,0:T(8,128)S(1)}, u32[]{:S(2)}, u32[]{:S(2)}) collective-permute-start(f32[512,128]{1,0:T(8,128)S(1)} %bitcast_add_fusion.4), channel_id=1, source_target_pairs={{0,1},{1,2},{2,3},{3,4},{4,5},{5,6},{6,7},{7,0},{8,9},{9,10},{10,1... | collective-permute-start | bytes 786440 | tf_op jit(solution)/shard_map/ppermute | solution.py:211
  204.8 8.6 %collective-permute-start.18 = (f32[512,128]{1,0:T(8,128)S(1)}, f32[512,128]{1,0:T(8,128)S(1)}, u32[]{:S(2)}, u32[]{:S(2)}) collective-permute-start(f32[512,128]{1,0:T(8,128)S(1)} %get-tuple-element.33), channel_id=1, source_target_pairs={{0,7},{1,0},{2,1},{3,2},{4,3},{5,4},{6,5},{7,6},{8,15},{9,8},{10,9... | collective-permute-start | bytes 786440 | tf_op jit(solution)/shard_map/ppermute | solution.py:212
  211.6 6.7 %collective-permute-start.15 = (f32[512,128]{1,0:T(8,128)S(1)}, f32[512,128]{1,0:T(8,128)S(1)}, u32[]{:S(2)}, u32[]{:S(2)}) collective-permute-start(f32[512,128]{1,0:T(8,128)S(1)} %bitcast_add_fusion.3), channel_id=1, source_target_pairs={{0,1},{1,2},{2,3},{3,4},{4,5},{5,6},{6,7},{7,0},{8,9},{9,10},{10,1... | collective-permute-start | bytes 786440 | tf_op jit(solution)/shard_map/ppermute | solution.py:215
  222.7 19.7 %copy-start.20 = (f32[16,128]{1,0:T(8,128)S(1)}, f32[16,128]{1,0:T(8,128)}, u32[]{:S(2)}) copy-start(f32[16,128]{1,0:T(8,128)} %param.12) | copy-start | bytes 24580
  222.7 19.7 %copy-start.21 = (f32[16,128]{1,0:T(8,128)S(1)}, f32[16,128]{1,0:T(8,128)}, u32[]{:S(2)}) copy-start(f32[16,128]{1,0:T(8,128)} %param.17) | copy-start | bytes 24580
  223.5 18.8 %all-to-all-start = ((f32[16,3,16,128]{3,2,1,0:T(8,128)}), f32[16,3,16,128]{3,2,1,0:T(8,128)S(1)}, u32[]{:S(2)}, u32[]{:S(2)}) async-start(f32[16,3,16,128]{3,2,1,0:T(8,128)} %copy.19), calls=%async_computation.1 | async-start | bytes 786432 | tf_op jit(solution)/shard_map/all_to_all | solution.py:233
  (18 other events, 138.4 us)
Sparse Core Ops, SparseCore 0:
  50.0 96.9 all-gather.2
  154.8 47.8 reduce-scatter.1

commit v4 on v3

v4 whole, which is shorter than its diff:
```python
import functools

import jax
import jax.numpy as jnp
from jax import lax
from jax.experimental import pallas as pl
from jax.experimental.pallas import tpu as pltpu
from jax.sharding import PartitionSpec as P

ROW_AXES = ("x", "y_lo", "core")
COL_AXES = ("y_hi", "z")
ALL_AXES = ROW_AXES + COL_AXES
exact = lax.Precision.HIGHEST


def split(a):
    hi = a.astype(jnp.bfloat16)
    return hi, (a - hi.astype(jnp.float32)).astype(jnp.bfloat16)


def dot3(a, b):
    f = functools.partial(jnp.dot, preferred_element_type=jnp.float32)
    return f(a[0], b[0]) + (f(a[0], b[1]) + f(a[1], b[0]))


def one_kernel(sc_ref, gh_ref, gl_ref, a_ref, b_ref, out_ref):
    h = sc_ref[0]
    acc = None
    for k in range(2):
        half = h if k == 0 else 1 - h
        one = jnp.concatenate([a_ref[half, 0, 0, 0], b_ref[half, 0, 0, 0]], axis=1)
        term = dot3((gh_ref[k], gl_ref[k]), split(one))
        acc = term if acc is None else acc + term
    out_ref[0] = -acc[:, :128]
    out_ref[1] = -acc[:, 128:]


def two_kernel(sc_ref, gh_ref, gl_ref, *refs):
    twos, lps, pars, out_ref = refs[:4], refs[4:8], refs[8:10], refs[10]
    h = sc_ref[0]
    lp = jnp.concatenate(
        [jnp.concatenate([r[0, 0, 0] for r in lps[2 * t : 2 * t + 2]], axis=0) for t in range(2)],
        axis=1,
    )
    lp = split(lp)
    acc = None
    for k in range(2):
        half = h if k == 0 else 1 - h
        two = jnp.concatenate([twos[k][0, 0, 0], twos[2 + k][0, 0, 0]], axis=1)
        par = jnp.concatenate([r[half, 0, 0, 0] for r in pars], axis=1)
        folded = two - dot3(split(par), lp)
        term = dot3((gh_ref[k], gl_ref[k]), split(folded))
        acc = term if acc is None else acc + term
    out_ref[0] = -acc[:, :128]
    out_ref[1] = -acc[:, 128:]


WHOLE_G = pl.BlockSpec((2, 512, 512), lambda i, sc: (0, 0, 0))
PARAMS = pltpu.CompilerParams(vmem_limit_bytes=56 * 2**20)


def one_piece(first, stride):
    def place(i, sc):
        code = sc[first + stride * i]
        return (0, code // 8, code // 4 % 2, code % 4, 0, 0)

    return pl.BlockSpec((2, 1, 1, 1, 512, 128), place)


def two_piece(rows, block, first, stride):
    def place(i, sc):
        code = sc[first + stride * i]
        return (code // 8, code // 2 % 4, code % 2, block, 0)

    return pl.BlockSpec((1, 1, 1, rows, 128), place)


def product(kernel, pieces, flops, scalars, pairs, g_hi, g_lo, *gathered):
    return pl.pallas_call(
        kernel,
        grid_spec=pltpu.PrefetchScalarGridSpec(
            num_scalar_prefetch=1,
            grid=(pairs,),
            in_specs=[WHOLE_G, WHOLE_G, *pieces],
            out_specs=pl.BlockSpec((2, 512, 128), lambda i, sc: (i, 0, 0)),
        ),
        out_shape=jax.ShapeDtypeStruct((2 * pairs, 512, 128), jnp.float32),
        compiler_params=PARAMS,
        cost_estimate=pl.CostEstimate(
            flops=pairs * flops, bytes_accessed=pairs * 4_000_000, transcendentals=0
        ),
    )(scalars, g_hi, g_lo, *gathered)


ONE_PIECES = [one_piece(1 + t, 2) for t in range(2)]
TWO_PIECES = (
    [two_piece(512, 0, 1 + i, 10) for i in range(4)]
    + [two_piece(128, 4, 5 + i, 10) for i in range(4)]
    + [one_piece(9 + t, 10) for t in range(2)]
)


def chip_and_core(shift):
    up = (shift >= 1) & (shift <= 4)
    return (up * (4 - shift) + (1 - up) * (8 - shift)) % 4, 1 - up


def spread_pairs(sign):
    pairs = []
    for i in range(256):
        row, col = divmod(i, 16)
        half, z, h, s = row // 8, row % 8, col // 8, col % 8
        chip, core = chip_and_core(sign * (z - s) % 8)
        pairs.append((i, (half * 8 + chip * 2 + int(core)) * 16 + h * 8 + z))
    return pairs


def ring(n, step):
    return [(i, (i + step) % n) for i in range(n)]


def local(g_top, l_one, struct_one, dinv_one, l_two, lp_two, parent_two, pos_two, dinv_two):
    row = lax.axis_index(ROW_AXES)
    h = lax.axis_index("y_hi")
    z = lax.axis_index("z")
    mine = h * 4 + z // 2
    parent = parent_two[mine]

    blocks = jnp.arange(2, dtype=jnp.int32) * 16 + row
    list_one = lax.dynamic_index_in_dim(struct_one, mine, 0, keepdims=False)
    list_parent = lax.dynamic_index_in_dim(struct_one, parent, 0, keepdims=False)
    places = lax.dynamic_index_in_dim(pos_two, mine, 0, keepdims=False)
    picked = jnp.any(places[:, None] == jnp.arange(16)[None, :], axis=0)
    keep_one = jnp.any(list_one[None, :] == blocks[:, None], axis=1)[:, None, None]
    keep_two = jnp.any((list_parent[None, :] == blocks[:, None]) & picked[None, :], axis=1)
    keep_two = keep_two[:, None, None]
    one = jnp.where(keep_one, l_one, 0.0).reshape(512, 128)
    two = jnp.where(keep_two, l_two, 0.0).reshape(512, 128)

    lp_piece = lax.dynamic_slice_in_dim(lp_two, row // 8 * 128, 128, 0)
    near_one = lax.ppermute(one, ALL_AXES, spread_pairs(1))
    near_two = lax.ppermute(jnp.concatenate([two, lp_piece]), ALL_AXES, spread_pairs(-1))
    g_other = lax.ppermute(g_top, "y_hi", ring(2, 1))
    gathered = lax.all_gather(near_one, ("x", "y_hi", "y_lo", "core"), axis=0, tiled=False)
    gathered = gathered.reshape(2, 2, 2, 4, 512, 128)
    near_two, packed, two_sent, g_other = lax.optimization_barrier(
        (near_two, jnp.concatenate([one, dinv_one]), jnp.concatenate([two, lp_two]), g_other)
    )
    y_pair = jnp.stack([near_two, lax.ppermute(near_two, "y_lo", ring(2, 1))])
    x_all = jnp.stack([y_pair] + [lax.ppermute(y_pair, "x", ring(4, d)) for d in (1, 2, 3)])
    gathered_two = jnp.stack([x_all, lax.ppermute(x_all, "core", ring(2, 1))])

    def place_one(slot):
        chip, core = chip_and_core((z - slot) % 8)
        return chip // 2 * 8 + slot // 8 * 4 + chip % 2 * 2 + core

    def place_two(slot, half):
        chip, core = chip_and_core((slot - z) % 8)
        x_off = (lax.axis_index("x") - half * 2 - chip // 2) % 4
        y_off = lax.axis_index("y_lo") ^ (chip % 2)
        return (lax.axis_index("core") ^ core) * 8 + x_off * 2 + y_off

    g = jnp.stack([g_top, g_other]).reshape(2, 512, 512)
    g_hi32 = lax.reduce_precision(g, 8, 7)
    g_hi = g_hi32.astype(jnp.bfloat16)
    g_lo = (g - g_hi32).astype(jnp.bfloat16)

    pieces = {0: packed}
    right = left = packed
    for d in range(1, 5):
        right = lax.ppermute(right, "z", ring(8, 1))
        pieces[-d] = right
        if d < 4:
            left = lax.ppermute(left, "z", ring(8, -1))
            pieces[d] = left

    def fetch(super_index):
        parts = []
        for part in range(2):
            want = super_index % 4 * 2 + part
            total = jnp.zeros((528, 128), jnp.float32)
            for d, one_piece_here in pieces.items():
                total = jnp.where(want == (z + d) % 8, one_piece_here, total)
            parts.append(total)
        return jnp.concatenate(parts, axis=1)

    par_here = fetch(parent)
    par_there = fetch(parent_two[(1 - h) * 4 + z // 2])
    even = z % 2 == 0
    pair_up = lambda a, b: jnp.where(even, jnp.concatenate([a, b], 1), jnp.concatenate([b, a], 1))
    own_one = pair_up(one, jnp.where(even, pieces[1], pieces[-1])[:512])
    two_next = lax.ppermute(two_sent, "z", [(i, i ^ 1) for i in range(8)])
    own_two = pair_up(two, two_next[:512])
    lp_own = pair_up(lp_two, two_next[512:])

    slots = h * 8 + jnp.arange(8, dtype=jnp.int32)
    h_now, par_here, par_there, own_one, own_two, lp_own = lax.optimization_barrier(
        (h, par_here, par_there, own_one, own_two, lp_own)
    )
    scalars = jnp.concatenate([h_now[None], place_one(slots)]).astype(jnp.int32)
    part_one = product(
        one_kernel, ONE_PIECES, 800_000_000, scalars, 4, g_hi, g_lo, gathered, gathered
    )
    inv_one = lax.psum_scatter(part_one, "z", scatter_dimension=0, tiled=False)

    def level_two(first_pair, h_in):
        both = jnp.arange(2, dtype=jnp.int32)
        supers = h * 4 + (first_pair + both) % 4
        parents = parent_two.at[supers].get(mode="promise_in_bounds")
        two_slots = supers[:, None, None] * 2 + both[None, :, None]
        near_first = place_two(two_slots, jnp.where(both == 0, h, 1 - h)[None, None, :])
        in_order = place_two(two_slots, both[None, None, :])
        par_codes = place_one(parents[:, None] * 2 + both[None, :])
        codes = jnp.concatenate(
            [near_first.reshape(2, 4), in_order.reshape(2, 4), par_codes], axis=1
        )
        scalars = jnp.concatenate([h_in[None], codes.reshape(20)]).astype(jnp.int32)
        arrays = [gathered_two] * 8 + [gathered] * 2
        return product(two_kernel, TWO_PIECES, 1_600_000_000, scalars, 2, g_hi, g_lo, *arrays)

    pair_now = (z + 4) // 2
    h_next, part_one = lax.optimization_barrier((h_now, part_one[0, :8]))
    early = level_two(pair_now, h_next)
    h_last, early = lax.optimization_barrier((h_next, early))
    late = level_two(pair_now + 2, h_last)

    def term(d):
        take = lambda i: early[i] if i < 4 else late[i - 4]
        return jnp.where(even, take((d - 4) % 8), take((d - 3) % 8))

    up = lax.ppermute(term(4), "z", ring(8, 1))
    down = lax.ppermute(term(-3), "z", ring(8, -1))
    up, down, late = lax.optimization_barrier((up, down, late))
    up = lax.ppermute(up + term(3), "z", ring(8, 1))
    down = lax.ppermute(down + term(-2), "z", ring(8, -1))
    up = lax.ppermute(up + term(2), "z", ring(8, 1))
    down = lax.ppermute(down + term(-1), "z", ring(8, -1))
    inv_two = lax.ppermute(up + term(1), "z", ring(8, 1)) + down + term(0)
    par_other = lax.ppermute(par_there, "y_hi", ring(2, 1))
    par = jnp.where(parent // 4 == h, par_here, par_other)
    panel_one = jnp.where(keep_one, inv_one.reshape(2, 256, 128), 0.0)
    panel_two = jnp.where(keep_two, inv_two.reshape(2, 256, 128), 0.0)

    dot_t = lambda a, b: lax.dot_general(a, b, (((0,), (0,)), ((), ())), precision=exact)
    scaled = jnp.dot(par[512:], lp_two, precision=exact)
    lp_slab = lax.dynamic_slice_in_dim(lp_own, row * 16, 16, 0)
    quad = dot_t(lp_slab, scaled)
    term_one = dot_t(own_one, inv_one)
    term_par = dot_t(par[:512], inv_two)
    term_two = quad - dot_t(own_two, inv_two) + dot_t(lp_own, term_par)
    terms = jnp.stack([term_one, term_par, term_two]).reshape(3, 16, 16, 128).transpose(1, 0, 2, 3)
    sums = jnp.sum(lax.all_to_all(terms, ROW_AXES, 0, 0), axis=0)
    diag_one = dinv_one - sums[0]
    parent_rows = -(sums[1] + scaled)
    diag_two = dinv_two + sums[2]
    return (panel_one, diag_one, panel_two, parent_rows, diag_two)


def solution(mesh):
    fine = jax.sharding.Mesh(mesh.devices.reshape(4, 2, 2, 2, 8), ALL_AXES)
    tall = P(None, ROW_AXES, COL_AXES)
    flat = P(ROW_AXES, COL_AXES)
    return jax.shard_map(
        local,
        mesh=fine,
        in_specs=(
            P(None, ROW_AXES, None, COL_AXES),
            tall,
            P(),
            flat,
            tall,
            P(None, COL_AXES),
            P(),
            P(),
            flat,
        ),
        out_specs=(tall, flat, tall, flat, flat),
        check_vma=False,
    )
```

time: 251 us -> 267 us (1.064)
  waiting for transfers between devices: 116 us -> 93.6 us
  starting transfers between devices: 57.3 us -> 75.7 us
  other arithmetic: 19.6 us -> 29 us
  Pallas kernels: 20.9 us -> 26.5 us
    all_gather x1, waiting for transfers between devices: 25.5 us -> 0.01 us  [local(): lax.all_gather(near_one, ('x', 'y_hi', 'y_lo', 'core'), axis=0, tiled=False)]
    ppermute x4, waiting for transfers between devices: 25.5 us -> 4.03 us  [local(): right = lax.ppermute(right, 'z', ring(8, 1))]
    ppermute x1, waiting for transfers between devices: 0.01 us -> 17.4 us  [local(): g_other = lax.ppermute(g_top, 'y_hi', ring(2, 1))]
    ppermute x8 -> x13, starting transfers between devices: 11.2 us -> 25.7 us  [the longest x3 12.8 us: local(): lax.ppermute(y_pair, 'x', ring(4, d))]
    ppermute x1, starting transfers between devices: 3.66 us -> 15.9 us  [local(): lax.ppermute(jnp.concatenate([two, lp_piece]), ALL_AXES, spread_pairs(-1))]
    another operation x1 -> x3, other arithmetic: 0.07 us -> 10.1 us  [the longest x2 8.96 us: local(): gathered_two = jnp.stack([x_all, lax.ppermute(x_all, 'core', ring(2, 1))])]
    ppermute x8 -> x13, waiting for transfers between devices: 45.6 us -> 52.6 us  [the longest x3 21 us: local(): lax.ppermute(y_pair, 'x', ring(4, d))]
    pallas_call x3, Pallas kernels: 20.9 us -> 26.5 us  [product(): pl.pallas_call(kernel, grid_spec=pltpu.PrefetchScalarGridSpec(num_scalar_...]
  transfers between devices with their start and end apart: 22 -> 27, of which waited for: 15 -> 15; matrix products, arithmetic and copies ran while one was open for 12% -> 16% of each run, Pallas kernels for 6% -> 10%
where the time goes in v4:
time: 267 us; the launch traced here: 265 us
  waiting for transfers between devices  93.6 us (35%)
  starting transfers between devices  75.7 us (28%)
  other arithmetic  29 us (11%)
  Pallas kernels  26.5 us (10%)
  between operations  20.7 us (8%)
  local copies, waits for them, and re-layouts  14.9 us (6%)
  matrix products  4.77 us (2%)
    pallas_call x3, Pallas kernels, product(): pl.pallas_call(kernel, grid_spec=pltpu.PrefetchScalarGridSpec(num_scalar_...  26.5 us
    ppermute x3, waiting for transfers between devices, local(): lax.ppermute(y_pair, 'x', ring(4, d))  21 us
    ppermute x1, waiting for transfers between devices, local(): g_other = lax.ppermute(g_top, 'y_hi', ring(2, 1))  17.4 us
    ppermute x1, starting transfers between devices, local(): lax.ppermute(jnp.concatenate([two, lp_piece]), ALL_AXES, spread_pairs(-1))  15.9 us
    ppermute x3, starting transfers between devices, local(): lax.ppermute(y_pair, 'x', ring(4, d))  12.8 us
    ppermute x3, starting transfers between devices, local(): left = lax.ppermute(left, 'z', ring(8, -1))  12.5 us
    another operation x2, other arithmetic, local(): gathered_two = jnp.stack([x_all, lax.ppermute(x_all, 'core', ring(2, 1))])  8.96 us
    all_to_all x1, starting transfers between devices, local(): sums = jnp.sum(lax.all_to_all(terms, ROW_AXES, 0, 0), axis=0)  8.95 us
  transfers between devices with their start and end apart: 27, of which 15 were waited for; matrix products, arithmetic and copies ran while one was open for 16% of the time, Pallas kernels for 10%

profile of v4, /device:TPU:1, one launch (start us, length us, event | category | flops | bytes accessed | tf_op | source)
XLA Modules:
  0.0 265.2 jit_solution(1377818638170900695)
XLA Ops:
  12.7 6.9 %collective-permute-start.10 = (f32[512,128]{1,0:T(8,128)S(1)}, f32[512,128]{1,0:T(8,128)S(1)}, u32[]{:S(2)}, u32[]{:S(2)}) collective-permute-start(f32[512,128]{1,0:T(8,128)S(1)} %bitcast.90), channel_id=1, source_target_pairs={{0,16},{1,48},{2,80},{3,112},{4,0},{5,32},{6,64},{7,96},{8,24},{9,... | collective-permute-start | bytes 786440 | tf_op jit(solution)/shard_map/ppermute | solution.py:141
  19.6 5.7 %collective-permute-done.10 = f32[512,128]{1,0:T(8,128)S(1)} collective-permute-done((f32[512,128]{1,0:T(8,128)S(1)}, f32[512,128]{1,0:T(8,128)S(1)}, u32[]{:S(2)}, u32[]{:S(2)}) %collective-permute-start.10) | collective-permute-done | bytes 262176 | tf_op jit(solution)/shard_map/ppermute | solution.py:141
  28.0 15.9 %collective-permute-start = (f32[640,128]{1,0:T(8,128)S(1)}, f32[640,128]{1,0:T(8,128)S(1)}, u32[]{:S(2)}, u32[]{:S(2)}) collective-permute-start(f32[640,128]{1,0:T(8,128)S(1)} %pad_maximum_fusion.6), channel_id=1, source_target_pairs={{0,16},{1,96},{2,64},{3,32},{4,0},{5,112},{6,80},{7,48},{8,24},{9,... | collective-permute-start | bytes 983048 | tf_op jit(solution)/shard_map/ppermute | solution.py:142
  43.9 2.7 %collective-permute-start.1 = (f32[2,256,2,256]{3,2,1,0:T(2,128)}, f32[2,256,2,256]{3,2,1,0:T(2,128)S(1)}, u32[]{:S(2)}, u32[]{:S(2)}) collective-permute-start(f32[2,256,2,256]{3,2,1,0:T(2,128)} %param.9), channel_id=1, source_target_pairs={{0,8},{8,0},{1,9},{9,1},{2,10},{10,2},{3,11},{11,3},{4,12},{12,4},... | collective-permute-start | bytes 3145736 | tf_op jit(solution)/shard_map/ppermute | solution.py:143
  50.0 3.3 %collective-permute-done = f32[640,128]{1,0:T(8,128)S(1)} collective-permute-done((f32[640,128]{1,0:T(8,128)S(1)}, f32[640,128]{1,0:T(8,128)S(1)}, u32[]{:S(2)}, u32[]{:S(2)}) %collective-permute-start) | collective-permute-done | bytes 327712 | tf_op jit(solution)/shard_map/ppermute | solution.py:142
  53.3 17.4 %collective-permute-done.1 = f32[2,256,2,256]{3,2,1,0:T(2,128)S(1)} collective-permute-done((f32[2,256,2,256]{3,2,1,0:T(2,128)}, f32[2,256,2,256]{3,2,1,0:T(2,128)S(1)}, u32[]{:S(2)}, u32[]{:S(2)}) %collective-permute-start.1) | collective-permute-done | bytes 1048608 | tf_op jit(solution)/shard_map/ppermute | solution.py:143
  70.8 7.6 %collective-permute-done.12 = f32[640,128]{1,0:T(8,128)S(1)} collective-permute-done((f32[640,128]{1,0:T(8,128)S(1)}, f32[640,128]{1,0:T(8,128)S(1)}, u32[]{:S(2)}, u32[]{:S(2)}) %collective-permute-start.12) | collective-permute-done | bytes 327712 | tf_op jit(solution)/shard_map/ppermute | solution.py:149
  79.6 10.4 %collective-permute-start.13 = (f32[2,640,128]{2,1,0:T(8,128)}, f32[2,640,128]{2,1,0:T(8,128)}, u32[]{:S(2)}, u32[]{:S(2)}) collective-permute-start(f32[2,640,128]{2,1,0:T(8,128)} %get-tuple-element.46), channel_id=1, source_target_pairs={{0,64},{64,128},{128,192},{192,0},{1,65},{65,129},{129,193},{193,1... | collective-permute-start | bytes 1966088 | tf_op jit(solution)/shard_map/ppermute | solution.py:150
  90.0 2.2 collective-permute-start.14
  98.2 3.5 %collective-permute-start.6 = (f32[528,128]{1,0:T(8,128)S(1)}, f32[528,128]{1,0:T(8,128)S(1)}, u32[]{:S(2)}, u32[]{:S(2)}) collective-permute-start(f32[528,128]{1,0:T(8,128)S(1)} %pad_maximum_fusion.7), channel_id=1, source_target_pairs={{0,7},{1,0},{2,1},{3,2},{4,3},{5,4},{6,5},{7,6},{8,15},{9,8},{10,9... | collective-permute-start | bytes 811016 | tf_op jit(solution)/shard_map/ppermute | solution.py:174
  104.6 3.1 %stack.53 = f32[1,512,512]{2,1,0:T(8,128)} reshape(f32[2,256,2,256]{3,2,1,0:T(2,128)} %copy-done.19) | data formatting | bytes 2097152 | tf_op jit(solution)/shard_map/stack | solution.py:163
  110.9 2.1 collective-permute-start.7
  112.9 5.7 %collective-permute-done.13 = f32[2,640,128]{2,1,0:T(8,128)} collective-permute-done((f32[2,640,128]{2,1,0:T(8,128)}, f32[2,640,128]{2,1,0:T(8,128)}, u32[]{:S(2)}, u32[]{:S(2)}) %collective-permute-start.13) | collective-permute-done | bytes 655392 | tf_op jit(solution)/shard_map/ppermute | solution.py:150
  118.6 15.4 %collective-permute-done.14 = f32[2,640,128]{2,1,0:T(8,128)} collective-permute-done((f32[2,640,128]{2,1,0:T(8,128)}, f32[2,640,128]{2,1,0:T(8,128)}, u32[]{:S(2)}, u32[]{:S(2)}) %collective-permute-start.14) | collective-permute-done | bytes 655392 | tf_op jit(solution)/shard_map/ppermute | solution.py:150
  134.0 3.9 %fusion.69 = (f32[1,4,2,640,128]{4,3,2,1,0:T(8,128)S(1)}, f32[4,2,640,128]{3,2,1,0:T(8,128)}) fusion(f32[1,2,640,128]{3,2,1,0:T(8,128)} %bitcast.22, f32[1,2,640,128]{3,2,1,0:T(8,128)} %bitcast.21, f32[1,2,640,128]{3,2,1,0:T(8,128)} %bitcast.20, f32[1,2,640,128]{3,2,1,0:T(8,128)} %get-tuple-element.45), kind=kLoop, calls=%fused_computation.236 | loop fusion | flops 1966080 | bytes 7864320 | tf_op jit(solution)/shard_map/stack | solution.py:151
  139.6 6.9 %collective-permute-start.8 = (f32[528,128]{1,0:T(8,128)S(1)}, f32[528,128]{1,0:T(8,128)S(1)}, u32[]{:S(2)}, u32[]{:S(2)}) collective-permute-start(f32[528,128]{1,0:T(8,128)S(1)} %collective-permute-done.7), channel_id=1, source_target_pairs={{0,7},{1,0},{2,1},{3,2},{4,3},{5,4},{6,5},{7,6},{8,15},{9,8},{10,9... | collective-permute-start | bytes 811016 | tf_op jit(solution)/shard_map/ppermute | solution.py:174
  149.0 3.4 %collective-permute-done.8 = f32[528,128]{1,0:T(8,128)S(1)} collective-permute-done((f32[528,128]{1,0:T(8,128)S(1)}, f32[528,128]{1,0:T(8,128)S(1)}, u32[]{:S(2)}, u32[]{:S(2)}) %collective-permute-start.8) | collective-permute-done | bytes 270368 | tf_op jit(solution)/shard_map/ppermute | solution.py:174
  152.4 3.6 %collective-permute-done.5 = f32[528,128]{1,0:T(8,128)S(1)} collective-permute-done((f32[528,128]{1,0:T(8,128)S(1)}, f32[528,128]{1,0:T(8,128)S(1)}, u32[]{:S(2)}, u32[]{:S(2)}) %collective-permute-start.5) | collective-permute-done | bytes 270368 | tf_op jit(solution)/shard_map/ppermute | solution.py:171
  160.1 8.1 %shard_map.128 = f32[8,512,128]{2,1,0:T(8,128)} custom-call(s32[9]{0:T(128)} %pad_add_fusion.2.sc_ref, bf16[2,512,512]{2,1,0:T(8,128)(2,1)} %get-tuple-element.42.gh_ref, bf16[2,512,512]{2,1,0:T(8,128)(2,1)} %get-tuple-element.41.gl_ref, f32[2,2,2,4,512,128]{5,4,3,2,1,0:T(8,128)} %bitcast.80, f32[2,2,2,4,512,128]{5,4,3,2,1,0:T(8,128)} %bitcast.81), custom_call_target="tpu_custom_call" | custom-call | flops 3200000000 | bytes 16000000 | tf_op jit(solution)/shard_map/pallas_call | solution.py:79
  168.2 5.0 %pad_maximum_fusion.refs_0_.refs_1_.refs_2_.refs_3_.refs_4_.refs_5_.refs_6_.refs_7_ = f32[2,4,2,640,128]{4,3,2,1,0:T(8,128)} fusion(f32[1,4,2,640,128]{4,3,2,1,0:T(8,128)} %bitcast.24, f32[1,4,2,640,128]{4,3,2,1,0:T(8,128)S(1)} %get-tuple-element.37), kind=kLoop, calls=%fused_computation.2 | loop fusion | flops 1310720 | bytes 10485760 | tf_op jit(solution)/shard_map/stack | solution.py:151
  173.2 9.1 %shard_map.129 = f32[4,512,128]{2,1,0:T(8,128)} custom-call(s32[21]{0:T(128)} %pad_add_fusion.3.sc_ref, bf16[2,512,512]{2,1,0:T(8,128)(2,1)} %get-tuple-element.42.gh_ref, bf16[2,512,512]{2,1,0:T(8,128)(2,1)} %get-tuple-element.41.gl_ref, f32[2,4,2,640,128]{4,3,2,1,0:T(8,128)} %pad_maximum_fusion.refs_0_.refs_1_.refs_2_.refs_3_.refs_4_.refs_5_.refs_6_.refs_7_, ...), custom_call_target="tpu_custom_call" | custom-call | flops 3200000000 | bytes 8000000 | tf_op jit(solution)/shard_map/pallas_call | solution.py:79
  183.6 2.7 %collective-permute-start.18 = (f32[512,128]{1,0:T(8,128)S(1)}, f32[512,128]{1,0:T(8,128)S(1)}, u32[]{:S(2)}, u32[]{:S(2)}) collective-permute-start(f32[512,128]{1,0:T(8,128)S(1)} %get-tuple-element.43), channel_id=1, source_target_pairs={{0,7},{1,0},{2,1},{3,2},{4,3},{5,4},{6,5},{7,6},{8,15},{9,8},{10,9... | collective-permute-start | bytes 786440 | tf_op jit(solution)/shard_map/ppermute | solution.py:232
  186.9 9.3 %shard_map.130 = f32[4,512,128]{2,1,0:T(8,128)} custom-call(s32[21]{0:T(128)} %pad_add_fusion.4.sc_ref, bf16[2,512,512]{2,1,0:T(8,128)(2,1)} %get-tuple-element.42.gh_ref, bf16[2,512,512]{2,1,0:T(8,128)(2,1)} %get-tuple-element.41.gl_ref, f32[2,4,2,640,128]{4,3,2,1,0:T(8,128)} %pad_maximum_fusion.refs_0_.refs_1_.refs_2_.refs_3_.refs_4_.refs_5_.refs_6_.refs_7_, ...), custom_call_target="tpu_custom_call" | custom-call | flops 3200000000 | bytes 8000000 | tf_op jit(solution)/shard_map/pallas_call | solution.py:79
  197.3 3.6 %collective-permute-start.22 = (f32[512,128]{1,0:T(8,128)S(1)}, f32[512,128]{1,0:T(8,128)S(1)}, u32[]{:S(2)}, u32[]{:S(2)}) collective-permute-start(f32[512,128]{1,0:T(8,128)S(1)} %bitcast_add_fusion.2), channel_id=1, source_target_pairs={{0,7},{1,0},{2,1},{3,2},{4,3},{5,4},{6,5},{7,6},{8,15},{9,8},{10,9... | collective-permute-start | bytes 786440 | tf_op jit(solution)/shard_map/ppermute | solution.py:235
  200.9 2.8 %collective-permute-start.11 = (f32[528,256]{1,0:T(8,128)}, f32[528,256]{1,0:T(8,128)}, u32[]{:S(2)}, u32[]{:S(2)}) collective-permute-start(f32[528,256]{1,0:T(8,128)} %get-tuple-element.26), channel_id=1, source_target_pairs={{0,8},{8,0},{1,9},{9,1},{2,10},{10,2},{3,11},{11,3},{4,12},{12,4},... | collective-permute-start | bytes 1622024 | tf_op jit(solution)/shard_map/ppermute | solution.py:239
  203.7 6.6 %collective-permute-done.22 = f32[512,128]{1,0:T(8,128)S(1)} collective-permute-done((f32[512,128]{1,0:T(8,128)S(1)}, f32[512,128]{1,0:T(8,128)S(1)}, u32[]{:S(2)}, u32[]{:S(2)}) %collective-permute-start.22) | collective-permute-done | bytes 262176 | tf_op jit(solution)/shard_map/ppermute | solution.py:235
  213.7 7.0 %collective-permute-done.19 = f32[512,128]{1,0:T(8,128)} collective-permute-done((f32[512,128]{1,0:T(8,128)}, f32[512,128]{1,0:T(8,128)}, u32[]{:S(2)}, u32[]{:S(2)}) %collective-permute-start.19) | collective-permute-done | bytes 262176 | tf_op jit(solution)/shard_map/ppermute | solution.py:234
  222.1 2.7 %collective-permute-start.23 = (f32[512,128]{1,0:T(8,128)S(1)}, f32[512,128]{1,0:T(8,128)S(1)}, u32[]{:S(2)}, u32[]{:S(2)}) collective-permute-start(f32[512,128]{1,0:T(8,128)S(1)} %get-tuple-element.39), channel_id=1, source_target_pairs={{0,7},{1,0},{2,1},{3,2},{4,3},{5,4},{6,5},{7,6},{8,15},{9,8},{10,9... | collective-permute-start | bytes 786440 | tf_op jit(solution)/shard_map/ppermute | solution.py:237
  224.8 3.6 %collective-permute-done.20 = f32[512,128]{1,0:T(8,128)S(1)} collective-permute-done((f32[512,128]{1,0:T(8,128)S(1)}, f32[512,128]{1,0:T(8,128)S(1)}, u32[]{:S(2)}, u32[]{:S(2)}) %collective-permute-start.20) | collective-permute-done | bytes 262176 | tf_op jit(solution)/shard_map/ppermute | solution.py:236
  229.2 5.8 %collective-permute-done.21 = f32[512,128]{1,0:T(8,128)S(1)} collective-permute-done((f32[512,128]{1,0:T(8,128)S(1)}, f32[512,128]{1,0:T(8,128)S(1)}, u32[]{:S(2)}, u32[]{:S(2)}) %collective-permute-start.21) | collective-permute-done | bytes 262176 | tf_op jit(solution)/shard_map/ppermute | solution.py:238
  240.1 9.0 %all-to-all-start = ((f32[16,3,16,128]{3,2,1,0:T(8,128)}), f32[16,3,16,128]{3,2,1,0:T(8,128)S(1)}, u32[]{:S(2)}, u32[]{:S(2)}) async-start(f32[16,3,16,128]{3,2,1,0:T(8,128)} %copy.19), calls=%async_computation.1 | async-start | bytes 786432 | tf_op jit(solution)/shard_map/all_to_all | solution.py:252
  250.7 7.0 %all-to-all-done = f32[16,3,16,128]{3,2,1,0:T(8,128)S(1)} async-done(((f32[16,3,16,128]{3,2,1,0:T(8,128)}), f32[16,3,16,128]{3,2,1,0:T(8,128)S(1)}, u32[]{:S(2)}, u32[]{:S(2)}) %all-to-all-start) | async-done | bytes 393248 | tf_op jit(solution)/shard_map/all_to_all | solution.py:252
  (163 shorter events, 42.6 us)
Async XLA Ops:
  7.2 40.6 %copy-start.1 = (s32[8]{0:T(128)S(1)}, s32[8]{0:T(128)}, u32[]{:S(2)}) copy-start(s32[8]{0:T(128)} %param.15) | copy-start | bytes 100
  7.2 42.0 %copy-start.13 = (f32[256,128]{1,0:T(8,128)S(1)}, f32[256,128]{1,0:T(8,128)}, u32[]{:S(2)}) copy-start(f32[256,128]{1,0:T(8,128)} %param.14) | copy-start | bytes 393220
  7.2 42.7 %copy-start.21 = (f32[16,128]{1,0:T(8,128)S(1)}, f32[16,128]{1,0:T(8,128)}, u32[]{:S(2)}) copy-start(f32[16,128]{1,0:T(8,128)} %param.12) | copy-start | bytes 24580
  7.2 152.9 %all-gather.3.cloned.1.call-start = ((), (), s32[]{:S(2)}) async-start(), calls=%async_computation.3 | async-start | bytes 8650752 | tf_op jit(solution)/shard_map/all_gather | solution.py:144
  12.7 66.9 %copy-start.8 = (f32[2,256,128]{2,1,0:T(8,128)}, f32[2,256,128]{2,1,0:T(8,128)S(1)}, u32[]{:S(2)}) copy-start(f32[2,256,128]{2,1,0:T(8,128)S(1)} %broadcast_select_fusion.3) | copy-start | bytes 786436
  12.7 12.6 %collective-permute-start.10 = (f32[512,128]{1,0:T(8,128)S(1)}, f32[512,128]{1,0:T(8,128)S(1)}, u32[]{:S(2)}, u32[]{:S(2)}) collective-permute-start(f32[512,128]{1,0:T(8,128)S(1)} %bitcast.90), channel_id=1, source_target_pairs={{0,16},{1,48},{2,80},{3,112},{4,0},{5,32},{6,64},{7,96},{8,24},{9,... | collective-permute-start | bytes 786440 | tf_op jit(solution)/shard_map/ppermute | solution.py:141
  26.0 211.7 %reduce-scatter.2.cloned.1.call-start = ((), (), s32[]{:S(2)}) async-start(), calls=%async_computation.2 | async-start | bytes 2359296 | tf_op jit(solution)/shard_map/reduce_scatter | solution.py:204
  28.0 68.2 %copy-start.18 = (f32[2,256,2,256]{3,2,1,0:T(2,128)S(1)}, f32[2,256,2,256]{3,2,1,0:T(2,128)}, u32[]{:S(2)}) copy-start(f32[2,256,2,256]{3,2,1,0:T(2,128)} %param.9) | copy-start | bytes 3145732
  28.0 25.2 %collective-permute-start = (f32[640,128]{1,0:T(8,128)S(1)}, f32[640,128]{1,0:T(8,128)S(1)}, u32[]{:S(2)}, u32[]{:S(2)}) collective-permute-start(f32[640,128]{1,0:T(8,128)S(1)} %pad_maximum_fusion.6), channel_id=1, source_target_pairs={{0,16},{1,96},{2,64},{3,32},{4,0},{5,112},{6,80},{7,48},{8,24},{9,... | collective-permute-start | bytes 983048 | tf_op jit(solution)/shard_map/ppermute | solution.py:142
  43.9 26.8 %collective-permute-start.1 = (f32[2,256,2,256]{3,2,1,0:T(2,128)}, f32[2,256,2,256]{3,2,1,0:T(2,128)S(1)}, u32[]{:S(2)}, u32[]{:S(2)}) collective-permute-start(f32[2,256,2,256]{3,2,1,0:T(2,128)} %param.9), channel_id=1, source_target_pairs={{0,8},{8,0},{1,9},{9,1},{2,10},{10,2},{3,11},{11,3},{4,12},{12,4},... | collective-permute-start | bytes 3145736 | tf_op jit(solution)/shard_map/ppermute | solution.py:143
  70.7 7.8 %collective-permute-start.12 = (f32[640,128]{1,0:T(8,128)S(1)}, f32[640,128]{1,0:T(8,128)S(1)}, u32[]{:S(2)}, u32[]{:S(2)}) collective-permute-start(f32[640,128]{1,0:T(8,128)S(1)} %collective-permute-done), channel_id=1, source_target_pairs={{0,32},{32,0},{1,33},{33,1},{2,34},{34,2},{3,35},{35,3},{4,36},{36... | collective-permute-start | bytes 983048 | tf_op jit(solution)/shard_map/ppermute | solution.py:149
  79.6 39.0 %collective-permute-start.13 = (f32[2,640,128]{2,1,0:T(8,128)}, f32[2,640,128]{2,1,0:T(8,128)}, u32[]{:S(2)}, u32[]{:S(2)}) collective-permute-start(f32[2,640,128]{2,1,0:T(8,128)} %get-tuple-element.46), channel_id=1, source_target_pairs={{0,64},{64,128},{128,192},{192,0},{1,65},{65,129},{129,193},{193,1... | collective-permute-start | bytes 1966088 | tf_op jit(solution)/shard_map/ppermute | solution.py:150
  90.0 43.9 %collective-permute-start.14 = (f32[2,640,128]{2,1,0:T(8,128)}, f32[2,640,128]{2,1,0:T(8,128)}, u32[]{:S(2)}, u32[]{:S(2)}) collective-permute-start(f32[2,640,128]{2,1,0:T(8,128)} %get-tuple-element.46), channel_id=1, source_target_pairs={{0,128},{64,192},{128,0},{192,64},{1,129},{65,193},{129,1},{193,65... | collective-permute-start | bytes 1966088 | tf_op jit(solution)/shard_map/ppermute | solution.py:150
  92.2 41.8 %collective-permute-start.15 = (f32[2,640,128]{2,1,0:T(8,128)}, f32[2,640,128]{2,1,0:T(8,128)}, u32[]{:S(2)}, u32[]{:S(2)}) collective-permute-start(f32[2,640,128]{2,1,0:T(8,128)} %get-tuple-element.46), channel_id=1, source_target_pairs={{0,192},{64,0},{128,64},{192,128},{1,193},{65,1},{129,65},{193,129... | collective-permute-start | bytes 1966088 | tf_op jit(solution)/shard_map/ppermute | solution.py:150
  92.5 9.2 %collective-permute-start.2 = (f32[528,128]{1,0:T(8,128)S(1)}, f32[528,128]{1,0:T(8,128)S(1)}, u32[]{:S(2)}, u32[]{:S(2)}) collective-permute-start(f32[528,128]{1,0:T(8,128)S(1)} %pad_maximum_fusion.7), channel_id=1, source_target_pairs={{0,1},{1,2},{2,3},{3,4},{4,5},{5,6},{6,7},{7,0},{8,9},{9,10},{10,1... | collective-permute-start | bytes 811016 | tf_op jit(solution)/shard_map/ppermute | solution.py:171
  98.2 10.8 %collective-permute-start.6 = (f32[528,128]{1,0:T(8,128)S(1)}, f32[528,128]{1,0:T(8,128)S(1)}, u32[]{:S(2)}, u32[]{:S(2)}) collective-permute-start(f32[528,128]{1,0:T(8,128)S(1)} %pad_maximum_fusion.7), channel_id=1, source_target_pairs={{0,7},{1,0},{2,1},{3,2},{4,3},{5,4},{6,5},{7,6},{8,15},{9,8},{10,9... | collective-permute-start | bytes 811016 | tf_op jit(solution)/shard_map/ppermute | solution.py:174
  101.7 9.1 %collective-permute-start.3 = (f32[528,128]{1,0:T(8,128)S(1)}, f32[528,128]{1,0:T(8,128)}, u32[]{:S(2)}, u32[]{:S(2)}) collective-permute-start(f32[528,128]{1,0:T(8,128)S(1)} %collective-permute-done.2), channel_id=1, source_target_pairs={{0,1},{1,2},{2,3},{3,4},{4,5},{5,6},{6,7},{7,0},{8,9},{9,10},{10,1... | collective-permute-start | bytes 811016 | tf_op jit(solution)/shard_map/ppermute | solution.py:171
  109.1 38.4 %collective-permute-start.9 = (f32[768,128]{1,0:T(8,128)}, f32[768,128]{1,0:T(8,128)S(1)}, u32[]{:S(2)}, u32[]{:S(2)}) collective-permute-start(f32[768,128]{1,0:T(8,128)} %pad_maximum_fusion.5), channel_id=1, source_target_pairs={{0,1},{1,0},{2,3},{3,2},{4,5},{5,4},{6,7},{7,6},{8,9},{9,8},{10,11... | collective-permute-start | bytes 1179656 | tf_op jit(solution)/shard_map/ppermute | solution.py:192
  110.9 28.8 %collective-permute-start.7 = (f32[528,128]{1,0:T(8,128)S(1)}, f32[528,128]{1,0:T(8,128)S(1)}, u32[]{:S(2)}, u32[]{:S(2)}) collective-permute-start(f32[528,128]{1,0:T(8,128)S(1)} %collective-permute-done.6), channel_id=1, source_target_pairs={{0,7},{1,0},{2,1},{3,2},{4,3},{5,4},{6,5},{7,6},{8,15},{9,8},{10,9... | collective-permute-start | bytes 811016 | tf_op jit(solution)/shard_map/ppermute | solution.py:174
  118.6 28.0 %collective-permute-start.4 = (f32[528,128]{1,0:T(8,128)}, f32[528,128]{1,0:T(8,128)S(1)}, u32[]{:S(2)}, u32[]{:S(2)}) collective-permute-start(f32[528,128]{1,0:T(8,128)} %collective-permute-done.3), channel_id=1, source_target_pairs={{0,1},{1,2},{2,3},{3,4},{4,5},{5,6},{6,7},{7,0},{8,9},{9,10},{10,1... | collective-permute-start | bytes 811016 | tf_op jit(solution)/shard_map/ppermute | solution.py:171
  137.9 30.3 %collective-permute-start.16 = (f32[4,2,640,128]{3,2,1,0:T(8,128)}, f32[4,2,640,128]{3,2,1,0:T(8,128)}, u32[]{:S(2)}, u32[]{:S(2)}) collective-permute-start(f32[4,2,640,128]{3,2,1,0:T(8,128)} %get-tuple-element.38), channel_id=1, source_target_pairs={{0,16},{16,0},{1,17},{17,1},{2,18},{18,2},{3,19},{19,3},{4,20},{20... | collective-permute-start | bytes 7864328 | tf_op jit(solution)/shard_map/ppermute | solution.py:151
  139.6 12.8 %collective-permute-start.8 = (f32[528,128]{1,0:T(8,128)S(1)}, f32[528,128]{1,0:T(8,128)S(1)}, u32[]{:S(2)}, u32[]{:S(2)}) collective-permute-start(f32[528,128]{1,0:T(8,128)S(1)} %collective-permute-done.7), channel_id=1, source_target_pairs={{0,7},{1,0},{2,1},{3,2},{4,3},{5,4},{6,5},{7,6},{8,15},{9,8},{10,9... | collective-permute-start | bytes 811016 | tf_op jit(solution)/shard_map/ppermute | solution.py:174
  146.6 9.5 %collective-permute-start.5 = (f32[528,128]{1,0:T(8,128)S(1)}, f32[528,128]{1,0:T(8,128)S(1)}, u32[]{:S(2)}, u32[]{:S(2)}) collective-permute-start(f32[528,128]{1,0:T(8,128)S(1)} %collective-permute-done.4), channel_id=1, source_target_pairs={{0,1},{1,2},{2,3},{3,4},{4,5},{5,6},{6,7},{7,0},{8,9},{9,10},{10,1... | collective-permute-start | bytes 811016 | tf_op jit(solution)/shard_map/ppermute | solution.py:171
  183.5 12.7 %collective-permute-start.17 = (f32[512,128]{1,0:T(8,128)S(1)}, f32[512,128]{1,0:T(8,128)S(1)}, u32[]{:S(2)}, u32[]{:S(2)}) collective-permute-start(f32[512,128]{1,0:T(8,128)S(1)} %get-tuple-element.44), channel_id=1, source_target_pairs={{0,1},{1,2},{2,3},{3,4},{4,5},{5,6},{6,7},{7,0},{8,9},{9,10},{10,1... | collective-permute-start | bytes 786440 | tf_op jit(solution)/shard_map/ppermute | solution.py:231
  183.6 13.6 %collective-permute-start.18 = (f32[512,128]{1,0:T(8,128)S(1)}, f32[512,128]{1,0:T(8,128)S(1)}, u32[]{:S(2)}, u32[]{:S(2)}) collective-permute-start(f32[512,128]{1,0:T(8,128)S(1)} %get-tuple-element.43), channel_id=1, source_target_pairs={{0,7},{1,0},{2,1},{3,2},{4,3},{5,4},{6,5},{7,6},{8,15},{9,8},{10,9... | collective-permute-start | bytes 786440 | tf_op jit(solution)/shard_map/ppermute | solution.py:232
  197.3 13.0 %collective-permute-start.22 = (f32[512,128]{1,0:T(8,128)S(1)}, f32[512,128]{1,0:T(8,128)S(1)}, u32[]{:S(2)}, u32[]{:S(2)}) collective-permute-start(f32[512,128]{1,0:T(8,128)S(1)} %bitcast_add_fusion.2), channel_id=1, source_target_pairs={{0,7},{1,0},{2,1},{3,2},{4,3},{5,4},{6,5},{7,6},{8,15},{9,8},{10,9... | collective-permute-start | bytes 786440 | tf_op jit(solution)/shard_map/ppermute | solution.py:235
  200.9 21.1 %collective-permute-start.11 = (f32[528,256]{1,0:T(8,128)}, f32[528,256]{1,0:T(8,128)}, u32[]{:S(2)}, u32[]{:S(2)}) collective-permute-start(f32[528,256]{1,0:T(8,128)} %get-tuple-element.26), channel_id=1, source_target_pairs={{0,8},{8,0},{1,9},{9,1},{2,10},{10,2},{3,11},{11,3},{4,12},{12,4},... | collective-permute-start | bytes 1622024 | tf_op jit(solution)/shard_map/ppermute | solution.py:239
  212.1 8.5 %collective-permute-start.19 = (f32[512,128]{1,0:T(8,128)}, f32[512,128]{1,0:T(8,128)}, u32[]{:S(2)}, u32[]{:S(2)}) collective-permute-start(f32[512,128]{1,0:T(8,128)} %get-tuple-element.40), channel_id=1, source_target_pairs={{0,1},{1,2},{2,3},{3,4},{4,5},{5,6},{6,7},{7,0},{8,9},{9,10},{10,1... | collective-permute-start | bytes 786440 | tf_op jit(solution)/shard_map/ppermute | solution.py:234
  221.7 6.7 %collective-permute-start.20 = (f32[512,128]{1,0:T(8,128)S(1)}, f32[512,128]{1,0:T(8,128)S(1)}, u32[]{:S(2)}, u32[]{:S(2)}) collective-permute-start(f32[512,128]{1,0:T(8,128)S(1)} %bitcast_add_fusion.4), channel_id=1, source_target_pairs={{0,1},{1,2},{2,3},{3,4},{4,5},{5,6},{6,7},{7,0},{8,9},{9,10},{10,1... | collective-permute-start | bytes 786440 | tf_op jit(solution)/shard_map/ppermute | solution.py:236
  222.1 7.0 %collective-permute-start.23 = (f32[512,128]{1,0:T(8,128)S(1)}, f32[512,128]{1,0:T(8,128)S(1)}, u32[]{:S(2)}, u32[]{:S(2)}) collective-permute-start(f32[512,128]{1,0:T(8,128)S(1)} %get-tuple-element.39), channel_id=1, source_target_pairs={{0,7},{1,0},{2,1},{3,2},{4,3},{5,4},{6,5},{7,6},{8,15},{9,8},{10,9... | collective-permute-start | bytes 786440 | tf_op jit(solution)/shard_map/ppermute | solution.py:237
  228.5 6.5 %collective-permute-start.21 = (f32[512,128]{1,0:T(8,128)S(1)}, f32[512,128]{1,0:T(8,128)S(1)}, u32[]{:S(2)}, u32[]{:S(2)}) collective-permute-start(f32[512,128]{1,0:T(8,128)S(1)} %bitcast_add_fusion.3), channel_id=1, source_target_pairs={{0,1},{1,2},{2,3},{3,4},{4,5},{5,6},{6,7},{7,0},{8,9},{9,10},{10,1... | collective-permute-start | bytes 786440 | tf_op jit(solution)/shard_map/ppermute | solution.py:238
  240.1 17.5 %all-to-all-start = ((f32[16,3,16,128]{3,2,1,0:T(8,128)}), f32[16,3,16,128]{3,2,1,0:T(8,128)S(1)}, u32[]{:S(2)}, u32[]{:S(2)}) async-start(f32[16,3,16,128]{3,2,1,0:T(8,128)} %copy.19), calls=%async_computation.1 | async-start | bytes 786432 | tf_op jit(solution)/shard_map/all_to_all | solution.py:252
  (18 other events, 270.5 us)
Sparse Core Ops, SparseCore 0:
  26.1 110.2 all-gather.2
  168.3 42.9 reduce-scatter.1

commit v5 on v1

v5 whole, which is shorter than its diff:
```python
import functools

import jax
import jax.numpy as jnp
from jax import lax
from jax.experimental import pallas as pl
from jax.experimental.pallas import tpu as pltpu
from jax.sharding import PartitionSpec as P

ROW_AXES = ("x", "y_lo", "core")
COL_AXES = ("y_hi", "z")
ALL_AXES = ROW_AXES + COL_AXES
exact = lax.Precision.HIGHEST


def split(a):
    hi = a.astype(jnp.bfloat16)
    return hi, (a - hi.astype(jnp.float32)).astype(jnp.bfloat16)


def dot3(a, b):
    f = functools.partial(jnp.dot, preferred_element_type=jnp.float32)
    return f(a[0], b[0]) + (f(a[0], b[1]) + f(a[1], b[0]))


def pair_kernel(sc_ref, gh_ref, gl_ref, a_ref, b_ref, out_ref):
    h = sc_ref[0]
    acc = None
    for k in range(2):
        half = h if k == 0 else 1 - h
        cols = jnp.concatenate([a_ref[half, 0, 0], b_ref[half, 0, 0]], axis=1)
        term = dot3((gh_ref[k], gl_ref[k]), split(cols))
        acc = term if acc is None else acc + term
    out_ref[0] = -acc[:, :128]
    out_ref[1] = -acc[:, 128:]


WHOLE_G = pl.BlockSpec((2, 512, 512), lambda i, sc: (0, 0, 0))
PARAMS = pltpu.CompilerParams(vmem_limit_bytes=40 * 2**20)


def slot_rows(first):
    def place(i, sc):
        code = sc[first + 2 * i]
        return (0, code // 4, code % 4, 0, 0)

    return pl.BlockSpec((2, 1, 1, 512, 128), place)


def product(scalars, g_hi, g_lo, gathered):
    return pl.pallas_call(
        pair_kernel,
        grid_spec=pltpu.PrefetchScalarGridSpec(
            num_scalar_prefetch=1,
            grid=(2,),
            in_specs=[WHOLE_G, WHOLE_G, slot_rows(1), slot_rows(2)],
            out_specs=pl.BlockSpec((2, 512, 128), lambda i, sc: (i, 0, 0)),
        ),
        out_shape=jax.ShapeDtypeStruct((4, 512, 128), jnp.float32),
        compiler_params=PARAMS,
        cost_estimate=pl.CostEstimate(
            flops=1_600_000_000, bytes_accessed=7_000_000, transcendentals=0
        ),
    )(scalars, g_hi, g_lo, gathered, gathered)


def chip_and_core(shift):
    up = (shift >= 1) & (shift <= 4)
    return (up * (4 - shift) + (1 - up) * (8 - shift)) % 4, 1 - up


def spread_pairs():
    pairs = []
    for i in range(256):
        row, col = divmod(i, 16)
        half, z, h, s = row // 8, row % 8, col // 8, col % 8
        chip, core = chip_and_core((z - s) % 8)
        pairs.append((i, (half * 8 + chip * 2 + int(core)) * 16 + h * 8 + z))
    return pairs


def ring(n, step):
    return [(i, (i + step) % n) for i in range(n)]


def local(g_top, l_one, struct_one, dinv_one, l_two, lp_two, parent_two, pos_two, dinv_two):
    row = lax.axis_index(ROW_AXES)
    h = lax.axis_index("y_hi")
    z = lax.axis_index("z")
    mine = h * 4 + z // 2
    parent = parent_two[mine]

    blocks = jnp.arange(2, dtype=jnp.int32) * 16 + row
    list_one = lax.dynamic_index_in_dim(struct_one, mine, 0, keepdims=False)
    list_parent = lax.dynamic_index_in_dim(struct_one, parent, 0, keepdims=False)
    places = lax.dynamic_index_in_dim(pos_two, mine, 0, keepdims=False)
    picked = jnp.any(places[:, None] == jnp.arange(16)[None, :], axis=0)
    keep_one = jnp.any(list_one[None, :] == blocks[:, None], axis=1)[:, None, None]
    keep_two = jnp.any((list_parent[None, :] == blocks[:, None]) & picked[None, :], axis=1)
    keep_two = keep_two[:, None, None]
    one = jnp.where(keep_one, l_one, 0.0).reshape(512, 128)
    two = jnp.where(keep_two, l_two, 0.0).reshape(512, 128)

    def gather(piece):
        rows = lax.all_gather(piece, ROW_AXES, axis=0, tiled=False)
        return rows.reshape(2, 2, 4, 512, 128)

    g_other = lax.ppermute(g_top, "y_hi", ring(2, 1))
    packed = jnp.concatenate([one, dinv_one])
    pieces = {0: packed}
    right = left = packed
    sent = one
    for d in range(1, 5):
        right = lax.ppermute(right, "z", ring(8, 1))
        if d < 4:
            left = lax.ppermute(left, "z", ring(8, -1))
        if d == 1:
            right, left, sent = lax.optimization_barrier((right, left, sent))
            near_one = lax.ppermute(sent, ALL_AXES, spread_pairs())
        if d == 4:
            right, left, near_one, g_other = lax.optimization_barrier(
                (right, left, near_one, g_other)
            )
        pieces[-d] = right
        if d < 4:
            pieces[d] = left
    gathered_one = gather(near_one)

    g = jnp.stack([g_top, g_other]).reshape(2, 512, 512)
    g_hi32 = lax.reduce_precision(g, 8, 7)
    g_hi = g_hi32.astype(jnp.bfloat16)
    g_lo = (g - g_hi32).astype(jnp.bfloat16)

    def fetch(super_index):
        parts = []
        for part in range(2):
            want = super_index % 4 * 2 + part
            total = jnp.zeros((528, 128), jnp.float32)
            for d, one_piece_here in pieces.items():
                total = jnp.where(want == (z + d) % 8, one_piece_here, total)
            parts.append(total)
        return jnp.concatenate(parts, axis=1)

    par_here = fetch(parent)
    par_there = fetch(parent_two[(1 - h) * 4 + z // 2])
    even = z % 2 == 0
    pair_up = lambda a, b: jnp.where(even, jnp.concatenate([a, b], 1), jnp.concatenate([b, a], 1))
    own_one = pair_up(one, jnp.where(even, pieces[1], pieces[-1])[:512])
    par_other = lax.ppermute(par_there, "y_hi", ring(2, 1))
    par = jnp.where(parent // 4 == h, par_here, par_other)
    folded = two - jnp.dot(par[:512], lp_two, precision=lax.Precision.HIGH)
    gathered_two = gather(lax.ppermute(folded, ALL_AXES, spread_pairs()))
    two_sent = jnp.concatenate([two, lp_two])
    two_next = lax.ppermute(two_sent, "z", [(i, i ^ 1) for i in range(8)])
    own_two = pair_up(two, two_next[:512])
    lp_own = pair_up(lp_two, two_next[512:])

    def multiply_and_sum(gathered, after):
        def part(first_pair, after):
            both = jnp.arange(2, dtype=jnp.int32)
            slots = (first_pair + both) % 4 * 2
            chip, core = chip_and_core((z - slots[:, None] - both[None, :]) % 8)
            codes = chip // 2 * 4 + chip % 2 * 2 + core
            scalars = jnp.concatenate([after[None], codes.reshape(4)]).astype(jnp.int32)
            return product(scalars, g_hi, g_lo, gathered)

        early = part((z + 4) // 2, after)
        after, early = lax.optimization_barrier((after, early))
        late = part((z + 4) // 2 + 2, after)

        def term(d):
            take = lambda i: early[i] if i < 4 else late[i - 4]
            return jnp.where(even, take((d - 4) % 8), take((d - 3) % 8))

        up = lax.ppermute(term(4), "z", ring(8, 1))
        down = lax.ppermute(term(-3), "z", ring(8, -1))
        up, down, late = lax.optimization_barrier((up, down, late))
        up = lax.ppermute(up + term(3), "z", ring(8, 1))
        down = lax.ppermute(down + term(-2), "z", ring(8, -1))
        up = lax.ppermute(up + term(2), "z", ring(8, 1))
        down = lax.ppermute(down + term(-1), "z", ring(8, -1))
        return lax.ppermute(up + term(1), "z", ring(8, 1)) + down + term(0)

    inv_one = multiply_and_sum(gathered_one, h)
    inv_one, own_one, own_two, lp_own, h_next = lax.optimization_barrier(
        (inv_one, own_one, own_two, lp_own, h)
    )
    inv_two = multiply_and_sum(gathered_two, h_next)
    panel_one = jnp.where(keep_one, inv_one.reshape(2, 256, 128), 0.0)
    panel_two = jnp.where(keep_two, inv_two.reshape(2, 256, 128), 0.0)

    dot_t = lambda a, b: lax.dot_general(a, b, (((0,), (0,)), ((), ())), precision=exact)
    scaled = jnp.dot(par[512:], lp_two, precision=exact)
    lp_slab = lax.dynamic_slice_in_dim(lp_own, row * 16, 16, 0)
    quad = dot_t(lp_slab, scaled)
    term_one = dot_t(own_one, inv_one)
    term_par = dot_t(par[:512], inv_two)
    term_two = quad - dot_t(own_two, inv_two) + dot_t(lp_own, term_par)
    terms = jnp.stack([term_one, term_par, term_two]).reshape(3, 16, 16, 128).transpose(1, 0, 2, 3)
    sums = jnp.sum(lax.all_to_all(terms, ROW_AXES, 0, 0), axis=0)
    diag_one = dinv_one - sums[0]
    parent_rows = -(sums[1] + scaled)
    diag_two = dinv_two + sums[2]
    return (panel_one, diag_one, panel_two, parent_rows, diag_two)


def solution(mesh):
    fine = jax.sharding.Mesh(mesh.devices.reshape(4, 2, 2, 2, 8), ALL_AXES)
    tall = P(None, ROW_AXES, COL_AXES)
    flat = P(ROW_AXES, COL_AXES)
    return jax.shard_map(
        local,
        mesh=fine,
        in_specs=(
            P(None, ROW_AXES, None, COL_AXES),
            tall,
            P(),
            flat,
            tall,
            P(None, COL_AXES),
            P(),
            P(),
            flat,
        ),
        out_specs=(tall, flat, tall, flat, flat),
        check_vma=False,
    )
```

time: 324 us -> 246 us (0.76)
  waiting for transfers between devices: 217 us -> 108 us
  starting transfers between devices: 41.7 us -> 70.9 us
  Pallas kernels: 18.2 us -> 11.7 us
  local copies, waits for them, and re-layouts: 11.5 us -> 14.8 us
    all_gather x1 -> x2, waiting for transfers between devices: 95.2 us -> 20.3 us  [gather(): rows = lax.all_gather(piece, ROW_AXES, axis=0, tiled=False)]
    ppermute x4, waiting for transfers between devices: 70.8 us -> 13.5 us  [local(): right = lax.ppermute(right, 'z', ring(8, 1))]
    ppermute x4 -> x18, waiting for transfers between devices: 18.7 us -> 67.5 us  [the longest x2 13 us: multiply_and_sum(): up = lax.ppermute(up + term(3), 'z', ring(8, 1))]
    ppermute x4 -> x18, starting transfers between devices: 12.1 us -> 42.4 us  [the longest x1 13.4 us: local(): gathered_two = gather(lax.ppermute(folded, ALL_AXES, spread_pairs()))]
    ppermute x1, waiting for transfers between devices: 24.1 us -> 0.01 us  [local(): g_other = lax.ppermute(g_top, 'y_hi', ring(2, 1))]
    ppermute x4, starting transfers between devices: 15.3 us -> 2.55 us  [local(): right = lax.ppermute(right, 'z', ring(8, 1))]
    pallas_call x1 -> x4, Pallas kernels: 18.2 us -> 11.7 us  [product(): pl.pallas_call(pair_kernel, grid_spec=pltpu.PrefetchScalarGridSpec(num_sc...]
    ppermute x3, starting transfers between devices: 3.53 us -> 9.38 us  [local(): left = lax.ppermute(left, 'z', ring(8, -1))]
  transfers between devices with their start and end apart: 15 -> 29, of which waited for: 11 -> 21; matrix products, arithmetic and copies ran while one was open for 5% -> 8% of each run, Pallas kernels for 0% -> 4%
where the time goes in v5:
time: 246 us
  waiting for transfers between devices  108 us (44%)
  starting transfers between devices  70.9 us (29%)
  between operations  20.6 us (8%)
  local copies, waits for them, and re-layouts  14.8 us (6%)
  other arithmetic  14 us (6%)
  Pallas kernels  11.7 us (5%)
  matrix products  5.27 us (2%)
    all_gather x2, waiting for transfers between devices, gather(): rows = lax.all_gather(piece, ROW_AXES, axis=0, tiled=False)  20.3 us
    all_to_all x1, starting transfers between devices, local(): sums = jnp.sum(lax.all_to_all(terms, ROW_AXES, 0, 0), axis=0)  13.5 us
    ppermute x4, waiting for transfers between devices, local(): right = lax.ppermute(right, 'z', ring(8, 1))  13.5 us
    ppermute x1, starting transfers between devices, local(): gathered_two = gather(lax.ppermute(folded, ALL_AXES, spread_pairs()))  13.4 us
    ppermute x2, waiting for transfers between devices, multiply_and_sum(): up = lax.ppermute(up + term(3), 'z', ring(8, 1))  13 us
    pallas_call x4, Pallas kernels, product(): pl.pallas_call(pair_kernel, grid_spec=pltpu.PrefetchScalarGridSpec(num_sc...  11.7 us
    ppermute x2, waiting for transfers between devices, multiply_and_sum(): return lax.ppermute(up + term(1), 'z', ring(8, 1)) + down + term(0)  10.6 us
    ppermute x3, starting transfers between devices, local(): left = lax.ppermute(left, 'z', ring(8, -1))  9.38 us
  transfers between devices with their start and end apart: 29, of which 21 were waited for; matrix products, arithmetic and copies ran while one was open for 8% of the time, Pallas kernels for 4%

profile of v5, /device:TPU:1, one launch (start us, length us, event | category | flops | bytes accessed | tf_op | source)
XLA Modules:
  0.0 245.5 jit_solution(15007549320189946056)
XLA Ops:
  15.9 4.0 %collective-permute-start.1 = (f32[528,128]{1,0:T(8,128)S(1)}, f32[528,128]{1,0:T(8,128)S(1)}, u32[]{:S(2)}, u32[]{:S(2)}) collective-permute-start(f32[528,128]{1,0:T(8,128)S(1)} %pad_maximum_fusion.2), channel_id=1, source_target_pairs={{0,7},{1,0},{2,1},{3,2},{4,3},{5,4},{6,5},{7,6},{8,15},{9,8},{10,9... | collective-permute-start | bytes 811016 | tf_op jit(solution)/shard_map/ppermute | solution.py:116
  20.0 2.9 %collective-permute-start.8 = (f32[2,256,2,256]{3,2,1,0:T(2,128)}, f32[2,256,2,256]{3,2,1,0:T(2,128)}, u32[]{:S(2)}, u32[]{:S(2)}) collective-permute-start(f32[2,256,2,256]{3,2,1,0:T(2,128)} %param.9), channel_id=1, source_target_pairs={{0,8},{8,0},{1,9},{9,1},{2,10},{10,2},{3,11},{11,3},{4,12},{12,4},... | collective-permute-start | bytes 3145736 | tf_op jit(solution)/shard_map/ppermute | solution.py:108
  22.9 3.3 %collective-permute-done = f32[528,128]{1,0:T(8,128)S(1)} collective-permute-done((f32[528,128]{1,0:T(8,128)S(1)}, f32[528,128]{1,0:T(8,128)S(1)}, u32[]{:S(2)}, u32[]{:S(2)}) %collective-permute-start) | collective-permute-done | bytes 270368 | tf_op jit(solution)/shard_map/ppermute | solution.py:114
  26.2 2.7 %collective-permute-start.5 = (f32[528,128]{1,0:T(8,128)S(1)}, f32[528,128]{1,0:T(8,128)S(1)}, u32[]{:S(2)}, u32[]{:S(2)}) collective-permute-start(f32[528,128]{1,0:T(8,128)S(1)} %collective-permute-done.1), channel_id=1, source_target_pairs={{0,7},{1,0},{2,1},{3,2},{4,3},{5,4},{6,5},{7,6},{8,15},{9,8},{10,9... | collective-permute-start | bytes 811016 | tf_op jit(solution)/shard_map/ppermute | solution.py:116
  28.9 5.5 %collective-permute-done.2 = f32[528,128]{1,0:T(8,128)S(1)} collective-permute-done((f32[528,128]{1,0:T(8,128)S(1)}, f32[528,128]{1,0:T(8,128)S(1)}, u32[]{:S(2)}, u32[]{:S(2)}) %collective-permute-start.2) | collective-permute-done | bytes 270368 | tf_op jit(solution)/shard_map/ppermute | solution.py:114
  34.4 2.7 %collective-permute-start.6 = (f32[528,128]{1,0:T(8,128)S(1)}, f32[528,128]{1,0:T(8,128)S(1)}, u32[]{:S(2)}, u32[]{:S(2)}) collective-permute-start(f32[528,128]{1,0:T(8,128)S(1)} %collective-permute-done.5), channel_id=1, source_target_pairs={{0,7},{1,0},{2,1},{3,2},{4,3},{5,4},{6,5},{7,6},{8,15},{9,8},{10,9... | collective-permute-start | bytes 811016 | tf_op jit(solution)/shard_map/ppermute | solution.py:116
  37.1 4.7 %collective-permute-done.3 = f32[528,128]{1,0:T(8,128)S(1)} collective-permute-done((f32[528,128]{1,0:T(8,128)S(1)}, f32[528,128]{1,0:T(8,128)S(1)}, u32[]{:S(2)}, u32[]{:S(2)}) %collective-permute-start.3) | collective-permute-done | bytes 270368 | tf_op jit(solution)/shard_map/ppermute | solution.py:114
  41.7 6.0 %collective-permute-start.7 = (f32[512,128]{1,0:T(8,128)S(1)}, f32[512,128]{1,0:T(8,128)S(1)}, u32[]{:S(2)}, u32[]{:S(2)}) collective-permute-start(f32[512,128]{1,0:T(8,128)S(1)} %bitcast.94), channel_id=1, source_target_pairs={{0,16},{1,48},{2,80},{3,112},{4,0},{5,32},{6,64},{7,96},{8,24},{9,... | collective-permute-start | bytes 786440 | tf_op jit(solution)/shard_map/ppermute | solution.py:119
  47.7 6.2 %collective-permute-done.7 = f32[512,128]{1,0:T(8,128)S(1)} collective-permute-done((f32[512,128]{1,0:T(8,128)S(1)}, f32[512,128]{1,0:T(8,128)S(1)}, u32[]{:S(2)}, u32[]{:S(2)}) %collective-permute-start.7) | collective-permute-done | bytes 262176 | tf_op jit(solution)/shard_map/ppermute | solution.py:119
  60.2 2.7 %collective-permute-start.17 = (f32[528,256]{1,0:T(8,128)S(1)}, f32[528,256]{1,0:T(8,128)S(1)}, u32[]{:S(2)}, u32[]{:S(2)}) collective-permute-start(f32[528,256]{1,0:T(8,128)S(1)} %pad_maximum_fusion), channel_id=1, source_target_pairs={{0,8},{8,0},{1,9},{9,1},{2,10},{10,2},{3,11},{11,3},{4,12},{12,4},... | collective-permute-start | bytes 1622024 | tf_op jit(solution)/shard_map/ppermute | solution.py:149
  63.2 6.8 %collective-permute-done.17 = f32[528,256]{1,0:T(8,128)S(1)} collective-permute-done((f32[528,256]{1,0:T(8,128)S(1)}, f32[528,256]{1,0:T(8,128)S(1)}, u32[]{:S(2)}, u32[]{:S(2)}) %collective-permute-start.17) | collective-permute-done | bytes 540704 | tf_op jit(solution)/shard_map/ppermute | solution.py:149
  70.5 13.4 %collective-permute-start.18 = (f32[512,128]{1,0:T(8,128)S(1)}, f32[512,128]{1,0:T(8,128)S(1)}, u32[]{:S(2)}, u32[]{:S(2)}) collective-permute-start(f32[512,128]{1,0:T(8,128)S(1)} %convolution_subtract_fusion), channel_id=1, source_target_pairs={{0,16},{1,48},{2,80},{3,112},{4,0},{5,32},{6,64},{7,96},{8,24},{9,... | collective-permute-start | bytes 786440 | tf_op jit(solution)/shard_map/ppermute | solution.py:152
  83.9 3.3 %collective-permute-done.18 = f32[512,128]{1,0:T(8,128)S(1)} collective-permute-done((f32[512,128]{1,0:T(8,128)S(1)}, f32[512,128]{1,0:T(8,128)S(1)}, u32[]{:S(2)}, u32[]{:S(2)}) %collective-permute-start.18) | collective-permute-done | bytes 262176 | tf_op jit(solution)/shard_map/ppermute | solution.py:152
  97.1 20.3 %all-gather.5.cloned.1.call-done = f32[8192,128]{1,0:T(8,128)} async-done(((f32[512,128]{1,0:T(8,128)}), f32[8192,128]{1,0:T(8,128)}) %all-gather.5.cloned.1.call-update) | async-done | bytes 4194320 | tf_op jit(solution)/shard_map/all_gather | solution.py:105
  119.6 2.9 %shard_map.128 = f32[4,512,128]{2,1,0:T(8,128)S(1)} custom-call(s32[5]{0:T(128)S(1)} %pad_add_fusion.sc_ref, bf16[2,512,512]{2,1,0:T(8,128)(2,1)S(1)} %get-tuple-element.54.gh_ref, bf16[2,512,512]{2,1,0:T(8,128)(2,1)S(1)} %get-tuple-element.53.gl_ref, f32[2,2,4,512,128]{4,3,2,1,0:T(8,128)S(1)} %bitcast.85, f32[2,2,4,512,128]{4,3,2,1,0:T(8,128)S(1)} %bitcast.86), custom_call_target="tpu_custom_call" | custom-call | flops 1600000000 | bytes 7000000 | tf_op jit(solution)/shard_map/pallas_call | solution.py:51
  123.4 4.3 %collective-permute-start.10 = (f32[512,128]{1,0:T(8,128)S(1)}, f32[512,128]{1,0:T(8,128)S(1)}, u32[]{:S(2)}, u32[]{:S(2)}) collective-permute-start(f32[512,128]{1,0:T(8,128)S(1)} %get-tuple-element.57), channel_id=1, source_target_pairs={{0,7},{1,0},{2,1},{3,2},{4,3},{5,4},{6,5},{7,6},{8,15},{9,8},{10,9... | collective-permute-start | bytes 786440 | tf_op jit(solution)/shard_map/ppermute | solution.py:176
  127.7 2.9 %shard_map.129 = f32[4,512,128]{2,1,0:T(8,128)S(1)} custom-call(s32[5]{0:T(128)S(1)} %pad_add_fusion.1.sc_ref, bf16[2,512,512]{2,1,0:T(8,128)(2,1)S(1)} %get-tuple-element.54.gh_ref, bf16[2,512,512]{2,1,0:T(8,128)(2,1)S(1)} %get-tuple-element.53.gl_ref, f32[2,2,4,512,128]{4,3,2,1,0:T(8,128)S(1)} %bitcast.87, f32[2,2,4,512,128]{4,3,2,1,0:T(8,128)S(1)} %bitcast.88), custom_call_target="tpu_custom_call" | custom-call | flops 1600000000 | bytes 7000000 | tf_op jit(solution)/shard_map/pallas_call | solution.py:51
  130.7 3.4 %collective-permute-done.9 = f32[512,128]{1,0:T(8,128)S(1)} collective-permute-done((f32[512,128]{1,0:T(8,128)S(1)}, f32[512,128]{1,0:T(8,128)S(1)}, u32[]{:S(2)}, u32[]{:S(2)}) %collective-permute-start.9) | collective-permute-done | bytes 262176 | tf_op jit(solution)/shard_map/ppermute | solution.py:175
  136.6 4.6 %collective-permute-done.14 = f32[512,128]{1,0:T(8,128)S(1)} collective-permute-done((f32[512,128]{1,0:T(8,128)S(1)}, f32[512,128]{1,0:T(8,128)S(1)}, u32[]{:S(2)}, u32[]{:S(2)}) %collective-permute-start.14) | collective-permute-done | bytes 262176 | tf_op jit(solution)/shard_map/ppermute | solution.py:179
  142.0 7.4 %collective-permute-done.11 = f32[512,128]{1,0:T(8,128)S(1)} collective-permute-done((f32[512,128]{1,0:T(8,128)S(1)}, f32[512,128]{1,0:T(8,128)S(1)}, u32[]{:S(2)}, u32[]{:S(2)}) %collective-permute-start.11) | collective-permute-done | bytes 262176 | tf_op jit(solution)/shard_map/ppermute | solution.py:178
  152.5 3.5 %collective-permute-done.12 = f32[512,128]{1,0:T(8,128)S(1)} collective-permute-done((f32[512,128]{1,0:T(8,128)S(1)}, f32[512,128]{1,0:T(8,128)S(1)}, u32[]{:S(2)}, u32[]{:S(2)}) %collective-permute-start.12) | collective-permute-done | bytes 262176 | tf_op jit(solution)/shard_map/ppermute | solution.py:180
  156.9 4.3 %collective-permute-done.16 = f32[768,128]{1,0:T(8,128)S(1)} collective-permute-done((f32[768,128]{1,0:T(8,128)S(1)}, f32[768,128]{1,0:T(8,128)S(1)}, u32[]{:S(2)}, u32[]{:S(2)}) %collective-permute-start.16) | collective-permute-done | bytes 393248 | tf_op jit(solution)/shard_map/ppermute | solution.py:154
  163.2 3.6 %collective-permute-done.13 = f32[512,128]{1,0:T(8,128)S(1)} collective-permute-done((f32[512,128]{1,0:T(8,128)S(1)}, f32[512,128]{1,0:T(8,128)S(1)}, u32[]{:S(2)}, u32[]{:S(2)}) %collective-permute-start.13) | collective-permute-done | bytes 262176 | tf_op jit(solution)/shard_map/ppermute | solution.py:182
  169.1 2.9 %shard_map.130 = f32[4,512,128]{2,1,0:T(8,128)S(1)} custom-call(s32[5]{0:T(128)S(1)} %pad_add_fusion.2.sc_ref, bf16[2,512,512]{2,1,0:T(8,128)(2,1)S(1)} %get-tuple-element.54.gh_ref, bf16[2,512,512]{2,1,0:T(8,128)(2,1)S(1)} %get-tuple-element.53.gl_ref, f32[2,2,4,512,128]{4,3,2,1,0:T(8,128)S(1)} %bitcast.89, f32[2,2,4,512,128]{4,3,2,1,0:T(8,128)S(1)} %bitcast.90), custom_call_target="tpu_custom_call" | custom-call | flops 1600000000 | bytes 7000000 | tf_op jit(solution)/shard_map/pallas_call | solution.py:51
  175.4 2.9 %shard_map.131 = f32[4,512,128]{2,1,0:T(8,128)S(1)} custom-call(s32[5]{0:T(128)S(1)} %pad_add_fusion.3.sc_ref, bf16[2,512,512]{2,1,0:T(8,128)(2,1)S(1)} %get-tuple-element.54.gh_ref, bf16[2,512,512]{2,1,0:T(8,128)(2,1)S(1)} %get-tuple-element.53.gl_ref, f32[2,2,4,512,128]{4,3,2,1,0:T(8,128)S(1)} %bitcast.91, f32[2,2,4,512,128]{4,3,2,1,0:T(8,128)S(1)} %bitcast.92), custom_call_target="tpu_custom_call" | custom-call | flops 1600000000 | bytes 7000000 | tf_op jit(solution)/shard_map/pallas_call | solution.py:51
  181.8 4.6 %collective-permute-done.24 = f32[512,128]{1,0:T(8,128)S(1)} collective-permute-done((f32[512,128]{1,0:T(8,128)S(1)}, f32[512,128]{1,0:T(8,128)S(1)}, u32[]{:S(2)}, u32[]{:S(2)}) %collective-permute-start.24) | collective-permute-done | bytes 262176 | tf_op jit(solution)/shard_map/ppermute | solution.py:179
  187.4 5.6 %collective-permute-done.21 = f32[512,128]{1,0:T(8,128)S(1)} collective-permute-done((f32[512,128]{1,0:T(8,128)S(1)}, f32[512,128]{1,0:T(8,128)S(1)}, u32[]{:S(2)}, u32[]{:S(2)}) %collective-permute-start.21) | collective-permute-done | bytes 262176 | tf_op jit(solution)/shard_map/ppermute | solution.py:178
  193.9 2.7 %collective-permute-start.25 = (f32[512,128]{1,0:T(8,128)S(1)}, f32[512,128]{1,0:T(8,128)S(1)}, u32[]{:S(2)}, u32[]{:S(2)}) collective-permute-start(f32[512,128]{1,0:T(8,128)S(1)} %get-tuple-element.49), channel_id=1, source_target_pairs={{0,7},{1,0},{2,1},{3,2},{4,3},{5,4},{6,5},{7,6},{8,15},{9,8},{10,9... | collective-permute-start | bytes 786440 | tf_op jit(solution)/shard_map/ppermute | solution.py:181
  196.7 5.5 %collective-permute-done.22 = f32[512,128]{1,0:T(8,128)} collective-permute-done((f32[512,128]{1,0:T(8,128)}, f32[512,128]{1,0:T(8,128)}, u32[]{:S(2)}, u32[]{:S(2)}) %collective-permute-start.22) | collective-permute-done | bytes 262176 | tf_op jit(solution)/shard_map/ppermute | solution.py:180
  205.4 7.0 %collective-permute-done.23 = f32[512,128]{1,0:T(8,128)S(1)} collective-permute-done((f32[512,128]{1,0:T(8,128)S(1)}, f32[512,128]{1,0:T(8,128)S(1)}, u32[]{:S(2)}, u32[]{:S(2)}) %collective-permute-start.23) | collective-permute-done | bytes 262176 | tf_op jit(solution)/shard_map/ppermute | solution.py:182
  216.0 13.5 %all-to-all-start = ((f32[16,3,16,128]{3,2,1,0:T(8,128)}), f32[16,3,16,128]{3,2,1,0:T(8,128)S(1)}, u32[]{:S(2)}, u32[]{:S(2)}) async-start(f32[16,3,16,128]{3,2,1,0:T(8,128)} %maximum_bitcast_fusion), calls=%async_computation | async-start | bytes 786432 | tf_op jit(solution)/shard_map/all_to_all | solution.py:200
  231.0 7.0 %all-to-all-done = f32[16,3,16,128]{3,2,1,0:T(8,128)S(1)} async-done(((f32[16,3,16,128]{3,2,1,0:T(8,128)}), f32[16,3,16,128]{3,2,1,0:T(8,128)S(1)}, u32[]{:S(2)}, u32[]{:S(2)}) %all-to-all-start) | async-done | bytes 393248 | tf_op jit(solution)/shard_map/all_to_all | solution.py:200
  (136 shorter events, 51.8 us)
Async XLA Ops:
  7.2 52.7 %copy-start.11 = (f32[16,128]{1,0:T(8,128)S(1)}, f32[16,128]{1,0:T(8,128)}, u32[]{:S(2)}) copy-start(f32[16,128]{1,0:T(8,128)} %param.12) | copy-start | bytes 24580
  7.2 110.2 %all-gather.5.cloned.1.call-start = ((), (), s32[]{:S(2)}) async-start(), calls=%async_computation.1 | async-start | bytes 4456448 | tf_op jit(solution)/shard_map/all_gather | solution.py:105
  13.4 12.8 %collective-permute-start = (f32[528,128]{1,0:T(8,128)S(1)}, f32[528,128]{1,0:T(8,128)S(1)}, u32[]{:S(2)}, u32[]{:S(2)}) collective-permute-start(f32[528,128]{1,0:T(8,128)S(1)} %pad_maximum_fusion.2), channel_id=1, source_target_pairs={{0,1},{1,2},{2,3},{3,4},{4,5},{5,6},{6,7},{7,0},{8,9},{9,10},{10,1... | collective-permute-start | bytes 811016 | tf_op jit(solution)/shard_map/ppermute | solution.py:114
  15.9 10.3 %collective-permute-start.1 = (f32[528,128]{1,0:T(8,128)S(1)}, f32[528,128]{1,0:T(8,128)S(1)}, u32[]{:S(2)}, u32[]{:S(2)}) collective-permute-start(f32[528,128]{1,0:T(8,128)S(1)} %pad_maximum_fusion.2), channel_id=1, source_target_pairs={{0,7},{1,0},{2,1},{3,2},{4,3},{5,4},{6,5},{7,6},{8,15},{9,8},{10,9... | collective-permute-start | bytes 811016 | tf_op jit(solution)/shard_map/ppermute | solution.py:116
  20.0 34.0 %collective-permute-start.8 = (f32[2,256,2,256]{3,2,1,0:T(2,128)}, f32[2,256,2,256]{3,2,1,0:T(2,128)}, u32[]{:S(2)}, u32[]{:S(2)}) collective-permute-start(f32[2,256,2,256]{3,2,1,0:T(2,128)} %param.9), channel_id=1, source_target_pairs={{0,8},{8,0},{1,9},{9,1},{2,10},{10,2},{3,11},{11,3},{4,12},{12,4},... | collective-permute-start | bytes 3145736 | tf_op jit(solution)/shard_map/ppermute | solution.py:108
  26.2 8.2 %collective-permute-start.2 = (f32[528,128]{1,0:T(8,128)S(1)}, f32[528,128]{1,0:T(8,128)S(1)}, u32[]{:S(2)}, u32[]{:S(2)}) collective-permute-start(f32[528,128]{1,0:T(8,128)S(1)} %collective-permute-done), channel_id=1, source_target_pairs={{0,1},{1,2},{2,3},{3,4},{4,5},{5,6},{6,7},{7,0},{8,9},{9,10},{10,1... | collective-permute-start | bytes 811016 | tf_op jit(solution)/shard_map/ppermute | solution.py:114
  26.2 8.2 %collective-permute-start.5 = (f32[528,128]{1,0:T(8,128)S(1)}, f32[528,128]{1,0:T(8,128)S(1)}, u32[]{:S(2)}, u32[]{:S(2)}) collective-permute-start(f32[528,128]{1,0:T(8,128)S(1)} %collective-permute-done.1), channel_id=1, source_target_pairs={{0,7},{1,0},{2,1},{3,2},{4,3},{5,4},{6,5},{7,6},{8,15},{9,8},{10,9... | collective-permute-start | bytes 811016 | tf_op jit(solution)/shard_map/ppermute | solution.py:116
  34.4 7.3 %collective-permute-start.3 = (f32[528,128]{1,0:T(8,128)S(1)}, f32[528,128]{1,0:T(8,128)S(1)}, u32[]{:S(2)}, u32[]{:S(2)}) collective-permute-start(f32[528,128]{1,0:T(8,128)S(1)} %collective-permute-done.2), channel_id=1, source_target_pairs={{0,1},{1,2},{2,3},{3,4},{4,5},{5,6},{6,7},{7,0},{8,9},{9,10},{10,1... | collective-permute-start | bytes 811016 | tf_op jit(solution)/shard_map/ppermute | solution.py:114
  34.4 19.6 %collective-permute-start.6 = (f32[528,128]{1,0:T(8,128)S(1)}, f32[528,128]{1,0:T(8,128)S(1)}, u32[]{:S(2)}, u32[]{:S(2)}) collective-permute-start(f32[528,128]{1,0:T(8,128)S(1)} %collective-permute-done.5), channel_id=1, source_target_pairs={{0,7},{1,0},{2,1},{3,2},{4,3},{5,4},{6,5},{7,6},{8,15},{9,8},{10,9... | collective-permute-start | bytes 811016 | tf_op jit(solution)/shard_map/ppermute | solution.py:116
  41.7 12.2 %collective-permute-start.4 = (f32[528,128]{1,0:T(8,128)S(1)}, f32[528,128]{1,0:T(8,128)S(1)}, u32[]{:S(2)}, u32[]{:S(2)}) collective-permute-start(f32[528,128]{1,0:T(8,128)S(1)} %collective-permute-done.3), channel_id=1, source_target_pairs={{0,1},{1,2},{2,3},{3,4},{4,5},{5,6},{6,7},{7,0},{8,9},{9,10},{10,1... | collective-permute-start | bytes 811016 | tf_op jit(solution)/shard_map/ppermute | solution.py:114
  41.7 12.2 %collective-permute-start.7 = (f32[512,128]{1,0:T(8,128)S(1)}, f32[512,128]{1,0:T(8,128)S(1)}, u32[]{:S(2)}, u32[]{:S(2)}) collective-permute-start(f32[512,128]{1,0:T(8,128)S(1)} %bitcast.94), channel_id=1, source_target_pairs={{0,16},{1,48},{2,80},{3,112},{4,0},{5,32},{6,64},{7,96},{8,24},{9,... | collective-permute-start | bytes 786440 | tf_op jit(solution)/shard_map/ppermute | solution.py:119
  54.7 112.2 %all-gather.7.cloned.1.call-start = ((), (), s32[]{:S(2)}) async-start(), calls=%async_computation.2 | async-start | bytes 4456448 | tf_op jit(solution)/shard_map/all_gather | solution.py:105
  60.2 9.8 %collective-permute-start.17 = (f32[528,256]{1,0:T(8,128)S(1)}, f32[528,256]{1,0:T(8,128)S(1)}, u32[]{:S(2)}, u32[]{:S(2)}) collective-permute-start(f32[528,256]{1,0:T(8,128)S(1)} %pad_maximum_fusion), channel_id=1, source_target_pairs={{0,8},{8,0},{1,9},{9,1},{2,10},{10,2},{3,11},{11,3},{4,12},{12,4},... | collective-permute-start | bytes 1622024 | tf_op jit(solution)/shard_map/ppermute | solution.py:149
  70.5 16.7 %collective-permute-start.18 = (f32[512,128]{1,0:T(8,128)S(1)}, f32[512,128]{1,0:T(8,128)S(1)}, u32[]{:S(2)}, u32[]{:S(2)}) collective-permute-start(f32[512,128]{1,0:T(8,128)S(1)} %convolution_subtract_fusion), channel_id=1, source_target_pairs={{0,16},{1,48},{2,80},{3,112},{4,0},{5,32},{6,64},{7,96},{8,24},{9,... | collective-permute-start | bytes 786440 | tf_op jit(solution)/shard_map/ppermute | solution.py:152
  92.0 35.6 %copy-start.17 = (s32[4]{0:T(128)}, s32[4]{0:T(128)S(1)}, u32[]{:S(2)}) copy-start(s32[4]{0:T(128)S(1)} %fusion.26) | copy-start | bytes 52
  122.6 11.5 %collective-permute-start.9 = (f32[512,128]{1,0:T(8,128)S(1)}, f32[512,128]{1,0:T(8,128)S(1)}, u32[]{:S(2)}, u32[]{:S(2)}) collective-permute-start(f32[512,128]{1,0:T(8,128)S(1)} %get-tuple-element.58), channel_id=1, source_target_pairs={{0,1},{1,2},{2,3},{3,4},{4,5},{5,6},{6,7},{7,0},{8,9},{9,10},{10,1... | collective-permute-start | bytes 786440 | tf_op jit(solution)/shard_map/ppermute | solution.py:175
  123.4 10.7 %collective-permute-start.10 = (f32[512,128]{1,0:T(8,128)S(1)}, f32[512,128]{1,0:T(8,128)S(1)}, u32[]{:S(2)}, u32[]{:S(2)}) collective-permute-start(f32[512,128]{1,0:T(8,128)S(1)} %get-tuple-element.57), channel_id=1, source_target_pairs={{0,7},{1,0},{2,1},{3,2},{4,3},{5,4},{6,5},{7,6},{8,15},{9,8},{10,9... | collective-permute-start | bytes 786440 | tf_op jit(solution)/shard_map/ppermute | solution.py:176
  134.1 7.2 %collective-permute-start.14 = (f32[512,128]{1,0:T(8,128)S(1)}, f32[512,128]{1,0:T(8,128)S(1)}, u32[]{:S(2)}, u32[]{:S(2)}) collective-permute-start(f32[512,128]{1,0:T(8,128)S(1)} %bitcast_add_fusion.8), channel_id=1, source_target_pairs={{0,7},{1,0},{2,1},{3,2},{4,3},{5,4},{6,5},{7,6},{8,15},{9,8},{10,9... | collective-permute-start | bytes 786440 | tf_op jit(solution)/shard_map/ppermute | solution.py:179
  141.4 8.0 %collective-permute-start.11 = (f32[512,128]{1,0:T(8,128)S(1)}, f32[512,128]{1,0:T(8,128)S(1)}, u32[]{:S(2)}, u32[]{:S(2)}) collective-permute-start(f32[512,128]{1,0:T(8,128)S(1)} %get-tuple-element.52), channel_id=1, source_target_pairs={{0,1},{1,2},{2,3},{3,4},{4,5},{5,6},{6,7},{7,0},{8,9},{9,10},{10,1... | collective-permute-start | bytes 786440 | tf_op jit(solution)/shard_map/ppermute | solution.py:178
  149.4 6.5 %collective-permute-start.12 = (f32[512,128]{1,0:T(8,128)S(1)}, f32[512,128]{1,0:T(8,128)S(1)}, u32[]{:S(2)}, u32[]{:S(2)}) collective-permute-start(f32[512,128]{1,0:T(8,128)S(1)} %bitcast_add_fusion.10), channel_id=1, source_target_pairs={{0,1},{1,2},{2,3},{3,4},{4,5},{5,6},{6,7},{7,0},{8,9},{9,10},{10,1... | collective-permute-start | bytes 786440 | tf_op jit(solution)/shard_map/ppermute | solution.py:180
  149.5 11.6 %collective-permute-start.16 = (f32[768,128]{1,0:T(8,128)S(1)}, f32[768,128]{1,0:T(8,128)S(1)}, u32[]{:S(2)}, u32[]{:S(2)}) collective-permute-start(f32[768,128]{1,0:T(8,128)S(1)} %pad_maximum_fusion.1), channel_id=1, source_target_pairs={{0,1},{1,0},{2,3},{3,2},{4,5},{5,4},{6,7},{7,6},{8,9},{9,8},{10,11... | collective-permute-start | bytes 1179656 | tf_op jit(solution)/shard_map/ppermute | solution.py:154
  150.0 13.2 %collective-permute-start.15 = (f32[512,128]{1,0:T(8,128)S(1)}, f32[512,128]{1,0:T(8,128)S(1)}, u32[]{:S(2)}, u32[]{:S(2)}) collective-permute-start(f32[512,128]{1,0:T(8,128)S(1)} %get-tuple-element.51), channel_id=1, source_target_pairs={{0,7},{1,0},{2,1},{3,2},{4,3},{5,4},{6,5},{7,6},{8,15},{9,8},{10,9... | collective-permute-start | bytes 786440 | tf_op jit(solution)/shard_map/ppermute | solution.py:181
  156.0 10.8 %collective-permute-start.13 = (f32[512,128]{1,0:T(8,128)S(1)}, f32[512,128]{1,0:T(8,128)S(1)}, u32[]{:S(2)}, u32[]{:S(2)}) collective-permute-start(f32[512,128]{1,0:T(8,128)S(1)} %bitcast_add_fusion.9), channel_id=1, source_target_pairs={{0,1},{1,2},{2,3},{3,4},{4,5},{5,6},{6,7},{7,0},{8,9},{9,10},{10,1... | collective-permute-start | bytes 786440 | tf_op jit(solution)/shard_map/ppermute | solution.py:182
  172.1 6.9 %collective-permute-start.19 = (f32[512,128]{1,0:T(8,128)S(1)}, f32[512,128]{1,0:T(8,128)S(1)}, u32[]{:S(2)}, u32[]{:S(2)}) collective-permute-start(f32[512,128]{1,0:T(8,128)S(1)} %get-tuple-element.56), channel_id=1, source_target_pairs={{0,1},{1,2},{2,3},{3,4},{4,5},{5,6},{6,7},{7,0},{8,9},{9,10},{10,1... | collective-permute-start | bytes 786440 | tf_op jit(solution)/shard_map/ppermute | solution.py:175
  174.4 5.2 %collective-permute-start.20 = (f32[512,128]{1,0:T(8,128)S(1)}, f32[512,128]{1,0:T(8,128)S(1)}, u32[]{:S(2)}, u32[]{:S(2)}) collective-permute-start(f32[512,128]{1,0:T(8,128)S(1)} %get-tuple-element.55), channel_id=1, source_target_pairs={{0,7},{1,0},{2,1},{3,2},{4,3},{5,4},{6,5},{7,6},{8,15},{9,8},{10,9... | collective-permute-start | bytes 786440 | tf_op jit(solution)/shard_map/ppermute | solution.py:176
  179.6 24.8 %copy-start.9 = (f32[512,256]{1,0:T(8,128)S(1)}, f32[512,256]{1,0:T(8,128)}, u32[]{:S(2)}) copy-start(f32[512,256]{1,0:T(8,128)} %maximum_select_fusion.1) | copy-start | bytes 1572868
  179.6 6.8 %collective-permute-start.24 = (f32[512,128]{1,0:T(8,128)S(1)}, f32[512,128]{1,0:T(8,128)S(1)}, u32[]{:S(2)}, u32[]{:S(2)}) collective-permute-start(f32[512,128]{1,0:T(8,128)S(1)} %bitcast_add_fusion.2), channel_id=1, source_target_pairs={{0,7},{1,0},{2,1},{3,2},{4,3},{5,4},{6,5},{7,6},{8,15},{9,8},{10,9... | collective-permute-start | bytes 786440 | tf_op jit(solution)/shard_map/ppermute | solution.py:179
  186.5 6.5 %collective-permute-start.21 = (f32[512,128]{1,0:T(8,128)S(1)}, f32[512,128]{1,0:T(8,128)S(1)}, u32[]{:S(2)}, u32[]{:S(2)}) collective-permute-start(f32[512,128]{1,0:T(8,128)S(1)} %get-tuple-element.50), channel_id=1, source_target_pairs={{0,1},{1,2},{2,3},{3,4},{4,5},{5,6},{6,7},{7,0},{8,9},{9,10},{10,1... | collective-permute-start | bytes 786440 | tf_op jit(solution)/shard_map/ppermute | solution.py:178
  193.7 8.4 %collective-permute-start.22 = (f32[512,128]{1,0:T(8,128)}, f32[512,128]{1,0:T(8,128)}, u32[]{:S(2)}, u32[]{:S(2)}) collective-permute-start(f32[512,128]{1,0:T(8,128)} %bitcast_add_fusion.4), channel_id=1, source_target_pairs={{0,1},{1,2},{2,3},{3,4},{4,5},{5,6},{6,7},{7,0},{8,9},{9,10},{10,1... | collective-permute-start | bytes 786440 | tf_op jit(solution)/shard_map/ppermute | solution.py:180
  193.9 11.5 %collective-permute-start.25 = (f32[512,128]{1,0:T(8,128)S(1)}, f32[512,128]{1,0:T(8,128)S(1)}, u32[]{:S(2)}, u32[]{:S(2)}) collective-permute-start(f32[512,128]{1,0:T(8,128)S(1)} %get-tuple-element.49), channel_id=1, source_target_pairs={{0,7},{1,0},{2,1},{3,2},{4,3},{5,4},{6,5},{7,6},{8,15},{9,8},{10,9... | collective-permute-start | bytes 786440 | tf_op jit(solution)/shard_map/ppermute | solution.py:181
  203.2 9.3 %collective-permute-start.23 = (f32[512,128]{1,0:T(8,128)S(1)}, f32[512,128]{1,0:T(8,128)S(1)}, u32[]{:S(2)}, u32[]{:S(2)}) collective-permute-start(f32[512,128]{1,0:T(8,128)S(1)} %bitcast_add_fusion.3), channel_id=1, source_target_pairs={{0,1},{1,2},{2,3},{3,4},{4,5},{5,6},{6,7},{7,0},{8,9},{9,10},{10,1... | collective-permute-start | bytes 786440 | tf_op jit(solution)/shard_map/ppermute | solution.py:182
  216.0 22.1 %all-to-all-start = ((f32[16,3,16,128]{3,2,1,0:T(8,128)}), f32[16,3,16,128]{3,2,1,0:T(8,128)S(1)}, u32[]{:S(2)}, u32[]{:S(2)}) async-start(f32[16,3,16,128]{3,2,1,0:T(8,128)} %maximum_bitcast_fusion), calls=%async_computation | async-start | bytes 786432 | tf_op jit(solution)/shard_map/all_to_all | solution.py:200
  (18 other events, 155.1 us)
Sparse Core Ops, SparseCore 0:
  54.8 62.6 all-gather.4
  119.9 40.1 all-gather.6

commit v6 on v5

--- a/solution.py
+++ b/solution.py
@@ -106,24 +106,20 @@
         return rows.reshape(2, 2, 4, 512, 128)
 
     g_other = lax.ppermute(g_top, "y_hi", ring(2, 1))
+    near_one = lax.ppermute(one, ALL_AXES, spread_pairs())
     packed = jnp.concatenate([one, dinv_one])
     pieces = {0: packed}
     right = left = packed
-    sent = one
     for d in range(1, 5):
         right = lax.ppermute(right, "z", ring(8, 1))
         if d < 4:
             left = lax.ppermute(left, "z", ring(8, -1))
-        if d == 1:
-            right, left, sent = lax.optimization_barrier((right, left, sent))
-            near_one = lax.ppermute(sent, ALL_AXES, spread_pairs())
-        if d == 4:
-            right, left, near_one, g_other = lax.optimization_barrier(
-                (right, left, near_one, g_other)
-            )
+            if d == 1:
+                right, left, near_one, g_other = lax.optimization_barrier(
+                    (right, left, near_one, g_other)
+                )
+            pieces[d] = left
         pieces[-d] = right
-        if d < 4:
-            pieces[d] = left
     gathered_one = gather(near_one)
 
     g = jnp.stack([g_top, g_other]).reshape(2, 512, 512)

time: 246 us -> 252 us (1.024)
  waiting for transfers between devices: 108 us -> 126 us
  starting transfers between devices: 70.9 us -> 58.1 us
    all_gather x2, waiting for transfers between devices: 20.3 us -> 0.02 us  [gather(): rows = lax.all_gather(piece, ROW_AXES, axis=0, tiled=False)]
    ppermute x1, waiting for transfers between devices: 6.77 us -> 23.9 us  [local(): par_other = lax.ppermute(par_there, 'y_hi', ring(2, 1))]
    ppermute x2, waiting for transfers between devices: 0.64 us -> 13.5 us  [multiply_and_sum(): down = lax.ppermute(term(-3), 'z', ring(8, -1))]
    ppermute x1, starting transfers between devices: 13.4 us -> 2.41 us  [local(): gathered_two = gather(lax.ppermute(folded, ALL_AXES, spread_pairs()))]
    ppermute x1, waiting for transfers between devices: 0.01 us -> 9.97 us  [local(): g_other = lax.ppermute(g_top, 'y_hi', ring(2, 1))]
    ppermute x1, starting transfers between devices: 6.01 us -> 1.91 us  [local(): near_one = lax.ppermute(one, ALL_AXES, spread_pairs())]
    ppermute x3, starting transfers between devices: 9.38 us -> 12.9 us  [local(): left = lax.ppermute(left, 'z', ring(8, -1))]
    ppermute x4, waiting for transfers between devices: 13.5 us -> 10.5 us  [local(): right = lax.ppermute(right, 'z', ring(8, 1))]
  transfers between devices with their start and end apart: 29 -> 29, of which waited for: 21 -> 21; matrix products, arithmetic and copies ran while one was open for 8% -> 9% of each run, Pallas kernels for 4% -> 4%
where the time goes in v6:
time: 252 us; the launch traced here: 250 us
  waiting for transfers between devices  126 us (50%)
  starting transfers between devices  58.1 us (23%)
  between operations  20.6 us (8%)
  local copies, waits for them, and re-layouts  14.1 us (6%)
  other arithmetic  13.9 us (6%)
  Pallas kernels  11.7 us (5%)
  matrix products  5.26 us (2%)
    ppermute x1, waiting for transfers between devices, local(): par_other = lax.ppermute(par_there, 'y_hi', ring(2, 1))  23.9 us
    all_to_all x1, starting transfers between devices, local(): sums = jnp.sum(lax.all_to_all(terms, ROW_AXES, 0, 0), axis=0)  16.1 us
    ppermute x2, waiting for transfers between devices, multiply_and_sum(): up = lax.ppermute(up + term(3), 'z', ring(8, 1))  13.7 us
    ppermute x2, waiting for transfers between devices, multiply_and_sum(): down = lax.ppermute(term(-3), 'z', ring(8, -1))  13.5 us
    ppermute x3, starting transfers between devices, local(): left = lax.ppermute(left, 'z', ring(8, -1))  12.9 us
    pallas_call x4, Pallas kernels, product(): pl.pallas_call(pair_kernel, grid_spec=pltpu.PrefetchScalarGridSpec(num_sc...  11.7 us
    ppermute x2, waiting for transfers between devices, multiply_and_sum(): down = lax.ppermute(down + term(-2), 'z', ring(8, -1))  11.4 us
    ppermute x4, waiting for transfers between devices, local(): right = lax.ppermute(right, 'z', ring(8, 1))  10.5 us
  transfers between devices with their start and end apart: 29, of which 21 were waited for; matrix products, arithmetic and copies ran while one was open for 9% of the time, Pallas kernels for 4%

profile of v6, /device:TPU:1, one launch (start us, length us, event | category | flops | bytes accessed | tf_op | source)
XLA Modules:
  0.0 249.8 jit_solution(17773377520027252929)
XLA Ops:
  7.2 3.8 %collective-permute-start.3 = (f32[2,256,2,256]{3,2,1,0:T(2,128)}, f32[2,256,2,256]{3,2,1,0:T(2,128)}, u32[]{:S(2)}, u32[]{:S(2)}) collective-permute-start(f32[2,256,2,256]{3,2,1,0:T(2,128)} %param.9), channel_id=1, source_target_pairs={{0,8},{8,0},{1,9},{9,1},{2,10},{10,2},{3,11},{11,3},{4,12},{12,4},... | collective-permute-start | bytes 3145736 | tf_op jit(solution)/shard_map/ppermute | solution.py:108
  18.9 4.0 %collective-permute-start.1 = (f32[528,128]{1,0:T(8,128)S(1)}, f32[528,128]{1,0:T(8,128)S(1)}, u32[]{:S(2)}, u32[]{:S(2)}) collective-permute-start(f32[528,128]{1,0:T(8,128)S(1)} %pad_maximum_fusion.2), channel_id=1, source_target_pairs={{0,7},{1,0},{2,1},{3,2},{4,3},{5,4},{6,5},{7,6},{8,15},{9,8},{10,9... | collective-permute-start | bytes 811016 | tf_op jit(solution)/shard_map/ppermute | solution.py:116
  24.9 3.6 %collective-permute-done.2 = f32[512,128]{1,0:T(8,128)S(1)} collective-permute-done((f32[512,128]{1,0:T(8,128)S(1)}, f32[512,128]{1,0:T(8,128)S(1)}, u32[]{:S(2)}, u32[]{:S(2)}) %collective-permute-start.2) | collective-permute-done | bytes 262176 | tf_op jit(solution)/shard_map/ppermute | solution.py:109
  28.9 10.0 %collective-permute-done.3 = f32[2,256,2,256]{3,2,1,0:T(2,128)} collective-permute-done((f32[2,256,2,256]{3,2,1,0:T(2,128)}, f32[2,256,2,256]{3,2,1,0:T(2,128)}, u32[]{:S(2)}, u32[]{:S(2)}) %collective-permute-start.3) | collective-permute-done | bytes 1048608 | tf_op jit(solution)/shard_map/ppermute | solution.py:108
  39.6 6.2 %collective-permute-start.15 = (f32[528,128]{1,0:T(8,128)S(1)}, f32[528,128]{1,0:T(8,128)S(1)}, u32[]{:S(2)}, u32[]{:S(2)}) collective-permute-start(f32[528,128]{1,0:T(8,128)S(1)} %collective-permute-done.1), channel_id=1, source_target_pairs={{0,7},{1,0},{2,1},{3,2},{4,3},{5,4},{6,5},{7,6},{8,15},{9,8},{10,9... | collective-permute-start | bytes 811016 | tf_op jit(solution)/shard_map/ppermute | solution.py:116
  45.8 5.0 %collective-permute-done.12 = f32[528,128]{1,0:T(8,128)S(1)} collective-permute-done((f32[528,128]{1,0:T(8,128)S(1)}, f32[528,128]{1,0:T(8,128)S(1)}, u32[]{:S(2)}, u32[]{:S(2)}) %collective-permute-start.12) | collective-permute-done | bytes 270368 | tf_op jit(solution)/shard_map/ppermute | solution.py:114
  50.8 2.7 %collective-permute-start.16 = (f32[528,128]{1,0:T(8,128)S(1)}, f32[528,128]{1,0:T(8,128)S(1)}, u32[]{:S(2)}, u32[]{:S(2)}) collective-permute-start(f32[528,128]{1,0:T(8,128)S(1)} %collective-permute-done.15), channel_id=1, source_target_pairs={{0,7},{1,0},{2,1},{3,2},{4,3},{5,4},{6,5},{7,6},{8,15},{9,8},{10,9... | collective-permute-start | bytes 811016 | tf_op jit(solution)/shard_map/ppermute | solution.py:116
  53.4 3.8 %collective-permute-done.13 = f32[528,128]{1,0:T(8,128)S(1)} collective-permute-done((f32[528,128]{1,0:T(8,128)S(1)}, f32[528,128]{1,0:T(8,128)S(1)}, u32[]{:S(2)}, u32[]{:S(2)}) %collective-permute-start.13) | collective-permute-done | bytes 270368 | tf_op jit(solution)/shard_map/ppermute | solution.py:114
  64.9 23.9 %collective-permute-done.17 = f32[528,256]{1,0:T(8,128)S(1)} collective-permute-done((f32[528,256]{1,0:T(8,128)S(1)}, f32[528,256]{1,0:T(8,128)S(1)}, u32[]{:S(2)}, u32[]{:S(2)}) %collective-permute-start.17) | collective-permute-done | bytes 540704 | tf_op jit(solution)/shard_map/ppermute | solution.py:145
  89.3 2.4 collective-permute-start.18
  91.7 5.9 %collective-permute-done.18 = f32[512,128]{1,0:T(8,128)S(1)} collective-permute-done((f32[512,128]{1,0:T(8,128)S(1)}, f32[512,128]{1,0:T(8,128)S(1)}, u32[]{:S(2)}, u32[]{:S(2)}) %collective-permute-start.18) | collective-permute-done | bytes 262176 | tf_op jit(solution)/shard_map/ppermute | solution.py:148
  109.6 2.9 %shard_map.128 = f32[4,512,128]{2,1,0:T(8,128)S(1)} custom-call(s32[5]{0:T(128)S(1)} %pad_add_fusion.sc_ref, bf16[2,512,512]{2,1,0:T(8,128)(2,1)S(1)} %get-tuple-element.50.gh_ref, bf16[2,512,512]{2,1,0:T(8,128)(2,1)S(1)} %get-tuple-element.49.gl_ref, f32[2,2,4,512,128]{4,3,2,1,0:T(8,128)S(1)} %bitcast.85, f32[2,2,4,512,128]{4,3,2,1,0:T(8,128)S(1)} %bitcast.86), custom_call_target="tpu_custom_call" | custom-call | flops 1600000000 | bytes 7000000 | tf_op jit(solution)/shard_map/pallas_call | solution.py:51
  112.8 5.6 %collective-permute-start.5 = (f32[512,128]{1,0:T(8,128)S(1)}, f32[512,128]{1,0:T(8,128)S(1)}, u32[]{:S(2)}, u32[]{:S(2)}) collective-permute-start(f32[512,128]{1,0:T(8,128)S(1)} %get-tuple-element.53), channel_id=1, source_target_pairs={{0,7},{1,0},{2,1},{3,2},{4,3},{5,4},{6,5},{7,6},{8,15},{9,8},{10,9... | collective-permute-start | bytes 786440 | tf_op jit(solution)/shard_map/ppermute | solution.py:172
  118.5 2.9 %shard_map.129 = f32[4,512,128]{2,1,0:T(8,128)S(1)} custom-call(s32[5]{0:T(128)S(1)} %pad_add_fusion.1.sc_ref, bf16[2,512,512]{2,1,0:T(8,128)(2,1)S(1)} %get-tuple-element.50.gh_ref, bf16[2,512,512]{2,1,0:T(8,128)(2,1)S(1)} %get-tuple-element.49.gl_ref, f32[2,2,4,512,128]{4,3,2,1,0:T(8,128)S(1)} %bitcast.87, f32[2,2,4,512,128]{4,3,2,1,0:T(8,128)S(1)} %bitcast.88), custom_call_target="tpu_custom_call" | custom-call | flops 1600000000 | bytes 7000000 | tf_op jit(solution)/shard_map/pallas_call | solution.py:51
  122.1 13.5 %collective-permute-done.5 = f32[512,128]{1,0:T(8,128)S(1)} collective-permute-done((f32[512,128]{1,0:T(8,128)S(1)}, f32[512,128]{1,0:T(8,128)S(1)}, u32[]{:S(2)}, u32[]{:S(2)}) %collective-permute-start.5) | collective-permute-done | bytes 262176 | tf_op jit(solution)/shard_map/ppermute | solution.py:172
  135.7 8.0 %collective-permute-done.9 = f32[512,128]{1,0:T(8,128)S(1)} collective-permute-done((f32[512,128]{1,0:T(8,128)S(1)}, f32[512,128]{1,0:T(8,128)S(1)}, u32[]{:S(2)}, u32[]{:S(2)}) %collective-permute-start.9) | collective-permute-done | bytes 262176 | tf_op jit(solution)/shard_map/ppermute | solution.py:175
  145.3 6.9 %collective-permute-done.6 = f32[512,128]{1,0:T(8,128)S(1)} collective-permute-done((f32[512,128]{1,0:T(8,128)S(1)}, f32[512,128]{1,0:T(8,128)S(1)}, u32[]{:S(2)}, u32[]{:S(2)}) %collective-permute-start.6) | collective-permute-done | bytes 262176 | tf_op jit(solution)/shard_map/ppermute | solution.py:174
  152.4 5.7 %collective-permute-done.11 = f32[768,128]{1,0:T(8,128)S(1)} collective-permute-done((f32[768,128]{1,0:T(8,128)S(1)}, f32[768,128]{1,0:T(8,128)S(1)}, u32[]{:S(2)}, u32[]{:S(2)}) %collective-permute-start.11) | collective-permute-done | bytes 393248 | tf_op jit(solution)/shard_map/ppermute | solution.py:150
  159.6 4.0 %collective-permute-done.7 = f32[512,128]{1,0:T(8,128)S(1)} collective-permute-done((f32[512,128]{1,0:T(8,128)S(1)}, f32[512,128]{1,0:T(8,128)S(1)}, u32[]{:S(2)}, u32[]{:S(2)}) %collective-permute-start.7) | collective-permute-done | bytes 262176 | tf_op jit(solution)/shard_map/ppermute | solution.py:176
  163.7 2.3 collective-permute-start.8
  166.9 4.0 %collective-permute-done.8 = f32[512,128]{1,0:T(8,128)S(1)} collective-permute-done((f32[512,128]{1,0:T(8,128)S(1)}, f32[512,128]{1,0:T(8,128)S(1)}, u32[]{:S(2)}, u32[]{:S(2)}) %collective-permute-start.8) | collective-permute-done | bytes 262176 | tf_op jit(solution)/shard_map/ppermute | solution.py:178
  171.0 2.2 copy-done.3
  173.2 2.9 %shard_map.130 = f32[4,512,128]{2,1,0:T(8,128)S(1)} custom-call(s32[5]{0:T(128)S(1)} %pad_add_fusion.2.sc_ref, bf16[2,512,512]{2,1,0:T(8,128)(2,1)S(1)} %get-tuple-element.50.gh_ref, bf16[2,512,512]{2,1,0:T(8,128)(2,1)S(1)} %get-tuple-element.49.gl_ref, f32[2,2,4,512,128]{4,3,2,1,0:T(8,128)S(1)} %bitcast.89, f32[2,2,4,512,128]{4,3,2,1,0:T(8,128)S(1)} %bitcast.90), custom_call_target="tpu_custom_call" | custom-call | flops 1600000000 | bytes 7000000 | tf_op jit(solution)/shard_map/pallas_call | solution.py:51
  179.0 2.9 %shard_map.131 = f32[4,512,128]{2,1,0:T(8,128)S(1)} custom-call(s32[5]{0:T(128)S(1)} %pad_add_fusion.3.sc_ref, bf16[2,512,512]{2,1,0:T(8,128)(2,1)S(1)} %get-tuple-element.50.gh_ref, bf16[2,512,512]{2,1,0:T(8,128)(2,1)S(1)} %get-tuple-element.49.gl_ref, f32[2,2,4,512,128]{4,3,2,1,0:T(8,128)S(1)} %bitcast.91, f32[2,2,4,512,128]{4,3,2,1,0:T(8,128)S(1)} %bitcast.92), custom_call_target="tpu_custom_call" | custom-call | flops 1600000000 | bytes 7000000 | tf_op jit(solution)/shard_map/pallas_call | solution.py:51
  182.7 2.7 %collective-permute-start.24 = (f32[512,128]{1,0:T(8,128)S(1)}, f32[512,128]{1,0:T(8,128)S(1)}, u32[]{:S(2)}, u32[]{:S(2)}) collective-permute-start(f32[512,128]{1,0:T(8,128)S(1)} %bitcast_add_fusion.2), channel_id=1, source_target_pairs={{0,7},{1,0},{2,1},{3,2},{4,3},{5,4},{6,5},{7,6},{8,15},{9,8},{10,9... | collective-permute-start | bytes 786440 | tf_op jit(solution)/shard_map/ppermute | solution.py:175
  185.5 3.4 %collective-permute-done.24 = f32[512,128]{1,0:T(8,128)S(1)} collective-permute-done((f32[512,128]{1,0:T(8,128)S(1)}, f32[512,128]{1,0:T(8,128)S(1)}, u32[]{:S(2)}, u32[]{:S(2)}) %collective-permute-start.24) | collective-permute-done | bytes 262176 | tf_op jit(solution)/shard_map/ppermute | solution.py:175
  189.0 6.8 %collective-permute-done.21 = f32[512,128]{1,0:T(8,128)S(1)} collective-permute-done((f32[512,128]{1,0:T(8,128)S(1)}, f32[512,128]{1,0:T(8,128)S(1)}, u32[]{:S(2)}, u32[]{:S(2)}) %collective-permute-start.21) | collective-permute-done | bytes 262176 | tf_op jit(solution)/shard_map/ppermute | solution.py:174
  196.7 2.7 %collective-permute-start.25 = (f32[512,128]{1,0:T(8,128)S(1)}, f32[512,128]{1,0:T(8,128)S(1)}, u32[]{:S(2)}, u32[]{:S(2)}) collective-permute-start(f32[512,128]{1,0:T(8,128)S(1)} %get-tuple-element.45), channel_id=1, source_target_pairs={{0,7},{1,0},{2,1},{3,2},{4,3},{5,4},{6,5},{7,6},{8,15},{9,8},{10,9... | collective-permute-start | bytes 786440 | tf_op jit(solution)/shard_map/ppermute | solution.py:177
  199.5 4.9 %collective-permute-done.22 = f32[512,128]{1,0:T(8,128)} collective-permute-done((f32[512,128]{1,0:T(8,128)}, f32[512,128]{1,0:T(8,128)}, u32[]{:S(2)}, u32[]{:S(2)}) %collective-permute-start.22) | collective-permute-done | bytes 262176 | tf_op jit(solution)/shard_map/ppermute | solution.py:176
  207.6 6.5 %collective-permute-done.23 = f32[512,128]{1,0:T(8,128)S(1)} collective-permute-done((f32[512,128]{1,0:T(8,128)S(1)}, f32[512,128]{1,0:T(8,128)S(1)}, u32[]{:S(2)}, u32[]{:S(2)}) %collective-permute-start.23) | collective-permute-done | bytes 262176 | tf_op jit(solution)/shard_map/ppermute | solution.py:178
  217.6 16.1 %all-to-all-start = ((f32[16,3,16,128]{3,2,1,0:T(8,128)}), f32[16,3,16,128]{3,2,1,0:T(8,128)S(1)}, u32[]{:S(2)}, u32[]{:S(2)}) async-start(f32[16,3,16,128]{3,2,1,0:T(8,128)} %maximum_bitcast_fusion), calls=%async_computation | async-start | bytes 786432 | tf_op jit(solution)/shard_map/all_to_all | solution.py:196
  235.3 7.0 %all-to-all-done = f32[16,3,16,128]{3,2,1,0:T(8,128)S(1)} async-done(((f32[16,3,16,128]{3,2,1,0:T(8,128)}), f32[16,3,16,128]{3,2,1,0:T(8,128)S(1)}, u32[]{:S(2)}, u32[]{:S(2)}) %all-to-all-start) | async-done | bytes 393248 | tf_op jit(solution)/shard_map/all_to_all | solution.py:196
  (136 shorter events, 43.9 us)
Async XLA Ops:
  7.2 56.6 %copy-start.11 = (f32[16,128]{1,0:T(8,128)S(1)}, f32[16,128]{1,0:T(8,128)}, u32[]{:S(2)}) copy-start(f32[16,128]{1,0:T(8,128)} %param.12) | copy-start | bytes 24580
  7.2 100.2 %all-gather.5.cloned.1.call-start = ((), (), s32[]{:S(2)}) async-start(), calls=%async_computation.1 | async-start | bytes 4456448 | tf_op jit(solution)/shard_map/all_gather | solution.py:105
  7.2 31.6 %collective-permute-start.3 = (f32[2,256,2,256]{3,2,1,0:T(2,128)}, f32[2,256,2,256]{3,2,1,0:T(2,128)}, u32[]{:S(2)}, u32[]{:S(2)}) collective-permute-start(f32[2,256,2,256]{3,2,1,0:T(2,128)} %param.9), channel_id=1, source_target_pairs={{0,8},{8,0},{1,9},{9,1},{2,10},{10,2},{3,11},{11,3},{4,12},{12,4},... | collective-permute-start | bytes 3145736 | tf_op jit(solution)/shard_map/ppermute | solution.py:108
  17.2 11.6 %collective-permute-start = (f32[528,128]{1,0:T(8,128)S(1)}, f32[528,128]{1,0:T(8,128)S(1)}, u32[]{:S(2)}, u32[]{:S(2)}) collective-permute-start(f32[528,128]{1,0:T(8,128)S(1)} %pad_maximum_fusion.2), channel_id=1, source_target_pairs={{0,1},{1,2},{2,3},{3,4},{4,5},{5,6},{6,7},{7,0},{8,9},{9,10},{10,1... | collective-permute-start | bytes 811016 | tf_op jit(solution)/shard_map/ppermute | solution.py:114
  18.9 9.9 %collective-permute-start.1 = (f32[528,128]{1,0:T(8,128)S(1)}, f32[528,128]{1,0:T(8,128)S(1)}, u32[]{:S(2)}, u32[]{:S(2)}) collective-permute-start(f32[528,128]{1,0:T(8,128)S(1)} %pad_maximum_fusion.2), channel_id=1, source_target_pairs={{0,7},{1,0},{2,1},{3,2},{4,3},{5,4},{6,5},{7,6},{8,15},{9,8},{10,9... | collective-permute-start | bytes 811016 | tf_op jit(solution)/shard_map/ppermute | solution.py:116
  23.0 5.5 %collective-permute-start.2 = (f32[512,128]{1,0:T(8,128)S(1)}, f32[512,128]{1,0:T(8,128)S(1)}, u32[]{:S(2)}, u32[]{:S(2)}) collective-permute-start(f32[512,128]{1,0:T(8,128)S(1)} %bitcast.94), channel_id=1, source_target_pairs={{0,16},{1,48},{2,80},{3,112},{4,0},{5,32},{6,64},{7,96},{8,24},{9,... | collective-permute-start | bytes 786440 | tf_op jit(solution)/shard_map/ppermute | solution.py:109
  38.9 132.1 %all-gather.7.cloned.1.call-start = ((), (), s32[]{:S(2)}) async-start(), calls=%async_computation.2 | async-start | bytes 4456448 | tf_op jit(solution)/shard_map/all_gather | solution.py:105
  38.9 11.9 %collective-permute-start.12 = (f32[528,128]{1,0:T(8,128)S(1)}, f32[528,128]{1,0:T(8,128)S(1)}, u32[]{:S(2)}, u32[]{:S(2)}) collective-permute-start(f32[528,128]{1,0:T(8,128)S(1)} %collective-permute-done), channel_id=1, source_target_pairs={{0,1},{1,2},{2,3},{3,4},{4,5},{5,6},{6,7},{7,0},{8,9},{9,10},{10,1... | collective-permute-start | bytes 811016 | tf_op jit(solution)/shard_map/ppermute | solution.py:114
  39.6 11.2 %collective-permute-start.15 = (f32[528,128]{1,0:T(8,128)S(1)}, f32[528,128]{1,0:T(8,128)S(1)}, u32[]{:S(2)}, u32[]{:S(2)}) collective-permute-start(f32[528,128]{1,0:T(8,128)S(1)} %collective-permute-done.1), channel_id=1, source_target_pairs={{0,7},{1,0},{2,1},{3,2},{4,3},{5,4},{6,5},{7,6},{8,15},{9,8},{10,9... | collective-permute-start | bytes 811016 | tf_op jit(solution)/shard_map/ppermute | solution.py:116
  50.8 6.5 %collective-permute-start.13 = (f32[528,128]{1,0:T(8,128)S(1)}, f32[528,128]{1,0:T(8,128)S(1)}, u32[]{:S(2)}, u32[]{:S(2)}) collective-permute-start(f32[528,128]{1,0:T(8,128)S(1)} %collective-permute-done.12), channel_id=1, source_target_pairs={{0,1},{1,2},{2,3},{3,4},{4,5},{5,6},{6,7},{7,0},{8,9},{9,10},{10,1... | collective-permute-start | bytes 811016 | tf_op jit(solution)/shard_map/ppermute | solution.py:114
  50.8 11.7 %collective-permute-start.16 = (f32[528,128]{1,0:T(8,128)S(1)}, f32[528,128]{1,0:T(8,128)S(1)}, u32[]{:S(2)}, u32[]{:S(2)}) collective-permute-start(f32[528,128]{1,0:T(8,128)S(1)} %collective-permute-done.15), channel_id=1, source_target_pairs={{0,7},{1,0},{2,1},{3,2},{4,3},{5,4},{6,5},{7,6},{8,15},{9,8},{10,9... | collective-permute-start | bytes 811016 | tf_op jit(solution)/shard_map/ppermute | solution.py:116
  57.3 6.5 %collective-permute-start.14 = (f32[528,128]{1,0:T(8,128)S(1)}, f32[528,128]{1,0:T(8,128)S(1)}, u32[]{:S(2)}, u32[]{:S(2)}) collective-permute-start(f32[528,128]{1,0:T(8,128)S(1)} %collective-permute-done.13), channel_id=1, source_target_pairs={{0,1},{1,2},{2,3},{3,4},{4,5},{5,6},{6,7},{7,0},{8,9},{9,10},{10,1... | collective-permute-start | bytes 811016 | tf_op jit(solution)/shard_map/ppermute | solution.py:114
  64.2 24.6 %collective-permute-start.17 = (f32[528,256]{1,0:T(8,128)S(1)}, f32[528,256]{1,0:T(8,128)S(1)}, u32[]{:S(2)}, u32[]{:S(2)}) collective-permute-start(f32[528,256]{1,0:T(8,128)S(1)} %pad_maximum_fusion), channel_id=1, source_target_pairs={{0,8},{8,0},{1,9},{9,1},{2,10},{10,2},{3,11},{11,3},{4,12},{12,4},... | collective-permute-start | bytes 1622024 | tf_op jit(solution)/shard_map/ppermute | solution.py:145
  64.7 24.2 %copy-start.7 = (f32[256,128]{1,0:T(8,128)S(1)}, f32[256,128]{1,0:T(8,128)}, u32[]{:S(2)}) copy-start(f32[256,128]{1,0:T(8,128)} %param.14) | copy-start | bytes 393220
  89.3 8.3 %collective-permute-start.18 = (f32[512,128]{1,0:T(8,128)S(1)}, f32[512,128]{1,0:T(8,128)S(1)}, u32[]{:S(2)}, u32[]{:S(2)}) collective-permute-start(f32[512,128]{1,0:T(8,128)S(1)} %convolution_subtract_fusion), channel_id=1, source_target_pairs={{0,16},{1,48},{2,80},{3,112},{4,0},{5,32},{6,64},{7,96},{8,24},{9,... | collective-permute-start | bytes 786440 | tf_op jit(solution)/shard_map/ppermute | solution.py:148
  112.6 9.5 %collective-permute-start.4 = (f32[512,128]{1,0:T(8,128)S(1)}, f32[512,128]{1,0:T(8,128)S(1)}, u32[]{:S(2)}, u32[]{:S(2)}) collective-permute-start(f32[512,128]{1,0:T(8,128)S(1)} %get-tuple-element.54), channel_id=1, source_target_pairs={{0,1},{1,2},{2,3},{3,4},{4,5},{5,6},{6,7},{7,0},{8,9},{9,10},{10,1... | collective-permute-start | bytes 786440 | tf_op jit(solution)/shard_map/ppermute | solution.py:171
  112.8 22.8 %collective-permute-start.5 = (f32[512,128]{1,0:T(8,128)S(1)}, f32[512,128]{1,0:T(8,128)S(1)}, u32[]{:S(2)}, u32[]{:S(2)}) collective-permute-start(f32[512,128]{1,0:T(8,128)S(1)} %get-tuple-element.53), channel_id=1, source_target_pairs={{0,7},{1,0},{2,1},{3,2},{4,3},{5,4},{6,5},{7,6},{8,15},{9,8},{10,9... | collective-permute-start | bytes 786440 | tf_op jit(solution)/shard_map/ppermute | solution.py:172
  135.6 8.1 %collective-permute-start.9 = (f32[512,128]{1,0:T(8,128)S(1)}, f32[512,128]{1,0:T(8,128)S(1)}, u32[]{:S(2)}, u32[]{:S(2)}) collective-permute-start(f32[512,128]{1,0:T(8,128)S(1)} %bitcast_add_fusion.8), channel_id=1, source_target_pairs={{0,7},{1,0},{2,1},{3,2},{4,3},{5,4},{6,5},{7,6},{8,15},{9,8},{10,9... | collective-permute-start | bytes 786440 | tf_op jit(solution)/shard_map/ppermute | solution.py:175
  143.8 8.4 %collective-permute-start.6 = (f32[512,128]{1,0:T(8,128)S(1)}, f32[512,128]{1,0:T(8,128)S(1)}, u32[]{:S(2)}, u32[]{:S(2)}) collective-permute-start(f32[512,128]{1,0:T(8,128)S(1)} %get-tuple-element.48), channel_id=1, source_target_pairs={{0,1},{1,2},{2,3},{3,4},{4,5},{5,6},{6,7},{7,0},{8,9},{9,10},{10,1... | collective-permute-start | bytes 786440 | tf_op jit(solution)/shard_map/ppermute | solution.py:174
  145.1 13.0 %collective-permute-start.11 = (f32[768,128]{1,0:T(8,128)S(1)}, f32[768,128]{1,0:T(8,128)S(1)}, u32[]{:S(2)}, u32[]{:S(2)}) collective-permute-start(f32[768,128]{1,0:T(8,128)S(1)} %pad_maximum_fusion.1), channel_id=1, source_target_pairs={{0,1},{1,0},{2,3},{3,2},{4,5},{5,4},{6,7},{7,6},{8,9},{9,8},{10,11... | collective-permute-start | bytes 1179656 | tf_op jit(solution)/shard_map/ppermute | solution.py:150
  152.3 11.4 %collective-permute-start.7 = (f32[512,128]{1,0:T(8,128)S(1)}, f32[512,128]{1,0:T(8,128)S(1)}, u32[]{:S(2)}, u32[]{:S(2)}) collective-permute-start(f32[512,128]{1,0:T(8,128)S(1)} %bitcast_add_fusion.10), channel_id=1, source_target_pairs={{0,1},{1,2},{2,3},{3,4},{4,5},{5,6},{6,7},{7,0},{8,9},{9,10},{10,1... | collective-permute-start | bytes 786440 | tf_op jit(solution)/shard_map/ppermute | solution.py:176
  159.6 7.2 %collective-permute-start.10 = (f32[512,128]{1,0:T(8,128)S(1)}, f32[512,128]{1,0:T(8,128)S(1)}, u32[]{:S(2)}, u32[]{:S(2)}) collective-permute-start(f32[512,128]{1,0:T(8,128)S(1)} %get-tuple-element.47), channel_id=1, source_target_pairs={{0,7},{1,0},{2,1},{3,2},{4,3},{5,4},{6,5},{7,6},{8,15},{9,8},{10,9... | collective-permute-start | bytes 786440 | tf_op jit(solution)/shard_map/ppermute | solution.py:177
  163.7 7.1 %collective-permute-start.8 = (f32[512,128]{1,0:T(8,128)S(1)}, f32[512,128]{1,0:T(8,128)S(1)}, u32[]{:S(2)}, u32[]{:S(2)}) collective-permute-start(f32[512,128]{1,0:T(8,128)S(1)} %bitcast_add_fusion.9), channel_id=1, source_target_pairs={{0,1},{1,2},{2,3},{3,4},{4,5},{5,6},{6,7},{7,0},{8,9},{9,10},{10,1... | collective-permute-start | bytes 786440 | tf_op jit(solution)/shard_map/ppermute | solution.py:178
  176.1 6.5 %collective-permute-start.19 = (f32[512,128]{1,0:T(8,128)S(1)}, f32[512,128]{1,0:T(8,128)S(1)}, u32[]{:S(2)}, u32[]{:S(2)}) collective-permute-start(f32[512,128]{1,0:T(8,128)S(1)} %get-tuple-element.52), channel_id=1, source_target_pairs={{0,1},{1,2},{2,3},{3,4},{4,5},{5,6},{6,7},{7,0},{8,9},{9,10},{10,1... | collective-permute-start | bytes 786440 | tf_op jit(solution)/shard_map/ppermute | solution.py:171
  177.2 5.5 %collective-permute-start.20 = (f32[512,128]{1,0:T(8,128)S(1)}, f32[512,128]{1,0:T(8,128)S(1)}, u32[]{:S(2)}, u32[]{:S(2)}) collective-permute-start(f32[512,128]{1,0:T(8,128)S(1)} %get-tuple-element.51), channel_id=1, source_target_pairs={{0,7},{1,0},{2,1},{3,2},{4,3},{5,4},{6,5},{7,6},{8,15},{9,8},{10,9... | collective-permute-start | bytes 786440 | tf_op jit(solution)/shard_map/ppermute | solution.py:172
  182.7 6.2 %collective-permute-start.24 = (f32[512,128]{1,0:T(8,128)S(1)}, f32[512,128]{1,0:T(8,128)S(1)}, u32[]{:S(2)}, u32[]{:S(2)}) collective-permute-start(f32[512,128]{1,0:T(8,128)S(1)} %bitcast_add_fusion.2), channel_id=1, source_target_pairs={{0,7},{1,0},{2,1},{3,2},{4,3},{5,4},{6,5},{7,6},{8,15},{9,8},{10,9... | collective-permute-start | bytes 786440 | tf_op jit(solution)/shard_map/ppermute | solution.py:175
  188.9 6.9 %collective-permute-start.21 = (f32[512,128]{1,0:T(8,128)S(1)}, f32[512,128]{1,0:T(8,128)S(1)}, u32[]{:S(2)}, u32[]{:S(2)}) collective-permute-start(f32[512,128]{1,0:T(8,128)S(1)} %get-tuple-element.46), channel_id=1, source_target_pairs={{0,1},{1,2},{2,3},{3,4},{4,5},{5,6},{6,7},{7,0},{8,9},{9,10},{10,1... | collective-permute-start | bytes 786440 | tf_op jit(solution)/shard_map/ppermute | solution.py:174
  196.5 7.8 %collective-permute-start.22 = (f32[512,128]{1,0:T(8,128)}, f32[512,128]{1,0:T(8,128)}, u32[]{:S(2)}, u32[]{:S(2)}) collective-permute-start(f32[512,128]{1,0:T(8,128)} %bitcast_add_fusion.4), channel_id=1, source_target_pairs={{0,1},{1,2},{2,3},{3,4},{4,5},{5,6},{6,7},{7,0},{8,9},{9,10},{10,1... | collective-permute-start | bytes 786440 | tf_op jit(solution)/shard_map/ppermute | solution.py:176
  196.7 10.9 %collective-permute-start.25 = (f32[512,128]{1,0:T(8,128)S(1)}, f32[512,128]{1,0:T(8,128)S(1)}, u32[]{:S(2)}, u32[]{:S(2)}) collective-permute-start(f32[512,128]{1,0:T(8,128)S(1)} %get-tuple-element.45), channel_id=1, source_target_pairs={{0,7},{1,0},{2,1},{3,2},{4,3},{5,4},{6,5},{7,6},{8,15},{9,8},{10,9... | collective-permute-start | bytes 786440 | tf_op jit(solution)/shard_map/ppermute | solution.py:177
  205.4 8.8 %collective-permute-start.23 = (f32[512,128]{1,0:T(8,128)S(1)}, f32[512,128]{1,0:T(8,128)S(1)}, u32[]{:S(2)}, u32[]{:S(2)}) collective-permute-start(f32[512,128]{1,0:T(8,128)S(1)} %bitcast_add_fusion.3), channel_id=1, source_target_pairs={{0,1},{1,2},{2,3},{3,4},{4,5},{5,6},{6,7},{7,0},{8,9},{9,10},{10,1... | collective-permute-start | bytes 786440 | tf_op jit(solution)/shard_map/ppermute | solution.py:178
  216.2 26.1 %copy-start.14 = (f32[16,128]{1,0:T(8,128)S(1)}, f32[16,128]{1,0:T(8,128)}, u32[]{:S(2)}) copy-start(f32[16,128]{1,0:T(8,128)} %param.17) | copy-start | bytes 24580
  217.6 24.6 %all-to-all-start = ((f32[16,3,16,128]{3,2,1,0:T(8,128)}), f32[16,3,16,128]{3,2,1,0:T(8,128)S(1)}, u32[]{:S(2)}, u32[]{:S(2)}) async-start(f32[16,3,16,128]{3,2,1,0:T(8,128)} %maximum_bitcast_fusion), calls=%async_computation | async-start | bytes 786432 | tf_op jit(solution)/shard_map/all_to_all | solution.py:196
  (18 other events, 170.9 us)
Sparse Core Ops, SparseCore 0:
  39.0 53.7 all-gather.4
  98.4 56.7 all-gather.6

commit v7 on v6

--- a/solution.py
+++ b/solution.py
@@ -106,6 +106,7 @@
         return rows.reshape(2, 2, 4, 512, 128)
 
     g_other = lax.ppermute(g_top, "y_hi", ring(2, 1))
+    lp_far = lax.ppermute(lp_two, "y_hi", ring(2, 1))
     near_one = lax.ppermute(one, ALL_AXES, spread_pairs())
     packed = jnp.concatenate([one, dinv_one])
     pieces = {0: packed}
@@ -115,11 +116,10 @@
         if d < 4:
             left = lax.ppermute(left, "z", ring(8, -1))
             if d == 1:
-                right, left, near_one, g_other = lax.optimization_barrier(
-                    (right, left, near_one, g_other)
-                )
+                right, left, near_one = lax.optimization_barrier((right, left, near_one))
             pieces[d] = left
         pieces[-d] = right
+    pieces[-4], g_other, lp_far = lax.optimization_barrier((right, g_other, lp_far))
     gathered_one = gather(near_one)
 
     g = jnp.stack([g_top, g_other]).reshape(2, 512, 512)
@@ -142,16 +142,17 @@
     even = z % 2 == 0
     pair_up = lambda a, b: jnp.where(even, jnp.concatenate([a, b], 1), jnp.concatenate([b, a], 1))
     own_one = pair_up(one, jnp.where(even, pieces[1], pieces[-1])[:512])
-    par_other = lax.ppermute(par_there, "y_hi", ring(2, 1))
-    par = jnp.where(parent // 4 == h, par_here, par_other)
-    folded = two - jnp.dot(par[:512], lp_two, precision=lax.Precision.HIGH)
-    gathered_two = gather(lax.ppermute(folded, ALL_AXES, spread_pairs()))
+    here = parent // 4 == h
+    by_lp = lambda cols, lp: jnp.dot(cols[:512], lp, precision=lax.Precision.HIGH)
+    from_far = lax.ppermute(by_lp(par_there, lp_far), "y_hi", ring(2, 1))
+    folded = two - jnp.where(here, by_lp(par_here, lp_two), from_far)
+    near_two = lax.ppermute(folded, ALL_AXES, spread_pairs())
     two_sent = jnp.concatenate([two, lp_two])
     two_next = lax.ppermute(two_sent, "z", [(i, i ^ 1) for i in range(8)])
     own_two = pair_up(two, two_next[:512])
     lp_own = pair_up(lp_two, two_next[512:])
 
-    def multiply_and_sum(gathered, after):
+    def multiply(gathered, after):
         def part(first_pair, after):
             both = jnp.arange(2, dtype=jnp.int32)
             slots = (first_pair + both) % 4 * 2
@@ -162,8 +163,9 @@
 
         early = part((z + 4) // 2, after)
         after, early = lax.optimization_barrier((after, early))
-        late = part((z + 4) // 2 + 2, after)
-
+        return early, part((z + 4) // 2 + 2, after)
+
+    def sum_over_z(early, late):
         def term(d):
             take = lambda i: early[i] if i < 4 else late[i - 4]
             return jnp.where(even, take((d - 4) % 8), take((d - 3) % 8))
@@ -177,11 +179,15 @@
         down = lax.ppermute(down + term(-1), "z", ring(8, -1))
         return lax.ppermute(up + term(1), "z", ring(8, 1)) + down + term(0)
 
-    inv_one = multiply_and_sum(gathered_one, h)
-    inv_one, own_one, own_two, lp_own, h_next = lax.optimization_barrier(
-        (inv_one, own_one, own_two, lp_own, h)
+    early, late = multiply(gathered_one, h)
+    near_two, early, late = lax.optimization_barrier((near_two, early, late))
+    gathered_two = gather(near_two)
+    inv_one = sum_over_z(early, late)
+    inv_one, own_one, own_two, lp_own, par_there, h_next = lax.optimization_barrier(
+        (inv_one, own_one, own_two, lp_own, par_there, h)
     )
-    inv_two = multiply_and_sum(gathered_two, h_next)
+    par = jnp.where(here, par_here, lax.ppermute(par_there, "y_hi", ring(2, 1)))
+    inv_two = sum_over_z(*multiply(gathered_two, h_next))
     panel_one = jnp.where(keep_one, inv_one.reshape(2, 256, 128), 0.0)
     panel_two = jnp.where(keep_two, inv_two.reshape(2, 256, 128), 0.0)
 

time: 252 us -> 241 us (0.956)
  waiting for transfers between devices: 126 us -> 74.2 us
  starting transfers between devices: 58.1 us -> 91.9 us
  other arithmetic: 13.9 us -> 18.8 us
  local copies, waits for them, and re-layouts: 14.1 us -> 17.4 us
    ppermute x16 -> x18, waiting for transfers between devices: 89.3 us -> 52.7 us  [the longest x2 11 us: sum_over_z(): up = lax.ppermute(up + term(3), 'z', ring(8, 1))]
    ppermute x16 -> x18, starting transfers between devices: 20.7 us -> 46.2 us  [the longest x2 16.2 us: sum_over_z(): down = lax.ppermute(term(-3), 'z', ring(8, -1))]
    ppermute x1, waiting for transfers between devices: 9.97 us -> 0.01 us  [local(): g_other = lax.ppermute(g_top, 'y_hi', ring(2, 1))]
    ppermute x3, starting transfers between devices: 12.9 us -> 22.6 us  [local(): left = lax.ppermute(left, 'z', ring(8, -1))]
    ppermute x4, waiting for transfers between devices: 10.5 us -> 7.1 us  [local(): right = lax.ppermute(right, 'z', ring(8, 1))]
    unnamed x43 -> x93, local copies, waits for them, and re-layouts: 6.62 us -> 7.56 us
  transfers between devices with their start and end apart: 29 -> 31, of which waited for: 21 -> 18; matrix products, arithmetic and copies ran while one was open for 9% -> 11% of each run, Pallas kernels for 4% -> 4%
where the time goes in v7:
time: 241 us; the launch traced here: 240 us
  starting transfers between devices  91.9 us (38%)
  waiting for transfers between devices  74.2 us (31%)
  between operations  20.9 us (9%)
  other arithmetic  18.8 us (8%)
  local copies, waits for them, and re-layouts  17.4 us (7%)
  Pallas kernels  11.6 us (5%)
  matrix products  5.65 us (2%)
    ppermute x3, starting transfers between devices, local(): left = lax.ppermute(left, 'z', ring(8, -1))  22.6 us
    ppermute x2, starting transfers between devices, sum_over_z(): down = lax.ppermute(term(-3), 'z', ring(8, -1))  16.2 us
    all_to_all x1, starting transfers between devices, local(): sums = jnp.sum(lax.all_to_all(terms, ROW_AXES, 0, 0), axis=0)  15.4 us
    pallas_call x4, Pallas kernels, product(): pl.pallas_call(pair_kernel, grid_spec=pltpu.PrefetchScalarGridSpec(num_sc...  11.6 us
    ppermute x2, waiting for transfers between devices, sum_over_z(): up = lax.ppermute(up + term(3), 'z', ring(8, 1))  11 us
    ppermute x2, waiting for transfers between devices, sum_over_z(): down = lax.ppermute(down + term(-2), 'z', ring(8, -1))  8.95 us
    ppermute x2, waiting for transfers between devices, sum_over_z(): return lax.ppermute(up + term(1), 'z', ring(8, 1)) + down + term(0)  8.57 us
    ppermute x1, waiting for transfers between devices, local(): from_far = lax.ppermute(by_lp(par_there, lp_far), 'y_hi', ring(2, 1))  7.91 us
  transfers between devices with their start and end apart: 31, of which 18 were waited for; matrix products, arithmetic and copies ran while one was open for 11% of the time, Pallas kernels for 4%

profile of v7, /device:TPU:1, one launch (start us, length us, event | category | flops | bytes accessed | tf_op | source)
XLA Modules:
  0.0 240.4 jit_solution(227873168054298022)
XLA Ops:
  15.9 4.0 %collective-permute-start.1 = (f32[528,128]{1,0:T(8,128)S(1)}, f32[528,128]{1,0:T(8,128)S(1)}, u32[]{:S(2)}, u32[]{:S(2)}) collective-permute-start(f32[528,128]{1,0:T(8,128)S(1)} %pad_maximum_fusion.3), channel_id=1, source_target_pairs={{0,7},{1,0},{2,1},{3,2},{4,3},{5,4},{6,5},{7,6},{8,15},{9,8},{10,9... | collective-permute-start | bytes 811016 | tf_op jit(solution)/shard_map/ppermute | solution.py:117
  22.4 3.7 %collective-permute-done.2 = f32[512,128]{1,0:T(8,128)S(1)} collective-permute-done((f32[512,128]{1,0:T(8,128)S(1)}, f32[512,128]{1,0:T(8,128)S(1)}, u32[]{:S(2)}, u32[]{:S(2)}) %collective-permute-start.2) | collective-permute-done | bytes 262176 | tf_op jit(solution)/shard_map/ppermute | solution.py:110
  30.3 15.9 %collective-permute-start.8 = (f32[528,128]{1,0:T(8,128)S(1)}, f32[528,128]{1,0:T(8,128)S(1)}, u32[]{:S(2)}, u32[]{:S(2)}) collective-permute-start(f32[528,128]{1,0:T(8,128)S(1)} %collective-permute-done.1), channel_id=1, source_target_pairs={{0,7},{1,0},{2,1},{3,2},{4,3},{5,4},{6,5},{7,6},{8,15},{9,8},{10,9... | collective-permute-start | bytes 811016 | tf_op jit(solution)/shard_map/ppermute | solution.py:117
  46.2 4.7 %collective-permute-done.3 = f32[528,128]{1,0:T(8,128)S(1)} collective-permute-done((f32[528,128]{1,0:T(8,128)S(1)}, f32[528,128]{1,0:T(8,128)S(1)}, u32[]{:S(2)}, u32[]{:S(2)}) %collective-permute-start.3) | collective-permute-done | bytes 270368 | tf_op jit(solution)/shard_map/ppermute | solution.py:115
  52.8 2.7 %collective-permute-start.9 = (f32[528,128]{1,0:T(8,128)S(1)}, f32[528,128]{1,0:T(8,128)S(1)}, u32[]{:S(2)}, u32[]{:S(2)}) collective-permute-start(f32[528,128]{1,0:T(8,128)S(1)} %collective-permute-done.8), channel_id=1, source_target_pairs={{0,7},{1,0},{2,1},{3,2},{4,3},{5,4},{6,5},{7,6},{8,15},{9,8},{10,9... | collective-permute-start | bytes 811016 | tf_op jit(solution)/shard_map/ppermute | solution.py:117
  57.9 3.2 %stack.21 = f32[1,512,512]{2,1,0:T(8,128)} reshape(f32[2,256,2,256]{3,2,1,0:T(2,128)} %param.9) | data formatting | bytes 2097152 | tf_op jit(solution)/shard_map/stack | solution.py:125
  67.6 3.3 %stack.22 = f32[1,512,512]{2,1,0:T(8,128)} reshape(f32[2,256,2,256]{3,2,1,0:T(2,128)} %collective-permute-done.6) | data formatting | bytes 2097152 | tf_op jit(solution)/shard_map/stack | solution.py:125
  71.7 2.6 %collective-permute-start.10 = (f32[512,128]{1,0:T(8,128)S(1)}, f32[512,128]{1,0:T(8,128)S(1)}, u32[]{:S(2)}, u32[]{:S(2)}) collective-permute-start(f32[512,128]{1,0:T(8,128)S(1)} %fusion.3), channel_id=1, source_target_pairs={{0,8},{8,0},{1,9},{9,1},{2,10},{10,2},{3,11},{11,3},{4,12},{12,4},... | collective-permute-start | bytes 786440 | tf_op jit(solution)/shard_map/ppermute | solution.py:147
  78.0 7.9 %collective-permute-done.10 = f32[512,128]{1,0:T(8,128)S(1)} collective-permute-done((f32[512,128]{1,0:T(8,128)S(1)}, f32[512,128]{1,0:T(8,128)S(1)}, u32[]{:S(2)}, u32[]{:S(2)}) %collective-permute-start.10) | collective-permute-done | bytes 262176 | tf_op jit(solution)/shard_map/ppermute | solution.py:147
  87.0 6.8 %collective-permute-start.11 = (f32[512,128]{1,0:T(8,128)}, f32[512,128]{1,0:T(8,128)}, u32[]{:S(2)}, u32[]{:S(2)}) collective-permute-start(f32[512,128]{1,0:T(8,128)} %fusion.11), channel_id=1, source_target_pairs={{0,16},{1,48},{2,80},{3,112},{4,0},{5,32},{6,64},{7,96},{8,24},{9,... | collective-permute-start | bytes 786440 | tf_op jit(solution)/shard_map/ppermute | solution.py:149
  96.0 2.9 %shard_map.128 = f32[4,512,128]{2,1,0:T(8,128)S(1)} custom-call(s32[5]{0:T(128)S(1)} %pad_add_fusion.sc_ref, bf16[2,512,512]{2,1,0:T(8,128)(2,1)S(1)} %get-tuple-element.62.gh_ref, bf16[2,512,512]{2,1,0:T(8,128)(2,1)S(1)} %get-tuple-element.61.gl_ref, f32[2,2,4,512,128]{4,3,2,1,0:T(8,128)S(1)} %bitcast.86, f32[2,2,4,512,128]{4,3,2,1,0:T(8,128)S(1)} %bitcast.87), custom_call_target="tpu_custom_call" | custom-call | flops 1600000000 | bytes 7000000 | tf_op jit(solution)/shard_map/pallas_call | solution.py:51
  99.0 2.9 %shard_map.129 = f32[4,512,128]{2,1,0:T(8,128)S(1)} custom-call(s32[5]{0:T(128)S(1)} %pad_add_fusion.1.sc_ref, bf16[2,512,512]{2,1,0:T(8,128)(2,1)S(1)} %get-tuple-element.62.gh_ref, bf16[2,512,512]{2,1,0:T(8,128)(2,1)S(1)} %get-tuple-element.61.gl_ref, f32[2,2,4,512,128]{4,3,2,1,0:T(8,128)S(1)} %bitcast.88, f32[2,2,4,512,128]{4,3,2,1,0:T(8,128)S(1)} %bitcast.89), custom_call_target="tpu_custom_call" | custom-call | flops 1600000000 | bytes 7000000 | tf_op jit(solution)/shard_map/pallas_call | solution.py:51
  104.4 13.6 %collective-permute-start.13 = (f32[512,128]{1,0:T(8,128)S(1)}, f32[512,128]{1,0:T(8,128)S(1)}, u32[]{:S(2)}, u32[]{:S(2)}) collective-permute-start(f32[512,128]{1,0:T(8,128)S(1)} %get-tuple-element.65), channel_id=1, source_target_pairs={{0,7},{1,0},{2,1},{3,2},{4,3},{5,4},{6,5},{7,6},{8,15},{9,8},{10,9... | collective-permute-start | bytes 786440 | tf_op jit(solution)/shard_map/ppermute | solution.py:174
  117.9 6.2 %collective-permute-done.12 = f32[512,128]{1,0:T(8,128)S(1)} collective-permute-done((f32[512,128]{1,0:T(8,128)S(1)}, f32[512,128]{1,0:T(8,128)S(1)}, u32[]{:S(2)}, u32[]{:S(2)}) %collective-permute-start.12) | collective-permute-done | bytes 262176 | tf_op jit(solution)/shard_map/ppermute | solution.py:173
  127.7 4.4 %collective-permute-done.17 = f32[512,128]{1,0:T(8,128)S(1)} collective-permute-done((f32[512,128]{1,0:T(8,128)S(1)}, f32[512,128]{1,0:T(8,128)S(1)}, u32[]{:S(2)}, u32[]{:S(2)}) %collective-permute-start.17) | collective-permute-done | bytes 262176 | tf_op jit(solution)/shard_map/ppermute | solution.py:177
  132.5 7.4 %collective-permute-done.14 = f32[512,128]{1,0:T(8,128)S(1)} collective-permute-done((f32[512,128]{1,0:T(8,128)S(1)}, f32[512,128]{1,0:T(8,128)S(1)}, u32[]{:S(2)}, u32[]{:S(2)}) %collective-permute-start.14) | collective-permute-done | bytes 262176 | tf_op jit(solution)/shard_map/ppermute | solution.py:176
  140.9 3.6 %collective-permute-done.19 = f32[768,128]{1,0:T(8,128)S(1)} collective-permute-done((f32[768,128]{1,0:T(8,128)S(1)}, f32[768,128]{1,0:T(8,128)S(1)}, u32[]{:S(2)}, u32[]{:S(2)}) %collective-permute-start.19) | collective-permute-done | bytes 393248 | tf_op jit(solution)/shard_map/ppermute | solution.py:151
  144.6 5.1 %collective-permute-start.18 = (f32[512,128]{1,0:T(8,128)S(1)}, f32[512,128]{1,0:T(8,128)S(1)}, u32[]{:S(2)}, u32[]{:S(2)}) collective-permute-start(f32[512,128]{1,0:T(8,128)S(1)} %get-tuple-element.59), channel_id=1, source_target_pairs={{0,7},{1,0},{2,1},{3,2},{4,3},{5,4},{6,5},{7,6},{8,15},{9,8},{10,9... | collective-permute-start | bytes 786440 | tf_op jit(solution)/shard_map/ppermute | solution.py:179
  155.1 4.0 %collective-permute-done.16 = f32[512,128]{1,0:T(8,128)S(1)} collective-permute-done((f32[512,128]{1,0:T(8,128)S(1)}, f32[512,128]{1,0:T(8,128)S(1)}, u32[]{:S(2)}, u32[]{:S(2)}) %collective-permute-start.16) | collective-permute-done | bytes 262176 | tf_op jit(solution)/shard_map/ppermute | solution.py:180
  161.4 2.9 %shard_map.130 = f32[4,512,128]{2,1,0:T(8,128)S(1)} custom-call(s32[5]{0:T(128)S(1)} %pad_add_fusion.2.sc_ref, bf16[2,512,512]{2,1,0:T(8,128)(2,1)S(1)} %get-tuple-element.62.gh_ref, bf16[2,512,512]{2,1,0:T(8,128)(2,1)S(1)} %get-tuple-element.61.gl_ref, f32[2,2,4,512,128]{4,3,2,1,0:T(8,128)S(1)} %bitcast.90, f32[2,2,4,512,128]{4,3,2,1,0:T(8,128)S(1)} %bitcast.91), custom_call_target="tpu_custom_call" | custom-call | flops 1600000000 | bytes 7000000 | tf_op jit(solution)/shard_map/pallas_call | solution.py:51
  164.5 2.7 %collective-permute-start.22 = (f32[512,128]{1,0:T(8,128)S(1)}, f32[512,128]{1,0:T(8,128)S(1)}, u32[]{:S(2)}, u32[]{:S(2)}) collective-permute-start(f32[512,128]{1,0:T(8,128)S(1)} %get-tuple-element.63), channel_id=1, source_target_pairs={{0,7},{1,0},{2,1},{3,2},{4,3},{5,4},{6,5},{7,6},{8,15},{9,8},{10,9... | collective-permute-start | bytes 786440 | tf_op jit(solution)/shard_map/ppermute | solution.py:174
  167.2 2.9 %shard_map.131 = f32[4,512,128]{2,1,0:T(8,128)S(1)} custom-call(s32[5]{0:T(128)S(1)} %pad_add_fusion.3.sc_ref, bf16[2,512,512]{2,1,0:T(8,128)(2,1)S(1)} %get-tuple-element.62.gh_ref, bf16[2,512,512]{2,1,0:T(8,128)(2,1)S(1)} %get-tuple-element.61.gl_ref, f32[2,2,4,512,128]{4,3,2,1,0:T(8,128)S(1)} %bitcast.92, f32[2,2,4,512,128]{4,3,2,1,0:T(8,128)S(1)} %bitcast.93), custom_call_target="tpu_custom_call" | custom-call | flops 1600000000 | bytes 7000000 | tf_op jit(solution)/shard_map/pallas_call | solution.py:51
  171.0 3.0 %collective-permute-start.26 = (f32[512,128]{1,0:T(8,128)S(1)}, f32[512,128]{1,0:T(8,128)S(1)}, u32[]{:S(2)}, u32[]{:S(2)}) collective-permute-start(f32[512,128]{1,0:T(8,128)S(1)} %bitcast_add_fusion.2), channel_id=1, source_target_pairs={{0,7},{1,0},{2,1},{3,2},{4,3},{5,4},{6,5},{7,6},{8,15},{9,8},{10,9... | collective-permute-start | bytes 786440 | tf_op jit(solution)/shard_map/ppermute | solution.py:177
  174.0 4.5 %collective-permute-done.26 = f32[512,128]{1,0:T(8,128)S(1)} collective-permute-done((f32[512,128]{1,0:T(8,128)S(1)}, f32[512,128]{1,0:T(8,128)S(1)}, u32[]{:S(2)}, u32[]{:S(2)}) %collective-permute-start.26) | collective-permute-done | bytes 262176 | tf_op jit(solution)/shard_map/ppermute | solution.py:177
  179.4 3.2 %collective-permute-start.20 = (f32[528,256]{1,0:T(8,128)S(1)}, f32[528,256]{1,0:T(8,128)}, u32[]{:S(2)}, u32[]{:S(2)}) collective-permute-start(f32[528,256]{1,0:T(8,128)S(1)} %copy-done.34), channel_id=1, source_target_pairs={{0,8},{8,0},{1,9},{9,1},{2,10},{10,2},{3,11},{11,3},{4,12},{12,4},... | collective-permute-start | bytes 1622024 | tf_op jit(solution)/shard_map/ppermute | solution.py:189
  182.7 3.6 %collective-permute-done.23 = f32[512,128]{1,0:T(8,128)} collective-permute-done((f32[512,128]{1,0:T(8,128)S(1)}, f32[512,128]{1,0:T(8,128)}, u32[]{:S(2)}, u32[]{:S(2)}) %collective-permute-start.23) | collective-permute-done | bytes 262176 | tf_op jit(solution)/shard_map/ppermute | solution.py:176
  188.4 2.9 %collective-permute-done.20 = f32[528,256]{1,0:T(8,128)} collective-permute-done((f32[528,256]{1,0:T(8,128)S(1)}, f32[528,256]{1,0:T(8,128)}, u32[]{:S(2)}, u32[]{:S(2)}) %collective-permute-start.20) | collective-permute-done | bytes 540704 | tf_op jit(solution)/shard_map/ppermute | solution.py:189
  193.5 3.0 %collective-permute-done.24 = f32[512,128]{1,0:T(8,128)S(1)} collective-permute-done((f32[512,128]{1,0:T(8,128)S(1)}, f32[512,128]{1,0:T(8,128)S(1)}, u32[]{:S(2)}, u32[]{:S(2)}) %collective-permute-start.24) | collective-permute-done | bytes 262176 | tf_op jit(solution)/shard_map/ppermute | solution.py:178
  197.2 2.9 %collective-permute-done.27 = f32[512,128]{1,0:T(8,128)S(1)} collective-permute-done((f32[512,128]{1,0:T(8,128)S(1)}, f32[512,128]{1,0:T(8,128)S(1)}, u32[]{:S(2)}, u32[]{:S(2)}) %collective-permute-start.27) | collective-permute-done | bytes 262176 | tf_op jit(solution)/shard_map/ppermute | solution.py:179
  200.2 4.5 %collective-permute-done.25 = f32[512,128]{1,0:T(8,128)S(1)} collective-permute-done((f32[512,128]{1,0:T(8,128)S(1)}, f32[512,128]{1,0:T(8,128)S(1)}, u32[]{:S(2)}, u32[]{:S(2)}) %collective-permute-start.25) | collective-permute-done | bytes 262176 | tf_op jit(solution)/shard_map/ppermute | solution.py:180
  208.2 15.4 %all-to-all-start = ((f32[16,3,16,128]{3,2,1,0:T(8,128)}), f32[16,3,16,128]{3,2,1,0:T(8,128)S(1)}, u32[]{:S(2)}, u32[]{:S(2)}) async-start(f32[16,3,16,128]{3,2,1,0:T(8,128)} %maximum_bitcast_fusion), calls=%async_computation | async-start | bytes 786432 | tf_op jit(solution)/shard_map/all_to_all | solution.py:202
  225.2 7.0 %all-to-all-done = f32[16,3,16,128]{3,2,1,0:T(8,128)S(1)} async-done(((f32[16,3,16,128]{3,2,1,0:T(8,128)}), f32[16,3,16,128]{3,2,1,0:T(8,128)S(1)}, u32[]{:S(2)}, u32[]{:S(2)}) %all-to-all-start) | async-done | bytes 393248 | tf_op jit(solution)/shard_map/all_to_all | solution.py:202
  (191 shorter events, 56.0 us)
Async XLA Ops:
  7.2 86.6 %all-gather.5.cloned.1.call-start = ((), (), s32[]{:S(2)}) async-start(), calls=%async_computation.1 | async-start | bytes 4456448 | tf_op jit(solution)/shard_map/all_gather | solution.py:105
  13.4 12.7 %collective-permute-start = (f32[528,128]{1,0:T(8,128)S(1)}, f32[528,128]{1,0:T(8,128)S(1)}, u32[]{:S(2)}, u32[]{:S(2)}) collective-permute-start(f32[528,128]{1,0:T(8,128)S(1)} %pad_maximum_fusion.3), channel_id=1, source_target_pairs={{0,1},{1,2},{2,3},{3,4},{4,5},{5,6},{6,7},{7,0},{8,9},{9,10},{10,1... | collective-permute-start | bytes 811016 | tf_op jit(solution)/shard_map/ppermute | solution.py:115
  15.9 10.2 %collective-permute-start.1 = (f32[528,128]{1,0:T(8,128)S(1)}, f32[528,128]{1,0:T(8,128)S(1)}, u32[]{:S(2)}, u32[]{:S(2)}) collective-permute-start(f32[528,128]{1,0:T(8,128)S(1)} %pad_maximum_fusion.3), channel_id=1, source_target_pairs={{0,7},{1,0},{2,1},{3,2},{4,3},{5,4},{6,5},{7,6},{8,15},{9,8},{10,9... | collective-permute-start | bytes 811016 | tf_op jit(solution)/shard_map/ppermute | solution.py:117
  20.0 6.1 %collective-permute-start.2 = (f32[512,128]{1,0:T(8,128)S(1)}, f32[512,128]{1,0:T(8,128)S(1)}, u32[]{:S(2)}, u32[]{:S(2)}) collective-permute-start(f32[512,128]{1,0:T(8,128)S(1)} %bitcast.95), channel_id=1, source_target_pairs={{0,16},{1,48},{2,80},{3,112},{4,0},{5,32},{6,64},{7,96},{8,24},{9,... | collective-permute-start | bytes 786440 | tf_op jit(solution)/shard_map/ppermute | solution.py:110
  26.1 51.6 %copy-start.9 = (f32[528,128]{1,0:T(8,128)}, f32[528,128]{1,0:T(8,128)S(1)}, u32[]{:S(2)}) copy-start(f32[528,128]{1,0:T(8,128)S(1)} %collective-permute-done.1) | copy-start | bytes 811012
  26.8 132.4 %all-gather.7.cloned.1.call-start = ((), (), s32[]{:S(2)}) async-start(), calls=%async_computation.2 | async-start | bytes 4456448 | tf_op jit(solution)/shard_map/all_gather | solution.py:105
  26.9 40.7 %collective-permute-start.6 = (f32[2,256,2,256]{3,2,1,0:T(2,128)}, f32[2,256,2,256]{3,2,1,0:T(2,128)}, u32[]{:S(2)}, u32[]{:S(2)}) collective-permute-start(f32[2,256,2,256]{3,2,1,0:T(2,128)} %param.9), channel_id=1, source_target_pairs={{0,8},{8,0},{1,9},{9,1},{2,10},{10,2},{3,11},{11,3},{4,12},{12,4},... | collective-permute-start | bytes 3145736 | tf_op jit(solution)/shard_map/ppermute | solution.py:108
  29.3 38.3 %collective-permute-start.7 = (f32[256,128]{1,0:T(8,128)}, f32[256,128]{1,0:T(8,128)S(1)}, u32[]{:S(2)}, u32[]{:S(2)}) collective-permute-start(f32[256,128]{1,0:T(8,128)} %param.14), channel_id=1, source_target_pairs={{0,8},{8,0},{1,9},{9,1},{2,10},{10,2},{3,11},{11,3},{4,12},{12,4},... | collective-permute-start | bytes 393224 | tf_op jit(solution)/shard_map/ppermute | solution.py:109
  30.0 21.0 %collective-permute-start.3 = (f32[528,128]{1,0:T(8,128)S(1)}, f32[528,128]{1,0:T(8,128)S(1)}, u32[]{:S(2)}, u32[]{:S(2)}) collective-permute-start(f32[528,128]{1,0:T(8,128)S(1)} %collective-permute-done), channel_id=1, source_target_pairs={{0,1},{1,2},{2,3},{3,4},{4,5},{5,6},{6,7},{7,0},{8,9},{9,10},{10,1... | collective-permute-start | bytes 811016 | tf_op jit(solution)/shard_map/ppermute | solution.py:115
  30.3 22.5 %collective-permute-start.8 = (f32[528,128]{1,0:T(8,128)S(1)}, f32[528,128]{1,0:T(8,128)S(1)}, u32[]{:S(2)}, u32[]{:S(2)}) collective-permute-start(f32[528,128]{1,0:T(8,128)S(1)} %collective-permute-done.1), channel_id=1, source_target_pairs={{0,7},{1,0},{2,1},{3,2},{4,3},{5,4},{6,5},{7,6},{8,15},{9,8},{10,9... | collective-permute-start | bytes 811016 | tf_op jit(solution)/shard_map/ppermute | solution.py:117
  50.9 6.9 %collective-permute-start.4 = (f32[528,128]{1,0:T(8,128)S(1)}, f32[528,128]{1,0:T(8,128)S(1)}, u32[]{:S(2)}, u32[]{:S(2)}) collective-permute-start(f32[528,128]{1,0:T(8,128)S(1)} %collective-permute-done.3), channel_id=1, source_target_pairs={{0,1},{1,2},{2,3},{3,4},{4,5},{5,6},{6,7},{7,0},{8,9},{9,10},{10,1... | collective-permute-start | bytes 811016 | tf_op jit(solution)/shard_map/ppermute | solution.py:115
  52.8 18.1 %collective-permute-start.9 = (f32[528,128]{1,0:T(8,128)S(1)}, f32[528,128]{1,0:T(8,128)S(1)}, u32[]{:S(2)}, u32[]{:S(2)}) collective-permute-start(f32[528,128]{1,0:T(8,128)S(1)} %collective-permute-done.8), channel_id=1, source_target_pairs={{0,7},{1,0},{2,1},{3,2},{4,3},{5,4},{6,5},{7,6},{8,15},{9,8},{10,9... | collective-permute-start | bytes 811016 | tf_op jit(solution)/shard_map/ppermute | solution.py:117
  57.8 9.8 %collective-permute-start.5 = (f32[528,128]{1,0:T(8,128)S(1)}, f32[528,128]{1,0:T(8,128)S(1)}, u32[]{:S(2)}, u32[]{:S(2)}) collective-permute-start(f32[528,128]{1,0:T(8,128)S(1)} %collective-permute-done.4), channel_id=1, source_target_pairs={{0,1},{1,2},{2,3},{3,4},{4,5},{5,6},{6,7},{7,0},{8,9},{9,10},{10,1... | collective-permute-start | bytes 811016 | tf_op jit(solution)/shard_map/ppermute | solution.py:115
  71.7 14.2 %collective-permute-start.10 = (f32[512,128]{1,0:T(8,128)S(1)}, f32[512,128]{1,0:T(8,128)S(1)}, u32[]{:S(2)}, u32[]{:S(2)}) collective-permute-start(f32[512,128]{1,0:T(8,128)S(1)} %fusion.3), channel_id=1, source_target_pairs={{0,8},{8,0},{1,9},{9,1},{2,10},{10,2},{3,11},{11,3},{4,12},{12,4},... | collective-permute-start | bytes 786440 | tf_op jit(solution)/shard_map/ppermute | solution.py:147
  87.0 14.9 %collective-permute-start.11 = (f32[512,128]{1,0:T(8,128)}, f32[512,128]{1,0:T(8,128)}, u32[]{:S(2)}, u32[]{:S(2)}) collective-permute-start(f32[512,128]{1,0:T(8,128)} %fusion.11), channel_id=1, source_target_pairs={{0,16},{1,48},{2,80},{3,112},{4,0},{5,32},{6,64},{7,96},{8,24},{9,... | collective-permute-start | bytes 786440 | tf_op jit(solution)/shard_map/ppermute | solution.py:149
  103.2 20.8 %collective-permute-start.12 = (f32[512,128]{1,0:T(8,128)S(1)}, f32[512,128]{1,0:T(8,128)S(1)}, u32[]{:S(2)}, u32[]{:S(2)}) collective-permute-start(f32[512,128]{1,0:T(8,128)S(1)} %get-tuple-element.66), channel_id=1, source_target_pairs={{0,1},{1,2},{2,3},{3,4},{4,5},{5,6},{6,7},{7,0},{8,9},{9,10},{10,1... | collective-permute-start | bytes 786440 | tf_op jit(solution)/shard_map/ppermute | solution.py:173
  104.4 19.7 %collective-permute-start.13 = (f32[512,128]{1,0:T(8,128)S(1)}, f32[512,128]{1,0:T(8,128)S(1)}, u32[]{:S(2)}, u32[]{:S(2)}) collective-permute-start(f32[512,128]{1,0:T(8,128)S(1)} %get-tuple-element.65), channel_id=1, source_target_pairs={{0,7},{1,0},{2,1},{3,2},{4,3},{5,4},{6,5},{7,6},{8,15},{9,8},{10,9... | collective-permute-start | bytes 786440 | tf_op jit(solution)/shard_map/ppermute | solution.py:174
  125.2 7.0 %collective-permute-start.17 = (f32[512,128]{1,0:T(8,128)S(1)}, f32[512,128]{1,0:T(8,128)S(1)}, u32[]{:S(2)}, u32[]{:S(2)}) collective-permute-start(f32[512,128]{1,0:T(8,128)S(1)} %bitcast_add_fusion.8), channel_id=1, source_target_pairs={{0,7},{1,0},{2,1},{3,2},{4,3},{5,4},{6,5},{7,6},{8,15},{9,8},{10,9... | collective-permute-start | bytes 786440 | tf_op jit(solution)/shard_map/ppermute | solution.py:177
  132.2 7.7 %collective-permute-start.14 = (f32[512,128]{1,0:T(8,128)S(1)}, f32[512,128]{1,0:T(8,128)S(1)}, u32[]{:S(2)}, u32[]{:S(2)}) collective-permute-start(f32[512,128]{1,0:T(8,128)S(1)} %get-tuple-element.60), channel_id=1, source_target_pairs={{0,1},{1,2},{2,3},{3,4},{4,5},{5,6},{6,7},{7,0},{8,9},{9,10},{10,1... | collective-permute-start | bytes 786440 | tf_op jit(solution)/shard_map/ppermute | solution.py:176
  132.4 12.2 %collective-permute-start.19 = (f32[768,128]{1,0:T(8,128)S(1)}, f32[768,128]{1,0:T(8,128)S(1)}, u32[]{:S(2)}, u32[]{:S(2)}) collective-permute-start(f32[768,128]{1,0:T(8,128)S(1)} %pad_maximum_fusion.2), channel_id=1, source_target_pairs={{0,1},{1,0},{2,3},{3,2},{4,5},{5,4},{6,7},{7,6},{8,9},{9,8},{10,11... | collective-permute-start | bytes 1179656 | tf_op jit(solution)/shard_map/ppermute | solution.py:151
  139.9 10.2 %collective-permute-start.15 = (f32[512,128]{1,0:T(8,128)S(1)}, f32[512,128]{1,0:T(8,128)S(1)}, u32[]{:S(2)}, u32[]{:S(2)}) collective-permute-start(f32[512,128]{1,0:T(8,128)S(1)} %bitcast_add_fusion.10), channel_id=1, source_target_pairs={{0,1},{1,2},{2,3},{3,4},{4,5},{5,6},{6,7},{7,0},{8,9},{9,10},{10,1... | collective-permute-start | bytes 786440 | tf_op jit(solution)/shard_map/ppermute | solution.py:178
  144.6 10.5 %collective-permute-start.18 = (f32[512,128]{1,0:T(8,128)S(1)}, f32[512,128]{1,0:T(8,128)S(1)}, u32[]{:S(2)}, u32[]{:S(2)}) collective-permute-start(f32[512,128]{1,0:T(8,128)S(1)} %get-tuple-element.59), channel_id=1, source_target_pairs={{0,7},{1,0},{2,1},{3,2},{4,3},{5,4},{6,5},{7,6},{8,15},{9,8},{10,9... | collective-permute-start | bytes 786440 | tf_op jit(solution)/shard_map/ppermute | solution.py:179
  150.2 8.9 %collective-permute-start.16 = (f32[512,128]{1,0:T(8,128)S(1)}, f32[512,128]{1,0:T(8,128)S(1)}, u32[]{:S(2)}, u32[]{:S(2)}) collective-permute-start(f32[512,128]{1,0:T(8,128)S(1)} %bitcast_add_fusion.9), channel_id=1, source_target_pairs={{0,1},{1,2},{2,3},{3,4},{4,5},{5,6},{6,7},{7,0},{8,9},{9,10},{10,1... | collective-permute-start | bytes 786440 | tf_op jit(solution)/shard_map/ppermute | solution.py:180
  164.4 6.5 %collective-permute-start.21 = (f32[512,128]{1,0:T(8,128)S(1)}, f32[512,128]{1,0:T(8,128)S(1)}, u32[]{:S(2)}, u32[]{:S(2)}) collective-permute-start(f32[512,128]{1,0:T(8,128)S(1)} %get-tuple-element.64), channel_id=1, source_target_pairs={{0,1},{1,2},{2,3},{3,4},{4,5},{5,6},{6,7},{7,0},{8,9},{9,10},{10,1... | collective-permute-start | bytes 786440 | tf_op jit(solution)/shard_map/ppermute | solution.py:173
  164.5 6.4 %collective-permute-start.22 = (f32[512,128]{1,0:T(8,128)S(1)}, f32[512,128]{1,0:T(8,128)S(1)}, u32[]{:S(2)}, u32[]{:S(2)}) collective-permute-start(f32[512,128]{1,0:T(8,128)S(1)} %get-tuple-element.63), channel_id=1, source_target_pairs={{0,7},{1,0},{2,1},{3,2},{4,3},{5,4},{6,5},{7,6},{8,15},{9,8},{10,9... | collective-permute-start | bytes 786440 | tf_op jit(solution)/shard_map/ppermute | solution.py:174
  171.0 7.5 %collective-permute-start.26 = (f32[512,128]{1,0:T(8,128)S(1)}, f32[512,128]{1,0:T(8,128)S(1)}, u32[]{:S(2)}, u32[]{:S(2)}) collective-permute-start(f32[512,128]{1,0:T(8,128)S(1)} %bitcast_add_fusion.2), channel_id=1, source_target_pairs={{0,7},{1,0},{2,1},{3,2},{4,3},{5,4},{6,5},{7,6},{8,15},{9,8},{10,9... | collective-permute-start | bytes 786440 | tf_op jit(solution)/shard_map/ppermute | solution.py:177
  179.3 7.0 %collective-permute-start.23 = (f32[512,128]{1,0:T(8,128)S(1)}, f32[512,128]{1,0:T(8,128)}, u32[]{:S(2)}, u32[]{:S(2)}) collective-permute-start(f32[512,128]{1,0:T(8,128)S(1)} %get-tuple-element.58), channel_id=1, source_target_pairs={{0,1},{1,2},{2,3},{3,4},{4,5},{5,6},{6,7},{7,0},{8,9},{9,10},{10,1... | collective-permute-start | bytes 786440 | tf_op jit(solution)/shard_map/ppermute | solution.py:176
  179.4 11.8 %collective-permute-start.20 = (f32[528,256]{1,0:T(8,128)S(1)}, f32[528,256]{1,0:T(8,128)}, u32[]{:S(2)}, u32[]{:S(2)}) collective-permute-start(f32[528,256]{1,0:T(8,128)S(1)} %copy-done.34), channel_id=1, source_target_pairs={{0,8},{8,0},{1,9},{9,1},{2,10},{10,2},{3,11},{11,3},{4,12},{12,4},... | collective-permute-start | bytes 1622024 | tf_op jit(solution)/shard_map/ppermute | solution.py:189
  187.3 9.2 %collective-permute-start.24 = (f32[512,128]{1,0:T(8,128)S(1)}, f32[512,128]{1,0:T(8,128)S(1)}, u32[]{:S(2)}, u32[]{:S(2)}) collective-permute-start(f32[512,128]{1,0:T(8,128)S(1)} %bitcast_add_fusion.4), channel_id=1, source_target_pairs={{0,1},{1,2},{2,3},{3,4},{4,5},{5,6},{6,7},{7,0},{8,9},{9,10},{10,1... | collective-permute-start | bytes 786440 | tf_op jit(solution)/shard_map/ppermute | solution.py:178
  191.4 8.8 %collective-permute-start.27 = (f32[512,128]{1,0:T(8,128)S(1)}, f32[512,128]{1,0:T(8,128)S(1)}, u32[]{:S(2)}, u32[]{:S(2)}) collective-permute-start(f32[512,128]{1,0:T(8,128)S(1)} %copy-done.36), channel_id=1, source_target_pairs={{0,7},{1,0},{2,1},{3,2},{4,3},{5,4},{6,5},{7,6},{8,15},{9,8},{10,9... | collective-permute-start | bytes 786440 | tf_op jit(solution)/shard_map/ppermute | solution.py:179
  196.5 8.2 %collective-permute-start.25 = (f32[512,128]{1,0:T(8,128)S(1)}, f32[512,128]{1,0:T(8,128)S(1)}, u32[]{:S(2)}, u32[]{:S(2)}) collective-permute-start(f32[512,128]{1,0:T(8,128)S(1)} %bitcast_add_fusion.3), channel_id=1, source_target_pairs={{0,1},{1,2},{2,3},{3,4},{4,5},{5,6},{6,7},{7,0},{8,9},{9,10},{10,1... | collective-permute-start | bytes 786440 | tf_op jit(solution)/shard_map/ppermute | solution.py:180
  208.2 24.0 %all-to-all-start = ((f32[16,3,16,128]{3,2,1,0:T(8,128)}), f32[16,3,16,128]{3,2,1,0:T(8,128)S(1)}, u32[]{:S(2)}, u32[]{:S(2)}) async-start(f32[16,3,16,128]{3,2,1,0:T(8,128)} %maximum_bitcast_fusion), calls=%async_computation | async-start | bytes 786432 | tf_op jit(solution)/shard_map/all_to_all | solution.py:202
  (45 other events, 541.1 us)
Sparse Core Ops, SparseCore 0:
  26.9 65.9 all-gather.4
  102.1 55.2 all-gather.6

commit v8 on v7

--- a/solution.py
+++ b/solution.py
@@ -23,19 +23,20 @@
     return f(a[0], b[0]) + (f(a[0], b[1]) + f(a[1], b[0]))
 
 
-def pair_kernel(sc_ref, gh_ref, gl_ref, a_ref, b_ref, out_ref):
+def pair_kernel(sc_ref, *refs):
+    g_refs, (a_ref, b_ref, out_ref) = refs[:4], refs[4:]
     h = sc_ref[0]
     acc = None
     for k in range(2):
         half = h if k == 0 else 1 - h
         cols = jnp.concatenate([a_ref[half, 0, 0], b_ref[half, 0, 0]], axis=1)
-        term = dot3((gh_ref[k], gl_ref[k]), split(cols))
+        term = dot3((g_refs[2 * k][...], g_refs[2 * k + 1][...]), split(cols))
         acc = term if acc is None else acc + term
     out_ref[0] = -acc[:, :128]
     out_ref[1] = -acc[:, 128:]
 
 
-WHOLE_G = pl.BlockSpec((2, 512, 512), lambda i, sc: (0, 0, 0))
+WHOLE_G = pl.BlockSpec((512, 512), lambda i, sc: (0, 0))
 PARAMS = pltpu.CompilerParams(vmem_limit_bytes=40 * 2**20)
 
 
@@ -47,13 +48,13 @@
     return pl.BlockSpec((2, 1, 1, 512, 128), place)
 
 
-def product(scalars, g_hi, g_lo, gathered):
+def product(scalars, g_parts, gathered):
     return pl.pallas_call(
         pair_kernel,
         grid_spec=pltpu.PrefetchScalarGridSpec(
             num_scalar_prefetch=1,
             grid=(2,),
-            in_specs=[WHOLE_G, WHOLE_G, slot_rows(1), slot_rows(2)],
+            in_specs=[WHOLE_G] * 4 + [slot_rows(1), slot_rows(2)],
             out_specs=pl.BlockSpec((2, 512, 128), lambda i, sc: (i, 0, 0)),
         ),
         out_shape=jax.ShapeDtypeStruct((4, 512, 128), jnp.float32),
@@ -61,7 +62,7 @@
         cost_estimate=pl.CostEstimate(
             flops=1_600_000_000, bytes_accessed=7_000_000, transcendentals=0
         ),
-    )(scalars, g_hi, g_lo, gathered, gathered)
+    )(scalars, *g_parts, gathered, gathered)
 
 
 def chip_and_core(shift):
@@ -116,16 +117,13 @@
         if d < 4:
             left = lax.ppermute(left, "z", ring(8, -1))
             if d == 1:
-                right, left, near_one = lax.optimization_barrier((right, left, near_one))
+                right, left, near_one, lp_far = lax.optimization_barrier(
+                    (right, left, near_one, lp_far)
+                )
             pieces[d] = left
         pieces[-d] = right
-    pieces[-4], g_other, lp_far = lax.optimization_barrier((right, g_other, lp_far))
+    pieces[-4], g_other = lax.optimization_barrier((right, g_other))
     gathered_one = gather(near_one)
-
-    g = jnp.stack([g_top, g_other]).reshape(2, 512, 512)
-    g_hi32 = lax.reduce_precision(g, 8, 7)
-    g_hi = g_hi32.astype(jnp.bfloat16)
-    g_lo = (g - g_hi32).astype(jnp.bfloat16)
 
     def fetch(super_index):
         parts = []
@@ -146,7 +144,15 @@
     by_lp = lambda cols, lp: jnp.dot(cols[:512], lp, precision=lax.Precision.HIGH)
     from_far = lax.ppermute(by_lp(par_there, lp_far), "y_hi", ring(2, 1))
     folded = two - jnp.where(here, by_lp(par_here, lp_two), from_far)
+    folded, g_other = lax.optimization_barrier((folded, g_other))
     near_two = lax.ppermute(folded, ALL_AXES, spread_pairs())
+
+    g_parts = []
+    for g in (g_top, g_other):
+        g = g.reshape(512, 512)
+        g_hi = lax.reduce_precision(g, 8, 7)
+        g_parts += [g_hi.astype(jnp.bfloat16), (g - g_hi).astype(jnp.bfloat16)]
+
     two_sent = jnp.concatenate([two, lp_two])
     two_next = lax.ppermute(two_sent, "z", [(i, i ^ 1) for i in range(8)])
     own_two = pair_up(two, two_next[:512])
@@ -159,7 +165,7 @@
             chip, core = chip_and_core((z - slots[:, None] - both[None, :]) % 8)
             codes = chip // 2 * 4 + chip % 2 * 2 + core
             scalars = jnp.concatenate([after[None], codes.reshape(4)]).astype(jnp.int32)
-            return product(scalars, g_hi, g_lo, gathered)
+            return product(scalars, g_parts, gathered)
 
         early = part((z + 4) // 2, after)
         after, early = lax.optimization_barrier((after, early))

time: 241 us -> 237 us (0.983)
  waiting for transfers between devices: 74.2 us -> 81.6 us
  local copies, waits for them, and re-layouts: 17.4 us -> 10.1 us
  starting transfers between devices: 91.9 us -> 88.3 us
    another operation x3 -> x0, local copies, waits for them, and re-layouts: 7.52 us -> none  [local(): g = jnp.stack([g_top, g_other]).reshape(2, 512, 512)]
    ppermute x2, starting transfers between devices: 16.2 us -> 8.83 us  [sum_over_z(): down = lax.ppermute(term(-3), 'z', ring(8, -1))]
    all_gather x2, waiting for transfers between devices: 0.02 us -> 6.34 us  [gather(): rows = lax.all_gather(piece, ROW_AXES, axis=0, tiled=False)]
    ppermute x1, waiting for transfers between devices: 7.91 us -> 13.6 us  [local(): from_far = lax.ppermute(by_lp(par_there, lp_far), 'y_hi', ring(2, 1))]
    ppermute x1, waiting for transfers between devices: 0.01 us -> 5.62 us  [local(): lp_far = lax.ppermute(lp_two, 'y_hi', ring(2, 1))]
    ppermute x2, waiting for transfers between devices: 11 us -> 5.68 us  [sum_over_z(): up = lax.ppermute(up + term(3), 'z', ring(8, 1))]
    ppermute x3, starting transfers between devices: 22.6 us -> 17.4 us  [local(): left = lax.ppermute(left, 'z', ring(8, -1))]
    ppermute x2, starting transfers between devices: 7.18 us -> 2.81 us  [sum_over_z(): down = lax.ppermute(down + term(-1), 'z', ring(8, -1))]
  transfers between devices with their start and end apart: 31 -> 31, of which waited for: 18 -> 20; matrix products, arithmetic and copies ran while one was open for 11% -> 8% of each run, Pallas kernels for 4% -> 4%
where the time goes in v8:
time: 237 us; the launch traced here: 236 us
  starting transfers between devices  88.3 us (37%)
  waiting for transfers between devices  81.6 us (34%)
  between operations  20.7 us (9%)
  other arithmetic  18.2 us (8%)
  Pallas kernels  11.6 us (5%)
  local copies, waits for them, and re-layouts  10.1 us (4%)
  matrix products  5.65 us (2%)
    ppermute x3, starting transfers between devices, local(): left = lax.ppermute(left, 'z', ring(8, -1))  17.4 us
    all_to_all x1, starting transfers between devices, local(): sums = jnp.sum(lax.all_to_all(terms, ROW_AXES, 0, 0), axis=0)  16.8 us
    ppermute x1, waiting for transfers between devices, local(): from_far = lax.ppermute(by_lp(par_there, lp_far), 'y_hi', ring(2, 1))  13.6 us
    pallas_call x4, Pallas kernels, product(): pl.pallas_call(pair_kernel, grid_spec=pltpu.PrefetchScalarGridSpec(num_sc...  11.6 us
    ppermute x2, waiting for transfers between devices, sum_over_z(): return lax.ppermute(up + term(1), 'z', ring(8, 1)) + down + term(0)  9.23 us
    ppermute x4, waiting for transfers between devices, local(): right = lax.ppermute(right, 'z', ring(8, 1))  9.06 us
    ppermute x2, starting transfers between devices, sum_over_z(): down = lax.ppermute(term(-3), 'z', ring(8, -1))  8.83 us
    unnamed x66, local copies, waits for them, and re-layouts  7.79 us
  transfers between devices with their start and end apart: 31, of which 20 were waited for; matrix products, arithmetic and copies ran while one was open for 8% of the time, Pallas kernels for 4%

profile of v8, /device:TPU:1, one launch (start us, length us, event | category | flops | bytes accessed | tf_op | source)
XLA Modules:
  0.0 236.1 jit_solution(2621485039822180803)
XLA Ops:
  13.4 2.5 %collective-permute-start = (f32[528,128]{1,0:T(8,128)S(1)}, f32[528,128]{1,0:T(8,128)S(1)}, u32[]{:S(2)}, u32[]{:S(2)}) collective-permute-start(f32[528,128]{1,0:T(8,128)S(1)} %pad_maximum_fusion.3), channel_id=1, source_target_pairs={{0,1},{1,2},{2,3},{3,4},{4,5},{5,6},{6,7},{7,0},{8,9},{9,10},{10,1... | collective-permute-start | bytes 811016 | tf_op jit(solution)/shard_map/ppermute | solution.py:116
  15.9 4.0 %collective-permute-start.1 = (f32[528,128]{1,0:T(8,128)S(1)}, f32[528,128]{1,0:T(8,128)S(1)}, u32[]{:S(2)}, u32[]{:S(2)}) collective-permute-start(f32[528,128]{1,0:T(8,128)S(1)} %pad_maximum_fusion.3), channel_id=1, source_target_pairs={{0,7},{1,0},{2,1},{3,2},{4,3},{5,4},{6,5},{7,6},{8,15},{9,8},{10,9... | collective-permute-start | bytes 811016 | tf_op jit(solution)/shard_map/ppermute | solution.py:118
  22.4 2.7 %collective-permute-start.3 = (f32[256,128]{1,0:T(8,128)}, f32[256,128]{1,0:T(8,128)S(1)}, u32[]{:S(2)}, u32[]{:S(2)}) collective-permute-start(f32[256,128]{1,0:T(8,128)} %param.14), channel_id=1, source_target_pairs={{0,8},{8,0},{1,9},{9,1},{2,10},{10,2},{3,11},{11,3},{4,12},{12,4},... | collective-permute-start | bytes 393224 | tf_op jit(solution)/shard_map/ppermute | solution.py:110
  25.1 5.6 %collective-permute-done.3 = f32[256,128]{1,0:T(8,128)S(1)} collective-permute-done((f32[256,128]{1,0:T(8,128)}, f32[256,128]{1,0:T(8,128)S(1)}, u32[]{:S(2)}, u32[]{:S(2)}) %collective-permute-start.3) | collective-permute-done | bytes 131104 | tf_op jit(solution)/shard_map/ppermute | solution.py:110
  31.5 3.7 %collective-permute-start.7 = (f32[2,256,2,256]{3,2,1,0:T(2,128)}, f32[2,256,2,256]{3,2,1,0:T(2,128)}, u32[]{:S(2)}, u32[]{:S(2)}) collective-permute-start(f32[2,256,2,256]{3,2,1,0:T(2,128)} %param.9), channel_id=1, source_target_pairs={{0,8},{8,0},{1,9},{9,1},{2,10},{10,2},{3,11},{11,3},{4,12},{12,4},... | collective-permute-start | bytes 3145736 | tf_op jit(solution)/shard_map/ppermute | solution.py:109
  35.5 10.6 %collective-permute-start.8 = (f32[528,128]{1,0:T(8,128)S(1)}, f32[528,128]{1,0:T(8,128)S(1)}, u32[]{:S(2)}, u32[]{:S(2)}) collective-permute-start(f32[528,128]{1,0:T(8,128)S(1)} %collective-permute-done.1), channel_id=1, source_target_pairs={{0,7},{1,0},{2,1},{3,2},{4,3},{5,4},{6,5},{7,6},{8,15},{9,8},{10,9... | collective-permute-start | bytes 811016 | tf_op jit(solution)/shard_map/ppermute | solution.py:118
  46.1 4.9 %collective-permute-done.4 = f32[528,128]{1,0:T(8,128)S(1)} collective-permute-done((f32[528,128]{1,0:T(8,128)S(1)}, f32[528,128]{1,0:T(8,128)S(1)}, u32[]{:S(2)}, u32[]{:S(2)}) %collective-permute-start.4) | collective-permute-done | bytes 270368 | tf_op jit(solution)/shard_map/ppermute | solution.py:116
  51.2 2.7 %collective-permute-start.9 = (f32[528,128]{1,0:T(8,128)S(1)}, f32[528,128]{1,0:T(8,128)S(1)}, u32[]{:S(2)}, u32[]{:S(2)}) collective-permute-start(f32[528,128]{1,0:T(8,128)S(1)} %collective-permute-done.8), channel_id=1, source_target_pairs={{0,7},{1,0},{2,1},{3,2},{4,3},{5,4},{6,5},{7,6},{8,15},{9,8},{10,9... | collective-permute-start | bytes 811016 | tf_op jit(solution)/shard_map/ppermute | solution.py:118
  54.0 4.1 %collective-permute-done.5 = f32[528,128]{1,0:T(8,128)S(1)} collective-permute-done((f32[528,128]{1,0:T(8,128)S(1)}, f32[528,128]{1,0:T(8,128)S(1)}, u32[]{:S(2)}, u32[]{:S(2)}) %collective-permute-start.5) | collective-permute-done | bytes 270368 | tf_op jit(solution)/shard_map/ppermute | solution.py:116
  66.0 13.6 %collective-permute-done.10 = f32[512,128]{1,0:T(8,128)S(1)} collective-permute-done((f32[512,128]{1,0:T(8,128)S(1)}, f32[512,128]{1,0:T(8,128)S(1)}, u32[]{:S(2)}, u32[]{:S(2)}) %collective-permute-start.10) | collective-permute-done | bytes 262176 | tf_op jit(solution)/shard_map/ppermute | solution.py:145
  82.0 7.2 %collective-permute-start.11 = (f32[512,128]{1,0:T(8,128)}, f32[512,128]{1,0:T(8,128)}, u32[]{:S(2)}, u32[]{:S(2)}) collective-permute-start(f32[512,128]{1,0:T(8,128)} %fusion.12), channel_id=1, source_target_pairs={{0,16},{1,48},{2,80},{3,112},{4,0},{5,32},{6,64},{7,96},{8,24},{9,... | collective-permute-start | bytes 786440 | tf_op jit(solution)/shard_map/ppermute | solution.py:148
  89.6 2.9 %all-gather.5.cloned.1.call-done = f32[8192,128]{1,0:T(8,128)} async-done(((f32[512,128]{1,0:T(8,128)}), f32[8192,128]{1,0:T(8,128)}) %all-gather.5.cloned.1.call-update) | async-done | bytes 4194320 | tf_op jit(solution)/shard_map/all_gather | solution.py:106
  94.7 2.9 %shard_map.128 = f32[4,512,128]{2,1,0:T(8,128)S(1)} custom-call(s32[5]{0:T(128)S(1)} %pad_add_fusion.sc_ref, bf16[512,512]{1,0:T(8,128)(2,1)S(1)} %get-tuple-element.72.refs_0_, bf16[512,512]{1,0:T(8,128)(2,1)S(1)} %get-tuple-element.71.refs_1_, bf16[512,512]{1,0:T(8,128)(2,1)S(1)} %get-tuple-element.82.refs_2_, ...), custom_call_target="tpu_custom_call" | custom-call | flops 1600000000 | bytes 7000000 | tf_op jit(solution)/shard_map/pallas_call | solution.py:52
  97.7 2.9 %shard_map.129 = f32[4,512,128]{2,1,0:T(8,128)S(1)} custom-call(s32[5]{0:T(128)S(1)} %pad_add_fusion.1.sc_ref, bf16[512,512]{1,0:T(8,128)(2,1)S(1)} %get-tuple-element.72.refs_0_, bf16[512,512]{1,0:T(8,128)(2,1)S(1)} %get-tuple-element.71.refs_1_, bf16[512,512]{1,0:T(8,128)(2,1)S(1)} %get-tuple-element.82.refs_2_, ...), custom_call_target="tpu_custom_call" | custom-call | flops 1600000000 | bytes 7000000 | tf_op jit(solution)/shard_map/pallas_call | solution.py:52
  101.9 3.4 %collective-permute-start.12 = (f32[512,128]{1,0:T(8,128)S(1)}, f32[512,128]{1,0:T(8,128)S(1)}, u32[]{:S(2)}, u32[]{:S(2)}) collective-permute-start(f32[512,128]{1,0:T(8,128)S(1)} %get-tuple-element.68), channel_id=1, source_target_pairs={{0,1},{1,2},{2,3},{3,4},{4,5},{5,6},{6,7},{7,0},{8,9},{9,10},{10,1... | collective-permute-start | bytes 786440 | tf_op jit(solution)/shard_map/ppermute | solution.py:179
  105.3 7.0 %collective-permute-start.13 = (f32[512,128]{1,0:T(8,128)S(1)}, f32[512,128]{1,0:T(8,128)S(1)}, u32[]{:S(2)}, u32[]{:S(2)}) collective-permute-start(f32[512,128]{1,0:T(8,128)S(1)} %get-tuple-element.67), channel_id=1, source_target_pairs={{0,7},{1,0},{2,1},{3,2},{4,3},{5,4},{6,5},{7,6},{8,15},{9,8},{10,9... | collective-permute-start | bytes 786440 | tf_op jit(solution)/shard_map/ppermute | solution.py:180
  112.3 3.7 %collective-permute-done.12 = f32[512,128]{1,0:T(8,128)S(1)} collective-permute-done((f32[512,128]{1,0:T(8,128)S(1)}, f32[512,128]{1,0:T(8,128)S(1)}, u32[]{:S(2)}, u32[]{:S(2)}) %collective-permute-start.12) | collective-permute-done | bytes 262176 | tf_op jit(solution)/shard_map/ppermute | solution.py:179
  117.1 2.8 %collective-permute-start.17 = (f32[512,128]{1,0:T(8,128)S(1)}, f32[512,128]{1,0:T(8,128)S(1)}, u32[]{:S(2)}, u32[]{:S(2)}) collective-permute-start(f32[512,128]{1,0:T(8,128)S(1)} %bitcast_add_fusion.8), channel_id=1, source_target_pairs={{0,7},{1,0},{2,1},{3,2},{4,3},{5,4},{6,5},{7,6},{8,15},{9,8},{10,9... | collective-permute-start | bytes 786440 | tf_op jit(solution)/shard_map/ppermute | solution.py:183
  119.9 3.3 %collective-permute-done.17 = f32[512,128]{1,0:T(8,128)S(1)} collective-permute-done((f32[512,128]{1,0:T(8,128)S(1)}, f32[512,128]{1,0:T(8,128)S(1)}, u32[]{:S(2)}, u32[]{:S(2)}) %collective-permute-start.17) | collective-permute-done | bytes 262176 | tf_op jit(solution)/shard_map/ppermute | solution.py:183
  126.7 2.6 %collective-permute-start.19 = (f32[768,128]{1,0:T(8,128)S(1)}, f32[768,128]{1,0:T(8,128)S(1)}, u32[]{:S(2)}, u32[]{:S(2)}) collective-permute-start(f32[768,128]{1,0:T(8,128)S(1)} %pad_maximum_fusion.2), channel_id=1, source_target_pairs={{0,1},{1,0},{2,3},{3,2},{4,5},{5,4},{6,7},{7,6},{8,9},{9,8},{10,11... | collective-permute-start | bytes 1179656 | tf_op jit(solution)/shard_map/ppermute | solution.py:157
  134.4 4.0 %collective-permute-done.19 = f32[768,128]{1,0:T(8,128)S(1)} collective-permute-done((f32[768,128]{1,0:T(8,128)S(1)}, f32[768,128]{1,0:T(8,128)S(1)}, u32[]{:S(2)}, u32[]{:S(2)}) %collective-permute-start.19) | collective-permute-done | bytes 393248 | tf_op jit(solution)/shard_map/ppermute | solution.py:157
  138.9 5.1 %collective-permute-done.15 = f32[512,128]{1,0:T(8,128)S(1)} collective-permute-done((f32[512,128]{1,0:T(8,128)S(1)}, f32[512,128]{1,0:T(8,128)S(1)}, u32[]{:S(2)}, u32[]{:S(2)}) %collective-permute-start.15) | collective-permute-done | bytes 262176 | tf_op jit(solution)/shard_map/ppermute | solution.py:184
  150.7 3.4 %all-gather.7.cloned.1.call-done = f32[8192,128]{1,0:T(8,128)} async-done(((f32[512,128]{1,0:T(8,128)}), f32[8192,128]{1,0:T(8,128)}) %all-gather.7.cloned.1.call-update) | async-done | bytes 4194320 | tf_op jit(solution)/shard_map/all_gather | solution.py:106
  156.3 2.9 %shard_map.130 = f32[4,512,128]{2,1,0:T(8,128)S(1)} custom-call(s32[5]{0:T(128)S(1)} %pad_add_fusion.2.sc_ref, bf16[512,512]{1,0:T(8,128)(2,1)S(1)} %get-tuple-element.72.refs_0_, bf16[512,512]{1,0:T(8,128)(2,1)S(1)} %get-tuple-element.71.refs_1_, bf16[512,512]{1,0:T(8,128)(2,1)S(1)} %get-tuple-element.82.refs_2_, ...), custom_call_target="tpu_custom_call" | custom-call | flops 1600000000 | bytes 7000000 | tf_op jit(solution)/shard_map/pallas_call | solution.py:52
  162.5 2.9 %shard_map.131 = f32[4,512,128]{2,1,0:T(8,128)S(1)} custom-call(s32[5]{0:T(128)S(1)} %pad_add_fusion.3.sc_ref, bf16[512,512]{1,0:T(8,128)(2,1)S(1)} %get-tuple-element.72.refs_0_, bf16[512,512]{1,0:T(8,128)(2,1)S(1)} %get-tuple-element.71.refs_1_, bf16[512,512]{1,0:T(8,128)(2,1)S(1)} %get-tuple-element.82.refs_2_, ...), custom_call_target="tpu_custom_call" | custom-call | flops 1600000000 | bytes 7000000 | tf_op jit(solution)/shard_map/pallas_call | solution.py:52
  166.2 2.8 %collective-permute-start.26 = (f32[512,128]{1,0:T(8,128)S(1)}, f32[512,128]{1,0:T(8,128)S(1)}, u32[]{:S(2)}, u32[]{:S(2)}) collective-permute-start(f32[512,128]{1,0:T(8,128)S(1)} %bitcast_add_fusion.2), channel_id=1, source_target_pairs={{0,7},{1,0},{2,1},{3,2},{4,3},{5,4},{6,5},{7,6},{8,15},{9,8},{10,9... | collective-permute-start | bytes 786440 | tf_op jit(solution)/shard_map/ppermute | solution.py:183
  169.0 3.7 %collective-permute-done.26 = f32[512,128]{1,0:T(8,128)S(1)} collective-permute-done((f32[512,128]{1,0:T(8,128)S(1)}, f32[512,128]{1,0:T(8,128)S(1)}, u32[]{:S(2)}, u32[]{:S(2)}) %collective-permute-start.26) | collective-permute-done | bytes 262176 | tf_op jit(solution)/shard_map/ppermute | solution.py:183
  177.1 3.7 %collective-permute-done.23 = f32[512,128]{1,0:T(8,128)} collective-permute-done((f32[512,128]{1,0:T(8,128)}, f32[512,128]{1,0:T(8,128)}, u32[]{:S(2)}, u32[]{:S(2)}) %collective-permute-start.23) | collective-permute-done | bytes 262176 | tf_op jit(solution)/shard_map/ppermute | solution.py:182
  183.1 2.4 %collective-permute-done.20 = f32[528,256]{1,0:T(8,128)} collective-permute-done((f32[528,256]{1,0:T(8,128)}, f32[528,256]{1,0:T(8,128)}, u32[]{:S(2)}, u32[]{:S(2)}) %collective-permute-start.20) | collective-permute-done | bytes 540704 | tf_op jit(solution)/shard_map/ppermute | solution.py:195
  191.6 7.5 %collective-permute-done.25 = f32[512,128]{1,0:T(8,128)S(1)} collective-permute-done((f32[512,128]{1,0:T(8,128)S(1)}, f32[512,128]{1,0:T(8,128)S(1)}, u32[]{:S(2)}, u32[]{:S(2)}) %collective-permute-start.25) | collective-permute-done | bytes 262176 | tf_op jit(solution)/shard_map/ppermute | solution.py:186
  202.6 16.8 %all-to-all-start = ((f32[16,3,16,128]{3,2,1,0:T(8,128)}), f32[16,3,16,128]{3,2,1,0:T(8,128)S(1)}, u32[]{:S(2)}, u32[]{:S(2)}) async-start(f32[16,3,16,128]{3,2,1,0:T(8,128)} %maximum_bitcast_fusion), calls=%async_computation | async-start | bytes 786432 | tf_op jit(solution)/shard_map/all_to_all | solution.py:208
  221.6 6.4 %all-to-all-done = f32[16,3,16,128]{3,2,1,0:T(8,128)S(1)} async-done(((f32[16,3,16,128]{3,2,1,0:T(8,128)}), f32[16,3,16,128]{3,2,1,0:T(8,128)S(1)}, u32[]{:S(2)}, u32[]{:S(2)}) %all-to-all-start) | async-done | bytes 393248 | tf_op jit(solution)/shard_map/all_to_all | solution.py:208
  (161 shorter events, 60.6 us)
Async XLA Ops:
  7.2 57.5 %copy-start.24 = (f32[16,128]{1,0:T(8,128)S(1)}, f32[16,128]{1,0:T(8,128)}, u32[]{:S(2)}) copy-start(f32[16,128]{1,0:T(8,128)} %param.12) | copy-start | bytes 24580
  7.2 85.3 %all-gather.5.cloned.1.call-start = ((), (), s32[]{:S(2)}) async-start(), calls=%async_computation.1 | async-start | bytes 4456448 | tf_op jit(solution)/shard_map/all_gather | solution.py:106
  13.4 17.3 %collective-permute-start = (f32[528,128]{1,0:T(8,128)S(1)}, f32[528,128]{1,0:T(8,128)S(1)}, u32[]{:S(2)}, u32[]{:S(2)}) collective-permute-start(f32[528,128]{1,0:T(8,128)S(1)} %pad_maximum_fusion.3), channel_id=1, source_target_pairs={{0,1},{1,2},{2,3},{3,4},{4,5},{5,6},{6,7},{7,0},{8,9},{9,10},{10,1... | collective-permute-start | bytes 811016 | tf_op jit(solution)/shard_map/ppermute | solution.py:116
  15.9 14.8 %collective-permute-start.1 = (f32[528,128]{1,0:T(8,128)S(1)}, f32[528,128]{1,0:T(8,128)S(1)}, u32[]{:S(2)}, u32[]{:S(2)}) collective-permute-start(f32[528,128]{1,0:T(8,128)S(1)} %pad_maximum_fusion.3), channel_id=1, source_target_pairs={{0,7},{1,0},{2,1},{3,2},{4,3},{5,4},{6,5},{7,6},{8,15},{9,8},{10,9... | collective-permute-start | bytes 811016 | tf_op jit(solution)/shard_map/ppermute | solution.py:118
  20.0 10.7 %collective-permute-start.2 = (f32[512,128]{1,0:T(8,128)S(1)}, f32[512,128]{1,0:T(8,128)S(1)}, u32[]{:S(2)}, u32[]{:S(2)}) collective-permute-start(f32[512,128]{1,0:T(8,128)S(1)} %bitcast.101), channel_id=1, source_target_pairs={{0,16},{1,48},{2,80},{3,112},{4,0},{5,32},{6,64},{7,96},{8,24},{9,... | collective-permute-start | bytes 786440 | tf_op jit(solution)/shard_map/ppermute | solution.py:111
  22.4 8.3 %collective-permute-start.3 = (f32[256,128]{1,0:T(8,128)}, f32[256,128]{1,0:T(8,128)S(1)}, u32[]{:S(2)}, u32[]{:S(2)}) collective-permute-start(f32[256,128]{1,0:T(8,128)} %param.14), channel_id=1, source_target_pairs={{0,8},{8,0},{1,9},{9,1},{2,10},{10,2},{3,11},{11,3},{4,12},{12,4},... | collective-permute-start | bytes 393224 | tf_op jit(solution)/shard_map/ppermute | solution.py:110
  31.4 122.7 %all-gather.7.cloned.1.call-start = ((), (), s32[]{:S(2)}) async-start(), calls=%async_computation.2 | async-start | bytes 4456448 | tf_op jit(solution)/shard_map/all_gather | solution.py:106
  31.5 33.2 %collective-permute-start.7 = (f32[2,256,2,256]{3,2,1,0:T(2,128)}, f32[2,256,2,256]{3,2,1,0:T(2,128)}, u32[]{:S(2)}, u32[]{:S(2)}) collective-permute-start(f32[2,256,2,256]{3,2,1,0:T(2,128)} %param.9), channel_id=1, source_target_pairs={{0,8},{8,0},{1,9},{9,1},{2,10},{10,2},{3,11},{11,3},{4,12},{12,4},... | collective-permute-start | bytes 3145736 | tf_op jit(solution)/shard_map/ppermute | solution.py:109
  35.2 15.9 %collective-permute-start.4 = (f32[528,128]{1,0:T(8,128)S(1)}, f32[528,128]{1,0:T(8,128)S(1)}, u32[]{:S(2)}, u32[]{:S(2)}) collective-permute-start(f32[528,128]{1,0:T(8,128)S(1)} %collective-permute-done), channel_id=1, source_target_pairs={{0,1},{1,2},{2,3},{3,4},{4,5},{5,6},{6,7},{7,0},{8,9},{9,10},{10,1... | collective-permute-start | bytes 811016 | tf_op jit(solution)/shard_map/ppermute | solution.py:116
  35.5 15.7 %collective-permute-start.8 = (f32[528,128]{1,0:T(8,128)S(1)}, f32[528,128]{1,0:T(8,128)S(1)}, u32[]{:S(2)}, u32[]{:S(2)}) collective-permute-start(f32[528,128]{1,0:T(8,128)S(1)} %collective-permute-done.1), channel_id=1, source_target_pairs={{0,7},{1,0},{2,1},{3,2},{4,3},{5,4},{6,5},{7,6},{8,15},{9,8},{10,9... | collective-permute-start | bytes 811016 | tf_op jit(solution)/shard_map/ppermute | solution.py:118
  51.1 7.0 %collective-permute-start.5 = (f32[528,128]{1,0:T(8,128)S(1)}, f32[528,128]{1,0:T(8,128)S(1)}, u32[]{:S(2)}, u32[]{:S(2)}) collective-permute-start(f32[528,128]{1,0:T(8,128)S(1)} %collective-permute-done.4), channel_id=1, source_target_pairs={{0,1},{1,2},{2,3},{3,4},{4,5},{5,6},{6,7},{7,0},{8,9},{9,10},{10,1... | collective-permute-start | bytes 811016 | tf_op jit(solution)/shard_map/ppermute | solution.py:116
  51.2 13.5 %collective-permute-start.9 = (f32[528,128]{1,0:T(8,128)S(1)}, f32[528,128]{1,0:T(8,128)S(1)}, u32[]{:S(2)}, u32[]{:S(2)}) collective-permute-start(f32[528,128]{1,0:T(8,128)S(1)} %collective-permute-done.8), channel_id=1, source_target_pairs={{0,7},{1,0},{2,1},{3,2},{4,3},{5,4},{6,5},{7,6},{8,15},{9,8},{10,9... | collective-permute-start | bytes 811016 | tf_op jit(solution)/shard_map/ppermute | solution.py:118
  58.1 6.6 %collective-permute-start.6 = (f32[528,128]{1,0:T(8,128)S(1)}, f32[528,128]{1,0:T(8,128)S(1)}, u32[]{:S(2)}, u32[]{:S(2)}) collective-permute-start(f32[528,128]{1,0:T(8,128)S(1)} %collective-permute-done.5), channel_id=1, source_target_pairs={{0,1},{1,2},{2,3},{3,4},{4,5},{5,6},{6,7},{7,0},{8,9},{9,10},{10,1... | collective-permute-start | bytes 811016 | tf_op jit(solution)/shard_map/ppermute | solution.py:116
  65.5 14.1 %collective-permute-start.10 = (f32[512,128]{1,0:T(8,128)S(1)}, f32[512,128]{1,0:T(8,128)S(1)}, u32[]{:S(2)}, u32[]{:S(2)}) collective-permute-start(f32[512,128]{1,0:T(8,128)S(1)} %fusion.4), channel_id=1, source_target_pairs={{0,8},{8,0},{1,9},{9,1},{2,10},{10,2},{3,11},{11,3},{4,12},{12,4},... | collective-permute-start | bytes 786440 | tf_op jit(solution)/shard_map/ppermute | solution.py:145
  82.0 18.6 %collective-permute-start.11 = (f32[512,128]{1,0:T(8,128)}, f32[512,128]{1,0:T(8,128)}, u32[]{:S(2)}, u32[]{:S(2)}) collective-permute-start(f32[512,128]{1,0:T(8,128)} %fusion.12), channel_id=1, source_target_pairs={{0,16},{1,48},{2,80},{3,112},{4,0},{5,32},{6,64},{7,96},{8,24},{9,... | collective-permute-start | bytes 786440 | tf_op jit(solution)/shard_map/ppermute | solution.py:148
  101.9 14.0 %collective-permute-start.12 = (f32[512,128]{1,0:T(8,128)S(1)}, f32[512,128]{1,0:T(8,128)S(1)}, u32[]{:S(2)}, u32[]{:S(2)}) collective-permute-start(f32[512,128]{1,0:T(8,128)S(1)} %get-tuple-element.68), channel_id=1, source_target_pairs={{0,1},{1,2},{2,3},{3,4},{4,5},{5,6},{6,7},{7,0},{8,9},{9,10},{10,1... | collective-permute-start | bytes 786440 | tf_op jit(solution)/shard_map/ppermute | solution.py:179
  105.3 10.7 %collective-permute-start.13 = (f32[512,128]{1,0:T(8,128)S(1)}, f32[512,128]{1,0:T(8,128)S(1)}, u32[]{:S(2)}, u32[]{:S(2)}) collective-permute-start(f32[512,128]{1,0:T(8,128)S(1)} %get-tuple-element.67), channel_id=1, source_target_pairs={{0,7},{1,0},{2,1},{3,2},{4,3},{5,4},{6,5},{7,6},{8,15},{9,8},{10,9... | collective-permute-start | bytes 786440 | tf_op jit(solution)/shard_map/ppermute | solution.py:180
  117.1 6.2 %collective-permute-start.17 = (f32[512,128]{1,0:T(8,128)S(1)}, f32[512,128]{1,0:T(8,128)S(1)}, u32[]{:S(2)}, u32[]{:S(2)}) collective-permute-start(f32[512,128]{1,0:T(8,128)S(1)} %bitcast_add_fusion.8), channel_id=1, source_target_pairs={{0,7},{1,0},{2,1},{3,2},{4,3},{5,4},{6,5},{7,6},{8,15},{9,8},{10,9... | collective-permute-start | bytes 786440 | tf_op jit(solution)/shard_map/ppermute | solution.py:183
  124.4 7.0 %collective-permute-start.14 = (f32[512,128]{1,0:T(8,128)S(1)}, f32[512,128]{1,0:T(8,128)S(1)}, u32[]{:S(2)}, u32[]{:S(2)}) collective-permute-start(f32[512,128]{1,0:T(8,128)S(1)} %get-tuple-element.64), channel_id=1, source_target_pairs={{0,1},{1,2},{2,3},{3,4},{4,5},{5,6},{6,7},{7,0},{8,9},{9,10},{10,1... | collective-permute-start | bytes 786440 | tf_op jit(solution)/shard_map/ppermute | solution.py:182
  126.7 11.7 %collective-permute-start.19 = (f32[768,128]{1,0:T(8,128)S(1)}, f32[768,128]{1,0:T(8,128)S(1)}, u32[]{:S(2)}, u32[]{:S(2)}) collective-permute-start(f32[768,128]{1,0:T(8,128)S(1)} %pad_maximum_fusion.2), channel_id=1, source_target_pairs={{0,1},{1,0},{2,3},{3,2},{4,5},{5,4},{6,7},{7,6},{8,9},{9,8},{10,11... | collective-permute-start | bytes 1179656 | tf_op jit(solution)/shard_map/ppermute | solution.py:157
  131.4 12.6 %collective-permute-start.15 = (f32[512,128]{1,0:T(8,128)S(1)}, f32[512,128]{1,0:T(8,128)S(1)}, u32[]{:S(2)}, u32[]{:S(2)}) collective-permute-start(f32[512,128]{1,0:T(8,128)S(1)} %bitcast_add_fusion.10), channel_id=1, source_target_pairs={{0,1},{1,2},{2,3},{3,4},{4,5},{5,6},{6,7},{7,0},{8,9},{9,10},{10,1... | collective-permute-start | bytes 786440 | tf_op jit(solution)/shard_map/ppermute | solution.py:184
  138.4 10.5 %collective-permute-start.18 = (f32[512,128]{1,0:T(8,128)S(1)}, f32[512,128]{1,0:T(8,128)S(1)}, u32[]{:S(2)}, u32[]{:S(2)}) collective-permute-start(f32[512,128]{1,0:T(8,128)S(1)} %get-tuple-element.63), channel_id=1, source_target_pairs={{0,7},{1,0},{2,1},{3,2},{4,3},{5,4},{6,5},{7,6},{8,15},{9,8},{10,9... | collective-permute-start | bytes 786440 | tf_op jit(solution)/shard_map/ppermute | solution.py:185
  144.0 6.5 %collective-permute-start.16 = (f32[512,128]{1,0:T(8,128)S(1)}, f32[512,128]{1,0:T(8,128)S(1)}, u32[]{:S(2)}, u32[]{:S(2)}) collective-permute-start(f32[512,128]{1,0:T(8,128)S(1)} %bitcast_add_fusion.9), channel_id=1, source_target_pairs={{0,1},{1,2},{2,3},{3,4},{4,5},{5,6},{6,7},{7,0},{8,9},{9,10},{10,1... | collective-permute-start | bytes 786440 | tf_op jit(solution)/shard_map/ppermute | solution.py:186
  159.2 6.9 %collective-permute-start.21 = (f32[512,128]{1,0:T(8,128)S(1)}, f32[512,128]{1,0:T(8,128)S(1)}, u32[]{:S(2)}, u32[]{:S(2)}) collective-permute-start(f32[512,128]{1,0:T(8,128)S(1)} %get-tuple-element.66), channel_id=1, source_target_pairs={{0,1},{1,2},{2,3},{3,4},{4,5},{5,6},{6,7},{7,0},{8,9},{9,10},{10,1... | collective-permute-start | bytes 786440 | tf_op jit(solution)/shard_map/ppermute | solution.py:179
  160.6 5.5 %collective-permute-start.22 = (f32[512,128]{1,0:T(8,128)S(1)}, f32[512,128]{1,0:T(8,128)S(1)}, u32[]{:S(2)}, u32[]{:S(2)}) collective-permute-start(f32[512,128]{1,0:T(8,128)S(1)} %get-tuple-element.65), channel_id=1, source_target_pairs={{0,7},{1,0},{2,1},{3,2},{4,3},{5,4},{6,5},{7,6},{8,15},{9,8},{10,9... | collective-permute-start | bytes 786440 | tf_op jit(solution)/shard_map/ppermute | solution.py:180
  166.2 6.5 %collective-permute-start.26 = (f32[512,128]{1,0:T(8,128)S(1)}, f32[512,128]{1,0:T(8,128)S(1)}, u32[]{:S(2)}, u32[]{:S(2)}) collective-permute-start(f32[512,128]{1,0:T(8,128)S(1)} %bitcast_add_fusion.2), channel_id=1, source_target_pairs={{0,7},{1,0},{2,1},{3,2},{4,3},{5,4},{6,5},{7,6},{8,15},{9,8},{10,9... | collective-permute-start | bytes 786440 | tf_op jit(solution)/shard_map/ppermute | solution.py:183
  173.6 7.2 %collective-permute-start.23 = (f32[512,128]{1,0:T(8,128)}, f32[512,128]{1,0:T(8,128)}, u32[]{:S(2)}, u32[]{:S(2)}) collective-permute-start(f32[512,128]{1,0:T(8,128)} %get-tuple-element.62), channel_id=1, source_target_pairs={{0,1},{1,2},{2,3},{3,4},{4,5},{5,6},{6,7},{7,0},{8,9},{9,10},{10,1... | collective-permute-start | bytes 786440 | tf_op jit(solution)/shard_map/ppermute | solution.py:182
  174.9 10.6 %collective-permute-start.20 = (f32[528,256]{1,0:T(8,128)}, f32[528,256]{1,0:T(8,128)}, u32[]{:S(2)}, u32[]{:S(2)}) collective-permute-start(f32[528,256]{1,0:T(8,128)} %pad_maximum_fusion.1), channel_id=1, source_target_pairs={{0,8},{8,0},{1,9},{9,1},{2,10},{10,2},{3,11},{11,3},{4,12},{12,4},... | collective-permute-start | bytes 1622024 | tf_op jit(solution)/shard_map/ppermute | solution.py:195
  181.8 8.1 %collective-permute-start.24 = (f32[512,128]{1,0:T(8,128)S(1)}, f32[512,128]{1,0:T(8,128)S(1)}, u32[]{:S(2)}, u32[]{:S(2)}) collective-permute-start(f32[512,128]{1,0:T(8,128)S(1)} %bitcast_add_fusion.4), channel_id=1, source_target_pairs={{0,1},{1,2},{2,3},{3,4},{4,5},{5,6},{6,7},{7,0},{8,9},{9,10},{10,1... | collective-permute-start | bytes 786440 | tf_op jit(solution)/shard_map/ppermute | solution.py:184
  185.6 5.9 %collective-permute-start.27 = (f32[512,128]{1,0:T(8,128)}, f32[512,128]{1,0:T(8,128)S(1)}, u32[]{:S(2)}, u32[]{:S(2)}) collective-permute-start(f32[512,128]{1,0:T(8,128)} %get-tuple-element.61), channel_id=1, source_target_pairs={{0,7},{1,0},{2,1},{3,2},{4,3},{5,4},{6,5},{7,6},{8,15},{9,8},{10,9... | collective-permute-start | bytes 786440 | tf_op jit(solution)/shard_map/ppermute | solution.py:185
  190.0 9.2 %collective-permute-start.25 = (f32[512,128]{1,0:T(8,128)S(1)}, f32[512,128]{1,0:T(8,128)S(1)}, u32[]{:S(2)}, u32[]{:S(2)}) collective-permute-start(f32[512,128]{1,0:T(8,128)S(1)} %bitcast_add_fusion.3), channel_id=1, source_target_pairs={{0,1},{1,2},{2,3},{3,4},{4,5},{5,6},{6,7},{7,0},{8,9},{9,10},{10,1... | collective-permute-start | bytes 786440 | tf_op jit(solution)/shard_map/ppermute | solution.py:186
  202.6 25.3 %all-to-all-start = ((f32[16,3,16,128]{3,2,1,0:T(8,128)}), f32[16,3,16,128]{3,2,1,0:T(8,128)S(1)}, u32[]{:S(2)}, u32[]{:S(2)}) async-start(f32[16,3,16,128]{3,2,1,0:T(8,128)} %maximum_bitcast_fusion), calls=%async_computation | async-start | bytes 786432 | tf_op jit(solution)/shard_map/all_to_all | solution.py:208
  (31 other events, 624.7 us)
Sparse Core Ops, SparseCore 0:
  31.5 60.9 all-gather.4
  100.8 53.2 all-gather.6

commit v9 on v8

--- a/solution.py
+++ b/solution.py
@@ -117,12 +117,11 @@
         if d < 4:
             left = lax.ppermute(left, "z", ring(8, -1))
             if d == 1:
-                right, left, near_one, lp_far = lax.optimization_barrier(
-                    (right, left, near_one, lp_far)
+                right, left, near_one, lp_far, g_other = lax.optimization_barrier(
+                    (right, left, near_one, lp_far, g_other)
                 )
             pieces[d] = left
         pieces[-d] = right
-    pieces[-4], g_other = lax.optimization_barrier((right, g_other))
     gathered_one = gather(near_one)
 
     def fetch(super_index):
@@ -144,7 +143,8 @@
     by_lp = lambda cols, lp: jnp.dot(cols[:512], lp, precision=lax.Precision.HIGH)
     from_far = lax.ppermute(by_lp(par_there, lp_far), "y_hi", ring(2, 1))
     folded = two - jnp.where(here, by_lp(par_here, lp_two), from_far)
-    folded, g_other = lax.optimization_barrier((folded, g_other))
+    two_sent = jnp.concatenate([two, lp_two])
+    folded, g_other, two_sent = lax.optimization_barrier((folded, g_other, two_sent))
     near_two = lax.ppermute(folded, ALL_AXES, spread_pairs())
 
     g_parts = []
@@ -153,10 +153,7 @@
         g_hi = lax.reduce_precision(g, 8, 7)
         g_parts += [g_hi.astype(jnp.bfloat16), (g - g_hi).astype(jnp.bfloat16)]
 
-    two_sent = jnp.concatenate([two, lp_two])
     two_next = lax.ppermute(two_sent, "z", [(i, i ^ 1) for i in range(8)])
-    own_two = pair_up(two, two_next[:512])
-    lp_own = pair_up(lp_two, two_next[512:])
 
     def multiply(gathered, after):
         def part(first_pair, after):
@@ -186,8 +183,12 @@
         return lax.ppermute(up + term(1), "z", ring(8, 1)) + down + term(0)
 
     early, late = multiply(gathered_one, h)
-    near_two, early, late = lax.optimization_barrier((near_two, early, late))
+    near_two, early, late, two_next = lax.optimization_barrier(
+        (near_two, early, late, two_next)
+    )
     gathered_two = gather(near_two)
+    own_two = pair_up(two, two_next[:512])
+    lp_own = pair_up(lp_two, two_next[512:])
     inv_one = sum_over_z(early, late)
     inv_one, own_one, own_two, lp_own, par_there, h_next = lax.optimization_barrier(
         (inv_one, own_one, own_two, lp_own, par_there, h)

time: 237 us -> 233 us (0.983)
  starting transfers between devices: 88.3 us -> 79.2 us
    ppermute x1, waiting for transfers between devices: 5.62 us -> 15.3 us  [local(): lp_far = lax.ppermute(lp_two, 'y_hi', ring(2, 1))]
    ppermute x3, starting transfers between devices: 17.4 us -> 8.05 us  [local(): left = lax.ppermute(left, 'z', ring(8, -1))]
    all_gather x2, waiting for transfers between devices: 6.34 us -> 0.02 us  [gather(): rows = lax.all_gather(piece, ROW_AXES, axis=0, tiled=False)]
    ppermute x2, waiting for transfers between devices: 5.68 us -> 11.3 us  [sum_over_z(): up = lax.ppermute(up + term(3), 'z', ring(8, 1))]
    ppermute x2, waiting for transfers between devices: 9.23 us -> 4.39 us  [sum_over_z(): return lax.ppermute(up + term(1), 'z', ring(8, 1)) + down + term(0)]
    ppermute x2, starting transfers between devices: 4.73 us -> 0.69 us  [sum_over_z(): up = lax.ppermute(term(4), 'z', ring(8, 1))]
    ppermute x1, waiting for transfers between devices: 3.98 us -> 0.01 us  [local(): two_next = lax.ppermute(two_sent, 'z', [(i, i ^ 1) for i in range(8)])]
    ppermute x2, starting transfers between devices: 8.83 us -> 12.7 us  [sum_over_z(): down = lax.ppermute(term(-3), 'z', ring(8, -1))]
  transfers between devices with their start and end apart: 31 -> 31, of which waited for: 20 -> 16; matrix products, arithmetic and copies ran while one was open for 8% -> 11% of each run, Pallas kernels for 4% -> 4%
where the time goes in v9:
time: 233 us; the launch traced here: 232 us
  waiting for transfers between devices  83.6 us (36%)
  starting transfers between devices  79.2 us (34%)
  between operations  20.8 us (9%)
  other arithmetic  19.8 us (8%)
  local copies, waits for them, and re-layouts  11.7 us (5%)
  Pallas kernels  11.6 us (5%)
  matrix products  5.65 us (2%)
    ppermute x1, waiting for transfers between devices, local(): lp_far = lax.ppermute(lp_two, 'y_hi', ring(2, 1))  15.3 us
    all_to_all x1, starting transfers between devices, local(): sums = jnp.sum(lax.all_to_all(terms, ROW_AXES, 0, 0), axis=0)  14.2 us
    ppermute x2, starting transfers between devices, sum_over_z(): down = lax.ppermute(term(-3), 'z', ring(8, -1))  12.7 us
    ppermute x1, waiting for transfers between devices, local(): from_far = lax.ppermute(by_lp(par_there, lp_far), 'y_hi', ring(2, 1))  12.3 us
    pallas_call x4, Pallas kernels, product(): pl.pallas_call(pair_kernel, grid_spec=pltpu.PrefetchScalarGridSpec(num_sc...  11.6 us
    ppermute x2, waiting for transfers between devices, sum_over_z(): up = lax.ppermute(up + term(3), 'z', ring(8, 1))  11.3 us
    ppermute x2, waiting for transfers between devices, sum_over_z(): down = lax.ppermute(down + term(-2), 'z', ring(8, -1))  9.34 us
    ppermute x3, starting transfers between devices, local(): left = lax.ppermute(left, 'z', ring(8, -1))  8.05 us
  transfers between devices with their start and end apart: 31, of which 16 were waited for; matrix products, arithmetic and copies ran while one was open for 11% of the time, Pallas kernels for 4%

profile of v9, /device:TPU:1, one launch (start us, length us, event | category | flops | bytes accessed | tf_op | source)
XLA Modules:
  0.0 232.4 jit_solution(12436381323845953351)
XLA Ops:
  7.2 3.8 %collective-permute-start.4 = (f32[2,256,2,256]{3,2,1,0:T(2,128)}, f32[2,256,2,256]{3,2,1,0:T(2,128)S(1)}, u32[]{:S(2)}, u32[]{:S(2)}) collective-permute-start(f32[2,256,2,256]{3,2,1,0:T(2,128)} %param.9), channel_id=1, source_target_pairs={{0,8},{8,0},{1,9},{9,1},{2,10},{10,2},{3,11},{11,3},{4,12},{12,4},... | collective-permute-start | bytes 3145736 | tf_op jit(solution)/shard_map/ppermute | solution.py:109
  18.9 4.0 %collective-permute-start.1 = (f32[528,128]{1,0:T(8,128)S(1)}, f32[528,128]{1,0:T(8,128)S(1)}, u32[]{:S(2)}, u32[]{:S(2)}) collective-permute-start(f32[528,128]{1,0:T(8,128)S(1)} %pad_maximum_fusion.3), channel_id=1, source_target_pairs={{0,7},{1,0},{2,1},{3,2},{4,3},{5,4},{6,5},{7,6},{8,15},{9,8},{10,9... | collective-permute-start | bytes 811016 | tf_op jit(solution)/shard_map/ppermute | solution.py:118
  26.4 15.3 %collective-permute-done.3 = f32[256,128]{1,0:T(8,128)S(1)} collective-permute-done((f32[256,128]{1,0:T(8,128)}, f32[256,128]{1,0:T(8,128)S(1)}, u32[]{:S(2)}, u32[]{:S(2)}) %collective-permute-start.3) | collective-permute-done | bytes 131104 | tf_op jit(solution)/shard_map/ppermute | solution.py:110
  47.1 3.6 %collective-permute-done.5 = f32[528,128]{1,0:T(8,128)S(1)} collective-permute-done((f32[528,128]{1,0:T(8,128)S(1)}, f32[528,128]{1,0:T(8,128)S(1)}, u32[]{:S(2)}, u32[]{:S(2)}) %collective-permute-start.5) | collective-permute-done | bytes 270368 | tf_op jit(solution)/shard_map/ppermute | solution.py:116
  52.5 2.6 %collective-permute-start.9 = (f32[528,128]{1,0:T(8,128)S(1)}, f32[528,128]{1,0:T(8,128)S(1)}, u32[]{:S(2)}, u32[]{:S(2)}) collective-permute-start(f32[528,128]{1,0:T(8,128)S(1)} %collective-permute-done.8), channel_id=1, source_target_pairs={{0,7},{1,0},{2,1},{3,2},{4,3},{5,4},{6,5},{7,6},{8,15},{9,8},{10,9... | collective-permute-start | bytes 811016 | tf_op jit(solution)/shard_map/ppermute | solution.py:118
  63.0 2.3 copy.20
  68.3 12.3 %collective-permute-done.10 = f32[512,128]{1,0:T(8,128)S(1)} collective-permute-done((f32[512,128]{1,0:T(8,128)S(1)}, f32[512,128]{1,0:T(8,128)S(1)}, u32[]{:S(2)}, u32[]{:S(2)}) %collective-permute-start.10) | collective-permute-done | bytes 262176 | tf_op jit(solution)/shard_map/ppermute | solution.py:144
  81.8 2.3 collective-permute-start.12
  84.0 7.2 %collective-permute-start.11 = (f32[512,128]{1,0:T(8,128)}, f32[512,128]{1,0:T(8,128)}, u32[]{:S(2)}, u32[]{:S(2)}) collective-permute-start(f32[512,128]{1,0:T(8,128)} %fusion), channel_id=1, source_target_pairs={{0,16},{1,48},{2,80},{3,112},{4,0},{5,32},{6,64},{7,96},{8,24},{9,... | collective-permute-start | bytes 786440 | tf_op jit(solution)/shard_map/ppermute | solution.py:148
  93.8 2.9 %shard_map.128 = f32[4,512,128]{2,1,0:T(8,128)S(1)} custom-call(s32[5]{0:T(128)S(1)} %pad_add_fusion.sc_ref, bf16[512,512]{1,0:T(8,128)(2,1)S(1)} %get-tuple-element.74.refs_0_, bf16[512,512]{1,0:T(8,128)(2,1)S(1)} %get-tuple-element.73.refs_1_, bf16[512,512]{1,0:T(8,128)(2,1)S(1)} %get-tuple-element.84.refs_2_, ...), custom_call_target="tpu_custom_call" | custom-call | flops 1600000000 | bytes 7000000 | tf_op jit(solution)/shard_map/pallas_call | solution.py:52
  96.8 2.9 %shard_map.129 = f32[4,512,128]{2,1,0:T(8,128)S(1)} custom-call(s32[5]{0:T(128)S(1)} %pad_add_fusion.1.sc_ref, bf16[512,512]{1,0:T(8,128)(2,1)S(1)} %get-tuple-element.74.refs_0_, bf16[512,512]{1,0:T(8,128)(2,1)S(1)} %get-tuple-element.73.refs_1_, bf16[512,512]{1,0:T(8,128)(2,1)S(1)} %get-tuple-element.84.refs_2_, ...), custom_call_target="tpu_custom_call" | custom-call | flops 1600000000 | bytes 7000000 | tf_op jit(solution)/shard_map/pallas_call | solution.py:52
  101.7 10.0 %collective-permute-start.14 = (f32[512,128]{1,0:T(8,128)S(1)}, f32[512,128]{1,0:T(8,128)S(1)}, u32[]{:S(2)}, u32[]{:S(2)}) collective-permute-start(f32[512,128]{1,0:T(8,128)S(1)} %get-tuple-element.69), channel_id=1, source_target_pairs={{0,7},{1,0},{2,1},{3,2},{4,3},{5,4},{6,5},{7,6},{8,15},{9,8},{10,9... | collective-permute-start | bytes 786440 | tf_op jit(solution)/shard_map/ppermute | solution.py:177
  111.7 5.2 %collective-permute-done.13 = f32[512,128]{1,0:T(8,128)S(1)} collective-permute-done((f32[512,128]{1,0:T(8,128)S(1)}, f32[512,128]{1,0:T(8,128)S(1)}, u32[]{:S(2)}, u32[]{:S(2)}) %collective-permute-start.13) | collective-permute-done | bytes 262176 | tf_op jit(solution)/shard_map/ppermute | solution.py:176
  118.0 3.1 %collective-permute-start.18 = (f32[512,128]{1,0:T(8,128)S(1)}, f32[512,128]{1,0:T(8,128)S(1)}, u32[]{:S(2)}, u32[]{:S(2)}) collective-permute-start(f32[512,128]{1,0:T(8,128)S(1)} %bitcast_add_fusion.8), channel_id=1, source_target_pairs={{0,7},{1,0},{2,1},{3,2},{4,3},{5,4},{6,5},{7,6},{8,15},{9,8},{10,9... | collective-permute-start | bytes 786440 | tf_op jit(solution)/shard_map/ppermute | solution.py:180
  121.1 6.0 %collective-permute-done.18 = f32[512,128]{1,0:T(8,128)S(1)} collective-permute-done((f32[512,128]{1,0:T(8,128)S(1)}, f32[512,128]{1,0:T(8,128)S(1)}, u32[]{:S(2)}, u32[]{:S(2)}) %collective-permute-start.18) | collective-permute-done | bytes 262176 | tf_op jit(solution)/shard_map/ppermute | solution.py:180
  128.4 9.6 %collective-permute-done.15 = f32[512,128]{1,0:T(8,128)S(1)} collective-permute-done((f32[512,128]{1,0:T(8,128)S(1)}, f32[512,128]{1,0:T(8,128)S(1)}, u32[]{:S(2)}, u32[]{:S(2)}) %collective-permute-start.15) | collective-permute-done | bytes 262176 | tf_op jit(solution)/shard_map/ppermute | solution.py:179
  139.1 2.6 %collective-permute-start.19 = (f32[512,128]{1,0:T(8,128)S(1)}, f32[512,128]{1,0:T(8,128)S(1)}, u32[]{:S(2)}, u32[]{:S(2)}) collective-permute-start(f32[512,128]{1,0:T(8,128)S(1)} %get-tuple-element.65), channel_id=1, source_target_pairs={{0,7},{1,0},{2,1},{3,2},{4,3},{5,4},{6,5},{7,6},{8,15},{9,8},{10,9... | collective-permute-start | bytes 786440 | tf_op jit(solution)/shard_map/ppermute | solution.py:182
  141.8 4.4 %collective-permute-done.16 = f32[512,128]{1,0:T(8,128)S(1)} collective-permute-done((f32[512,128]{1,0:T(8,128)S(1)}, f32[512,128]{1,0:T(8,128)S(1)}, u32[]{:S(2)}, u32[]{:S(2)}) %collective-permute-start.16) | collective-permute-done | bytes 262176 | tf_op jit(solution)/shard_map/ppermute | solution.py:181
  150.6 2.7 %collective-permute-done.17 = f32[512,128]{1,0:T(8,128)S(1)} collective-permute-done((f32[512,128]{1,0:T(8,128)S(1)}, f32[512,128]{1,0:T(8,128)S(1)}, u32[]{:S(2)}, u32[]{:S(2)}) %collective-permute-start.17) | collective-permute-done | bytes 262176 | tf_op jit(solution)/shard_map/ppermute | solution.py:183
  153.5 2.2 copy-done.3
  155.7 2.9 %shard_map.130 = f32[4,512,128]{2,1,0:T(8,128)S(1)} custom-call(s32[5]{0:T(128)S(1)} %pad_add_fusion.2.sc_ref, bf16[512,512]{1,0:T(8,128)(2,1)S(1)} %get-tuple-element.74.refs_0_, bf16[512,512]{1,0:T(8,128)(2,1)S(1)} %get-tuple-element.73.refs_1_, bf16[512,512]{1,0:T(8,128)(2,1)S(1)} %get-tuple-element.84.refs_2_, ...), custom_call_target="tpu_custom_call" | custom-call | flops 1600000000 | bytes 7000000 | tf_op jit(solution)/shard_map/pallas_call | solution.py:52
  158.8 2.7 %collective-permute-start.22 = (f32[512,128]{1,0:T(8,128)S(1)}, f32[512,128]{1,0:T(8,128)S(1)}, u32[]{:S(2)}, u32[]{:S(2)}) collective-permute-start(f32[512,128]{1,0:T(8,128)S(1)} %get-tuple-element.67), channel_id=1, source_target_pairs={{0,7},{1,0},{2,1},{3,2},{4,3},{5,4},{6,5},{7,6},{8,15},{9,8},{10,9... | collective-permute-start | bytes 786440 | tf_op jit(solution)/shard_map/ppermute | solution.py:177
  161.5 2.9 %shard_map.131 = f32[4,512,128]{2,1,0:T(8,128)S(1)} custom-call(s32[5]{0:T(128)S(1)} %pad_add_fusion.3.sc_ref, bf16[512,512]{1,0:T(8,128)(2,1)S(1)} %get-tuple-element.74.refs_0_, bf16[512,512]{1,0:T(8,128)(2,1)S(1)} %get-tuple-element.73.refs_1_, bf16[512,512]{1,0:T(8,128)(2,1)S(1)} %get-tuple-element.84.refs_2_, ...), custom_call_target="tpu_custom_call" | custom-call | flops 1600000000 | bytes 7000000 | tf_op jit(solution)/shard_map/pallas_call | solution.py:52
  165.2 3.0 %collective-permute-start.26 = (f32[512,128]{1,0:T(8,128)S(1)}, f32[512,128]{1,0:T(8,128)S(1)}, u32[]{:S(2)}, u32[]{:S(2)}) collective-permute-start(f32[512,128]{1,0:T(8,128)S(1)} %bitcast_add_fusion.2), channel_id=1, source_target_pairs={{0,7},{1,0},{2,1},{3,2},{4,3},{5,4},{6,5},{7,6},{8,15},{9,8},{10,9... | collective-permute-start | bytes 786440 | tf_op jit(solution)/shard_map/ppermute | solution.py:180
  168.2 3.3 %collective-permute-done.26 = f32[512,128]{1,0:T(8,128)S(1)} collective-permute-done((f32[512,128]{1,0:T(8,128)S(1)}, f32[512,128]{1,0:T(8,128)S(1)}, u32[]{:S(2)}, u32[]{:S(2)}) %collective-permute-start.26) | collective-permute-done | bytes 262176 | tf_op jit(solution)/shard_map/ppermute | solution.py:180
  172.4 4.2 %collective-permute-start.23 = (f32[512,128]{1,0:T(8,128)}, f32[512,128]{1,0:T(8,128)}, u32[]{:S(2)}, u32[]{:S(2)}) collective-permute-start(f32[512,128]{1,0:T(8,128)} %get-tuple-element.64), channel_id=1, source_target_pairs={{0,1},{1,2},{2,3},{3,4},{4,5},{5,6},{6,7},{7,0},{8,9},{9,10},{10,1... | collective-permute-start | bytes 786440 | tf_op jit(solution)/shard_map/ppermute | solution.py:179
  176.6 2.5 %collective-permute-start.20 = (f32[528,256]{1,0:T(8,128)}, f32[528,256]{1,0:T(8,128)}, u32[]{:S(2)}, u32[]{:S(2)}) collective-permute-start(f32[528,256]{1,0:T(8,128)} %pad_maximum_fusion.1), channel_id=1, source_target_pairs={{0,8},{8,0},{1,9},{9,1},{2,10},{10,2},{3,11},{11,3},{4,12},{12,4},... | collective-permute-start | bytes 1622024 | tf_op jit(solution)/shard_map/ppermute | solution.py:196
  181.8 2.3 collective-permute-start.24
  185.1 5.1 %collective-permute-done.20 = f32[528,256]{1,0:T(8,128)} collective-permute-done((f32[528,256]{1,0:T(8,128)}, f32[528,256]{1,0:T(8,128)}, u32[]{:S(2)}, u32[]{:S(2)}) %collective-permute-start.20) | collective-permute-done | bytes 540704 | tf_op jit(solution)/shard_map/ppermute | solution.py:196
  192.8 3.5 %collective-permute-done.27 = f32[512,128]{1,0:T(8,128)S(1)} collective-permute-done((f32[512,128]{1,0:T(8,128)}, f32[512,128]{1,0:T(8,128)S(1)}, u32[]{:S(2)}, u32[]{:S(2)}) %collective-permute-start.27) | collective-permute-done | bytes 262176 | tf_op jit(solution)/shard_map/ppermute | solution.py:182
  201.4 14.2 %all-to-all-start = ((f32[16,3,16,128]{3,2,1,0:T(8,128)}), f32[16,3,16,128]{3,2,1,0:T(8,128)S(1)}, u32[]{:S(2)}, u32[]{:S(2)}) async-start(f32[16,3,16,128]{3,2,1,0:T(8,128)} %maximum_bitcast_fusion), calls=%async_computation | async-start | bytes 786432 | tf_op jit(solution)/shard_map/all_to_all | solution.py:209
  217.8 6.4 %all-to-all-done = f32[16,3,16,128]{3,2,1,0:T(8,128)S(1)} async-done(((f32[16,3,16,128]{3,2,1,0:T(8,128)}), f32[16,3,16,128]{3,2,1,0:T(8,128)S(1)}, u32[]{:S(2)}, u32[]{:S(2)}) %all-to-all-start) | async-done | bytes 393248 | tf_op jit(solution)/shard_map/all_to_all | solution.py:209
  (167 shorter events, 53.5 us)
Async XLA Ops:
  7.2 58.3 %copy-start.27 = (f32[16,128]{1,0:T(8,128)S(1)}, f32[16,128]{1,0:T(8,128)}, u32[]{:S(2)}) copy-start(f32[16,128]{1,0:T(8,128)} %param.12) | copy-start | bytes 24580
  7.2 84.4 %all-gather.5.cloned.1.call-start = ((), (), s32[]{:S(2)}) async-start(), calls=%async_computation.1 | async-start | bytes 4456448 | tf_op jit(solution)/shard_map/all_gather | solution.py:106
  7.2 34.4 %collective-permute-start.4 = (f32[2,256,2,256]{3,2,1,0:T(2,128)}, f32[2,256,2,256]{3,2,1,0:T(2,128)S(1)}, u32[]{:S(2)}, u32[]{:S(2)}) collective-permute-start(f32[2,256,2,256]{3,2,1,0:T(2,128)} %param.9), channel_id=1, source_target_pairs={{0,8},{8,0},{1,9},{9,1},{2,10},{10,2},{3,11},{11,3},{4,12},{12,4},... | collective-permute-start | bytes 3145736 | tf_op jit(solution)/shard_map/ppermute | solution.py:109
  17.2 24.4 %collective-permute-start = (f32[528,128]{1,0:T(8,128)S(1)}, f32[528,128]{1,0:T(8,128)S(1)}, u32[]{:S(2)}, u32[]{:S(2)}) collective-permute-start(f32[528,128]{1,0:T(8,128)S(1)} %pad_maximum_fusion.3), channel_id=1, source_target_pairs={{0,1},{1,2},{2,3},{3,4},{4,5},{5,6},{6,7},{7,0},{8,9},{9,10},{10,1... | collective-permute-start | bytes 811016 | tf_op jit(solution)/shard_map/ppermute | solution.py:116
  18.9 22.7 %collective-permute-start.1 = (f32[528,128]{1,0:T(8,128)S(1)}, f32[528,128]{1,0:T(8,128)S(1)}, u32[]{:S(2)}, u32[]{:S(2)}) collective-permute-start(f32[528,128]{1,0:T(8,128)S(1)} %pad_maximum_fusion.3), channel_id=1, source_target_pairs={{0,7},{1,0},{2,1},{3,2},{4,3},{5,4},{6,5},{7,6},{8,15},{9,8},{10,9... | collective-permute-start | bytes 811016 | tf_op jit(solution)/shard_map/ppermute | solution.py:118
  22.9 18.7 %collective-permute-start.2 = (f32[512,128]{1,0:T(8,128)S(1)}, f32[512,128]{1,0:T(8,128)S(1)}, u32[]{:S(2)}, u32[]{:S(2)}) collective-permute-start(f32[512,128]{1,0:T(8,128)S(1)} %bitcast.101), channel_id=1, source_target_pairs={{0,16},{1,48},{2,80},{3,112},{4,0},{5,32},{6,64},{7,96},{8,24},{9,... | collective-permute-start | bytes 786440 | tf_op jit(solution)/shard_map/ppermute | solution.py:111
  24.9 16.8 %collective-permute-start.3 = (f32[256,128]{1,0:T(8,128)}, f32[256,128]{1,0:T(8,128)S(1)}, u32[]{:S(2)}, u32[]{:S(2)}) collective-permute-start(f32[256,128]{1,0:T(8,128)} %param.14), channel_id=1, source_target_pairs={{0,8},{8,0},{1,9},{9,1},{2,10},{10,2},{3,11},{11,3},{4,12},{12,4},... | collective-permute-start | bytes 393224 | tf_op jit(solution)/shard_map/ppermute | solution.py:110
  42.4 111.1 %all-gather.7.cloned.1.call-start = ((), (), s32[]{:S(2)}) async-start(), calls=%async_computation.2 | async-start | bytes 4456448 | tf_op jit(solution)/shard_map/all_gather | solution.py:106
  42.6 8.1 %collective-permute-start.5 = (f32[528,128]{1,0:T(8,128)S(1)}, f32[528,128]{1,0:T(8,128)S(1)}, u32[]{:S(2)}, u32[]{:S(2)}) collective-permute-start(f32[528,128]{1,0:T(8,128)S(1)} %collective-permute-done), channel_id=1, source_target_pairs={{0,1},{1,2},{2,3},{3,4},{4,5},{5,6},{6,7},{7,0},{8,9},{9,10},{10,1... | collective-permute-start | bytes 811016 | tf_op jit(solution)/shard_map/ppermute | solution.py:116
  45.7 6.8 %collective-permute-start.8 = (f32[528,128]{1,0:T(8,128)S(1)}, f32[528,128]{1,0:T(8,128)S(1)}, u32[]{:S(2)}, u32[]{:S(2)}) collective-permute-start(f32[528,128]{1,0:T(8,128)S(1)} %collective-permute-done.1), channel_id=1, source_target_pairs={{0,7},{1,0},{2,1},{3,2},{4,3},{5,4},{6,5},{7,6},{8,15},{9,8},{10,9... | collective-permute-start | bytes 811016 | tf_op jit(solution)/shard_map/ppermute | solution.py:118
  50.7 6.5 %collective-permute-start.6 = (f32[528,128]{1,0:T(8,128)S(1)}, f32[528,128]{1,0:T(8,128)S(1)}, u32[]{:S(2)}, u32[]{:S(2)}) collective-permute-start(f32[528,128]{1,0:T(8,128)S(1)} %collective-permute-done.5), channel_id=1, source_target_pairs={{0,1},{1,2},{2,3},{3,4},{4,5},{5,6},{6,7},{7,0},{8,9},{9,10},{10,1... | collective-permute-start | bytes 811016 | tf_op jit(solution)/shard_map/ppermute | solution.py:116
  52.5 13.0 %collective-permute-start.9 = (f32[528,128]{1,0:T(8,128)S(1)}, f32[528,128]{1,0:T(8,128)S(1)}, u32[]{:S(2)}, u32[]{:S(2)}) collective-permute-start(f32[528,128]{1,0:T(8,128)S(1)} %collective-permute-done.8), channel_id=1, source_target_pairs={{0,7},{1,0},{2,1},{3,2},{4,3},{5,4},{6,5},{7,6},{8,15},{9,8},{10,9... | collective-permute-start | bytes 811016 | tf_op jit(solution)/shard_map/ppermute | solution.py:118
  57.2 8.3 %collective-permute-start.7 = (f32[528,128]{1,0:T(8,128)S(1)}, f32[528,128]{1,0:T(8,128)S(1)}, u32[]{:S(2)}, u32[]{:S(2)}) collective-permute-start(f32[528,128]{1,0:T(8,128)S(1)} %collective-permute-done.6), channel_id=1, source_target_pairs={{0,1},{1,2},{2,3},{3,4},{4,5},{5,6},{6,7},{7,0},{8,9},{9,10},{10,1... | collective-permute-start | bytes 811016 | tf_op jit(solution)/shard_map/ppermute | solution.py:116
  66.3 14.2 %collective-permute-start.10 = (f32[512,128]{1,0:T(8,128)S(1)}, f32[512,128]{1,0:T(8,128)S(1)}, u32[]{:S(2)}, u32[]{:S(2)}) collective-permute-start(f32[512,128]{1,0:T(8,128)S(1)} %fusion.5), channel_id=1, source_target_pairs={{0,8},{8,0},{1,9},{9,1},{2,10},{10,2},{3,11},{11,3},{4,12},{12,4},... | collective-permute-start | bytes 786440 | tf_op jit(solution)/shard_map/ppermute | solution.py:144
  81.8 18.0 %collective-permute-start.12 = (f32[768,128]{1,0:T(8,128)}, f32[768,128]{1,0:T(8,128)}, u32[]{:S(2)}, u32[]{:S(2)}) collective-permute-start(f32[768,128]{1,0:T(8,128)} %pad_maximum_fusion.2), channel_id=1, source_target_pairs={{0,1},{1,0},{2,3},{3,2},{4,5},{5,4},{6,7},{7,6},{8,9},{9,8},{10,11... | collective-permute-start | bytes 1179656 | tf_op jit(solution)/shard_map/ppermute | solution.py:156
  84.0 15.8 %collective-permute-start.11 = (f32[512,128]{1,0:T(8,128)}, f32[512,128]{1,0:T(8,128)}, u32[]{:S(2)}, u32[]{:S(2)}) collective-permute-start(f32[512,128]{1,0:T(8,128)} %fusion), channel_id=1, source_target_pairs={{0,16},{1,48},{2,80},{3,112},{4,0},{5,32},{6,64},{7,96},{8,24},{9,... | collective-permute-start | bytes 786440 | tf_op jit(solution)/shard_map/ppermute | solution.py:148
  101.1 15.8 %collective-permute-start.13 = (f32[512,128]{1,0:T(8,128)S(1)}, f32[512,128]{1,0:T(8,128)S(1)}, u32[]{:S(2)}, u32[]{:S(2)}) collective-permute-start(f32[512,128]{1,0:T(8,128)S(1)} %get-tuple-element.70), channel_id=1, source_target_pairs={{0,1},{1,2},{2,3},{3,4},{4,5},{5,6},{6,7},{7,0},{8,9},{9,10},{10,1... | collective-permute-start | bytes 786440 | tf_op jit(solution)/shard_map/ppermute | solution.py:176
  101.7 15.2 %collective-permute-start.14 = (f32[512,128]{1,0:T(8,128)S(1)}, f32[512,128]{1,0:T(8,128)S(1)}, u32[]{:S(2)}, u32[]{:S(2)}) collective-permute-start(f32[512,128]{1,0:T(8,128)S(1)} %get-tuple-element.69), channel_id=1, source_target_pairs={{0,7},{1,0},{2,1},{3,2},{4,3},{5,4},{6,5},{7,6},{8,15},{9,8},{10,9... | collective-permute-start | bytes 786440 | tf_op jit(solution)/shard_map/ppermute | solution.py:177
  118.0 9.1 %collective-permute-start.18 = (f32[512,128]{1,0:T(8,128)S(1)}, f32[512,128]{1,0:T(8,128)S(1)}, u32[]{:S(2)}, u32[]{:S(2)}) collective-permute-start(f32[512,128]{1,0:T(8,128)S(1)} %bitcast_add_fusion.8), channel_id=1, source_target_pairs={{0,7},{1,0},{2,1},{3,2},{4,3},{5,4},{6,5},{7,6},{8,15},{9,8},{10,9... | collective-permute-start | bytes 786440 | tf_op jit(solution)/shard_map/ppermute | solution.py:180
  128.3 9.7 %collective-permute-start.15 = (f32[512,128]{1,0:T(8,128)S(1)}, f32[512,128]{1,0:T(8,128)S(1)}, u32[]{:S(2)}, u32[]{:S(2)}) collective-permute-start(f32[512,128]{1,0:T(8,128)S(1)} %get-tuple-element.66), channel_id=1, source_target_pairs={{0,1},{1,2},{2,3},{3,4},{4,5},{5,6},{6,7},{7,0},{8,9},{9,10},{10,1... | collective-permute-start | bytes 786440 | tf_op jit(solution)/shard_map/ppermute | solution.py:179
  138.1 8.1 %collective-permute-start.16 = (f32[512,128]{1,0:T(8,128)S(1)}, f32[512,128]{1,0:T(8,128)S(1)}, u32[]{:S(2)}, u32[]{:S(2)}) collective-permute-start(f32[512,128]{1,0:T(8,128)S(1)} %bitcast_add_fusion.10), channel_id=1, source_target_pairs={{0,1},{1,2},{2,3},{3,4},{4,5},{5,6},{6,7},{7,0},{8,9},{9,10},{10,1... | collective-permute-start | bytes 786440 | tf_op jit(solution)/shard_map/ppermute | solution.py:181
  139.1 11.5 %collective-permute-start.19 = (f32[512,128]{1,0:T(8,128)S(1)}, f32[512,128]{1,0:T(8,128)S(1)}, u32[]{:S(2)}, u32[]{:S(2)}) collective-permute-start(f32[512,128]{1,0:T(8,128)S(1)} %get-tuple-element.65), channel_id=1, source_target_pairs={{0,7},{1,0},{2,1},{3,2},{4,3},{5,4},{6,5},{7,6},{8,15},{9,8},{10,9... | collective-permute-start | bytes 786440 | tf_op jit(solution)/shard_map/ppermute | solution.py:182
  146.2 7.2 %collective-permute-start.17 = (f32[512,128]{1,0:T(8,128)S(1)}, f32[512,128]{1,0:T(8,128)S(1)}, u32[]{:S(2)}, u32[]{:S(2)}) collective-permute-start(f32[512,128]{1,0:T(8,128)S(1)} %bitcast_add_fusion.9), channel_id=1, source_target_pairs={{0,1},{1,2},{2,3},{3,4},{4,5},{5,6},{6,7},{7,0},{8,9},{9,10},{10,1... | collective-permute-start | bytes 786440 | tf_op jit(solution)/shard_map/ppermute | solution.py:183
  158.7 6.5 %collective-permute-start.21 = (f32[512,128]{1,0:T(8,128)S(1)}, f32[512,128]{1,0:T(8,128)S(1)}, u32[]{:S(2)}, u32[]{:S(2)}) collective-permute-start(f32[512,128]{1,0:T(8,128)S(1)} %get-tuple-element.68), channel_id=1, source_target_pairs={{0,1},{1,2},{2,3},{3,4},{4,5},{5,6},{6,7},{7,0},{8,9},{9,10},{10,1... | collective-permute-start | bytes 786440 | tf_op jit(solution)/shard_map/ppermute | solution.py:176
  158.8 6.4 %collective-permute-start.22 = (f32[512,128]{1,0:T(8,128)S(1)}, f32[512,128]{1,0:T(8,128)S(1)}, u32[]{:S(2)}, u32[]{:S(2)}) collective-permute-start(f32[512,128]{1,0:T(8,128)S(1)} %get-tuple-element.67), channel_id=1, source_target_pairs={{0,7},{1,0},{2,1},{3,2},{4,3},{5,4},{6,5},{7,6},{8,15},{9,8},{10,9... | collective-permute-start | bytes 786440 | tf_op jit(solution)/shard_map/ppermute | solution.py:177
  165.2 6.3 %collective-permute-start.26 = (f32[512,128]{1,0:T(8,128)S(1)}, f32[512,128]{1,0:T(8,128)S(1)}, u32[]{:S(2)}, u32[]{:S(2)}) collective-permute-start(f32[512,128]{1,0:T(8,128)S(1)} %bitcast_add_fusion.2), channel_id=1, source_target_pairs={{0,7},{1,0},{2,1},{3,2},{4,3},{5,4},{6,5},{7,6},{8,15},{9,8},{10,9... | collective-permute-start | bytes 786440 | tf_op jit(solution)/shard_map/ppermute | solution.py:180
  172.4 8.4 %collective-permute-start.23 = (f32[512,128]{1,0:T(8,128)}, f32[512,128]{1,0:T(8,128)}, u32[]{:S(2)}, u32[]{:S(2)}) collective-permute-start(f32[512,128]{1,0:T(8,128)} %get-tuple-element.64), channel_id=1, source_target_pairs={{0,1},{1,2},{2,3},{3,4},{4,5},{5,6},{6,7},{7,0},{8,9},{9,10},{10,1... | collective-permute-start | bytes 786440 | tf_op jit(solution)/shard_map/ppermute | solution.py:179
  176.6 13.6 %collective-permute-start.20 = (f32[528,256]{1,0:T(8,128)}, f32[528,256]{1,0:T(8,128)}, u32[]{:S(2)}, u32[]{:S(2)}) collective-permute-start(f32[528,256]{1,0:T(8,128)} %pad_maximum_fusion.1), channel_id=1, source_target_pairs={{0,8},{8,0},{1,9},{9,1},{2,10},{10,2},{3,11},{11,3},{4,12},{12,4},... | collective-permute-start | bytes 1622024 | tf_op jit(solution)/shard_map/ppermute | solution.py:196
  181.8 8.6 %collective-permute-start.24 = (f32[512,128]{1,0:T(8,128)S(1)}, f32[512,128]{1,0:T(8,128)S(1)}, u32[]{:S(2)}, u32[]{:S(2)}) collective-permute-start(f32[512,128]{1,0:T(8,128)S(1)} %bitcast_add_fusion.4), channel_id=1, source_target_pairs={{0,1},{1,2},{2,3},{3,4},{4,5},{5,6},{6,7},{7,0},{8,9},{9,10},{10,1... | collective-permute-start | bytes 786440 | tf_op jit(solution)/shard_map/ppermute | solution.py:181
  190.3 6.0 %collective-permute-start.27 = (f32[512,128]{1,0:T(8,128)}, f32[512,128]{1,0:T(8,128)S(1)}, u32[]{:S(2)}, u32[]{:S(2)}) collective-permute-start(f32[512,128]{1,0:T(8,128)} %get-tuple-element.63), channel_id=1, source_target_pairs={{0,7},{1,0},{2,1},{3,2},{4,3},{5,4},{6,5},{7,6},{8,15},{9,8},{10,9... | collective-permute-start | bytes 786440 | tf_op jit(solution)/shard_map/ppermute | solution.py:182
  190.4 7.4 %collective-permute-start.25 = (f32[512,128]{1,0:T(8,128)S(1)}, f32[512,128]{1,0:T(8,128)S(1)}, u32[]{:S(2)}, u32[]{:S(2)}) collective-permute-start(f32[512,128]{1,0:T(8,128)S(1)} %bitcast_add_fusion.3), channel_id=1, source_target_pairs={{0,1},{1,2},{2,3},{3,4},{4,5},{5,6},{6,7},{7,0},{8,9},{9,10},{10,1... | collective-permute-start | bytes 786440 | tf_op jit(solution)/shard_map/ppermute | solution.py:183
  201.4 22.8 %all-to-all-start = ((f32[16,3,16,128]{3,2,1,0:T(8,128)}), f32[16,3,16,128]{3,2,1,0:T(8,128)S(1)}, u32[]{:S(2)}, u32[]{:S(2)}) async-start(f32[16,3,16,128]{3,2,1,0:T(8,128)} %maximum_bitcast_fusion), calls=%async_computation | async-start | bytes 786432 | tf_op jit(solution)/shard_map/all_to_all | solution.py:209
  (34 other events, 724.4 us)
Sparse Core Ops, SparseCore 0:
  42.5 47.7 all-gather.4
  99.9 52.1 all-gather.6
